TPU v7x, 32 devices: a whole 2x2x4 slice. The times are simulated.
32 devices in a mesh: dp: 8 (over y, x, core), seq: 4 (over z).
Axes of the slice: x: 2, y: 2, z: 4, core: 2. Of those that a mesh axis runs over, the one named last changes fastest.
Arguments:
- tokens: float32 [8, 1024, 1152], P('dp', 'seq'), may hold values from -6 to 6
- cotangent: float32 [8, 1024, 1152], P('dp', 'seq'), may hold values from -6 to 6
- counts: int32 [8, 4], P('dp'), may hold values from 1 to 256, 729 in all within a row
- owner_table: int32 [6], replicated, may hold values from 0 to 7, as said below
- owned_weights: float32 [8, 1152, 4, 1076], P('dp', None, 'seq'), as said below
- owned_moments: float32 [8, 1152, 4, 1076], P('dp', None, 'seq'), as said below
- vectors: float32 [13520], P('seq')
- vector_moments: float32 [2, 13520], P(None, 'seq')
Outputs:
- block_out: float32 [8, 1024, 1152], P('dp', 'seq')
- grad_tokens: float32 [8, 1024, 1152], P('dp', 'seq')
- owned_first: float32 [8, 1152, 4, 1076], P('dp', None, 'seq')
- owned_new: float32 [8, 1152, 4, 1076], P('dp', None, 'seq')
- vector_first: float32 [13520], P('seq')
- vector_second: float32 [13520], P('seq')
- vector_new: float32 [13520], P('seq')
Inputs may be any that keep to these rules, and one draw needn't show every extreme that they name: A seq index holds counts[i, s] tokens of image i in its first slots; each row sums to 729 and reaches 256. `owner_table`: six different owners, for query, key, value, output, up and down matrices in that order. `owned_weights`: slot owner_table[m] holds matrix m as in the statement; other entries are zero. `owned_moments`: laid out as owned_weights, zero in the same entries.
All inputs are finite; a program needn't handle non-finite values.
Results may differ from a plain program's by a relative error of at most 0.025.
Values may be sent and summed in bfloat16 or wider, within the bound.
No kernel may reach another device: no remote copies, remote signals or barrier semaphores. Data moves between devices by JAX's collectives and lax.ppermute only.
A program may use at most 256 MiB of HBM per device.

v0:
```python
import math

import jax
import jax.numpy as jnp
from jax import lax
from jax.sharding import PartitionSpec as P

HEADS = 16
FF = 4304
NS_ITERS = 5
STEP = 10


norm_eps = 1e-06
coef_a = 3.4445
coef_b = -4.775
coef_c = 2.0315
momentum_decay = 0.95
matrix_rate = 0.15
matrix_decay = 0.1
beta_first = 0.9
beta_second = 0.999
vector_rate = 0.5
adam_eps = 1e-08
highest = lax.Precision.HIGHEST


def spread(x, axis, root):
    mine = lax.axis_index(axis) == root
    return lax.psum(jnp.where(mine, x, jnp.zeros_like(x)), axis)


def layer_norm(inputs, gain_row, shift_row):
    average = jnp.mean(inputs, axis=-1, keepdims=True)
    centered = inputs - average
    variance = jnp.mean(centered * centered, axis=-1, keepdims=True)
    return centered * lax.rsqrt(variance + norm_eps) * gain_row + shift_row


def gelu_tanh(inputs):
    return (
        0.5
        * inputs
        * (1.0 + jnp.tanh(0.7978845608028654 * (inputs + 0.044715 * inputs * inputs * inputs)))
    )


def product(form, left, right):
    return jnp.einsum(form, left, right, preferred_element_type=jnp.float32)


def gram_total(source):
    partial_gram = jnp.dot(source, source.T, precision=highest)
    gram_share = lax.psum_scatter(
        partial_gram.astype(jnp.bfloat16), "seq", scatter_dimension=0, tiled=True
    ).astype(jnp.float32)
    return lax.all_gather(gram_share.astype(jnp.bfloat16), "seq", axis=0, tiled=True).astype(
        gram_share.dtype
    )


def orthogonalize(direction):
    first_gram = gram_total(direction)
    scaling = 1.0 / (jnp.sqrt(jnp.trace(first_gram)) + 1e-07)
    orthogonal = direction * scaling
    gram_matrix = first_gram * (scaling * scaling)
    for sweep_index in range(NS_ITERS):
        if sweep_index > 0:
            gram_matrix = gram_total(orthogonal)
        mixing = coef_b * gram_matrix + coef_c * jnp.dot(
            gram_matrix, gram_matrix, precision=highest
        )
        orthogonal = coef_a * orthogonal + jnp.dot(mixing, orthogonal, precision=highest)
    return orthogonal


def local(
    tokens, cotangent, counts, owner_table, owned_weights, owned_moments, vectors, vector_moments
):
    seq_count = lax.axis_size("seq")
    seq_index = lax.axis_index("seq")
    dp_index = lax.axis_index("dp")
    images = tokens.shape[0]
    capacity = tokens.shape[1]
    model_width = tokens.shape[2]
    slot_count = capacity * seq_count
    head_size = model_width // HEADS
    score_scale = 1.0 / math.sqrt(head_size)
    widths = (model_width, model_width, model_width, model_width, FF, FF)
    slab_width = owned_weights.shape[3]
    token_rows = images * capacity
    weight_slab = owned_weights[0, :, 0, :]
    pieces = []
    lowered_slab = weight_slab.astype(jnp.bfloat16)
    for matrix in range(6):
        columns = widths[matrix] // seq_count
        pieces.append(spread(lowered_slab[:, :columns], "dp", owner_table[matrix]))
    piece_query, piece_key, piece_value, piece_out, piece_up, piece_down = pieces
    vector_low = vectors.astype(jnp.bfloat16)
    gathered = (
        lax.all_gather(piece_query, "seq", axis=1, tiled=True),
        lax.all_gather(piece_key, "seq", axis=1, tiled=True),
        lax.all_gather(piece_value, "seq", axis=1, tiled=True),
        lax.all_gather(piece_out, "seq", axis=1, tiled=True),
        lax.all_gather(piece_up, "seq", axis=1, tiled=True),
        lax.all_gather(piece_down, "seq", axis=1, tiled=True),
        lax.all_gather(vector_low, "seq", axis=0, tiled=True),
    )
    w_query, w_key, w_value, w_out, w_up, w_down = gathered[:6]
    vector_full = gathered[6].astype(jnp.float32)
    row_params = vector_full[: 8 * model_width].reshape(8, model_width)
    up_bias = vector_full[8 * model_width :]
    own_counts = lax.dynamic_index_in_dim(counts, seq_index, 1, keepdims=False)
    query_valid = jnp.arange(capacity)[None, :] < own_counts[:, None]
    key_valid = (jnp.arange(slot_count) % capacity)[None, :] < jnp.repeat(counts, capacity, axis=1)
    query_mask = query_valid[:, :, None].astype(jnp.float32)
    rows_in = tokens.reshape(token_rows, model_width)
    normed_f32, norm_back = jax.vjp(layer_norm, rows_in, row_params[0], row_params[1])
    normed = normed_f32.astype(jnp.bfloat16)
    queries = (product("rd,de->re", normed, w_query) + row_params[2]).astype(jnp.bfloat16)
    key_local = (
        product("rd,de->re", normed, w_key)
        .astype(jnp.bfloat16)
        .reshape(images, capacity, model_width)
    )
    value_local = (
        (product("rd,de->re", normed, w_value) + row_params[3])
        .astype(jnp.bfloat16)
        .reshape(images, capacity, model_width)
    )
    key_all, value_all = (
        lax.all_gather(key_local, "seq", axis=1, tiled=True),
        lax.all_gather(value_local, "seq", axis=1, tiled=True),
    )
    query_heads = queries.reshape(images, capacity, HEADS, head_size)

    def masked_scores(key_source):
        key_heads = key_source.reshape(images, slot_count, HEADS, head_size)
        raw_scores = product("gqhe,gkhe->ghqk", query_heads, key_heads) * score_scale
        return jnp.where(key_valid[:, None, None, :], raw_scores, -1e30)

    scores = masked_scores(key_all)
    row_max = jnp.max(scores, axis=-1, keepdims=True)
    exponent = jnp.exp(scores - row_max)
    row_total = jnp.sum(exponent, axis=-1, keepdims=True)
    log_total = row_max + jnp.log(row_total)
    soft_low = (exponent / row_total).astype(jnp.bfloat16)
    value_heads = value_all.reshape(images, slot_count, HEADS, head_size)
    context = (
        product("ghqk,gkhe->gqhe", soft_low, value_heads)
        .reshape(token_rows, model_width)
        .astype(jnp.bfloat16)
    )
    middle = rows_in + product("rd,de->re", context, w_out) + row_params[4]
    normed_two_f32, norm_two_back = jax.vjp(layer_norm, middle, row_params[5], row_params[6])
    normed_two = normed_two_f32.astype(jnp.bfloat16)
    pre_act = product("rd,df->rf", normed_two, w_up) + up_bias
    hidden_f32, gelu_back = jax.vjp(gelu_tanh, pre_act)
    hidden = hidden_f32.astype(jnp.bfloat16)
    out_rows = middle + product("rf,df->rd", hidden, w_down) + row_params[7]
    block_out = out_rows.reshape(images, capacity, model_width) * query_mask
    grad_rows = (cotangent * query_mask).reshape(token_rows, model_width)
    grad_branch = grad_rows.astype(jnp.bfloat16)
    grad_down = product("rd,rf->df", grad_branch, hidden)
    grad_bias_down = jnp.sum(grad_branch.astype(jnp.float32), axis=0)
    grad_hidden = product("rd,df->rf", grad_branch, w_down)
    grad_pre = gelu_back(grad_hidden)[0].astype(jnp.bfloat16)
    grad_up = product("rd,rf->df", normed_two, grad_pre)
    grad_up_bias = jnp.sum(grad_pre.astype(jnp.float32), axis=0)
    grad_normed_two = product("rf,df->rd", grad_pre, w_up)
    grad_mid_norm, grad_gain_two, grad_shift_two = norm_two_back(grad_normed_two)
    grad_middle = grad_rows + grad_mid_norm
    grad_attn_out = grad_middle.astype(jnp.bfloat16)
    grad_w_out = product("rd,re->de", context, grad_attn_out)
    grad_bias_out = jnp.sum(grad_attn_out.astype(jnp.float32), axis=0)
    grad_context = (
        product("re,de->rd", grad_attn_out, w_out)
        .astype(jnp.bfloat16)
        .reshape(images, capacity, HEADS, head_size)
    )
    key_heads = key_all.reshape(images, slot_count, HEADS, head_size)
    value_heads = value_all.reshape(images, slot_count, HEADS, head_size)
    soft_f32 = jnp.exp(masked_scores(key_all) - log_total)
    soft_back = soft_f32.astype(jnp.bfloat16)
    grad_value_part = product("ghqk,gqhe->gkhe", soft_back, grad_context)
    grad_soft = product("gqhe,gkhe->ghqk", grad_context, value_heads)
    grad_scores = soft_f32 * (grad_soft - jnp.sum(soft_f32 * grad_soft, axis=-1, keepdims=True))
    grad_scores = jnp.where(key_valid[:, None, None, :], grad_scores, 0.0).astype(jnp.bfloat16)
    grad_queries = (
        (product("ghqk,gkhe->gqhe", grad_scores, key_heads) * score_scale)
        .reshape(token_rows, model_width)
        .astype(jnp.bfloat16)
    )
    grad_key_part = product("ghqk,gqhe->gkhe", grad_scores, query_heads) * score_scale
    grad_key_sum, grad_value_sum = (
        lax.psum_scatter(
            grad_key_part.reshape(images, slot_count, model_width).astype(jnp.bfloat16),
            "seq",
            scatter_dimension=1,
            tiled=True,
        ).astype(jnp.float32),
        lax.psum_scatter(
            grad_value_part.reshape(images, slot_count, model_width).astype(jnp.bfloat16),
            "seq",
            scatter_dimension=1,
            tiled=True,
        ).astype(jnp.float32),
    )
    grad_keys = grad_key_sum.reshape(token_rows, model_width).astype(jnp.bfloat16)
    grad_values = grad_value_sum.reshape(token_rows, model_width).astype(jnp.bfloat16)
    grad_w_query = product("rd,re->de", normed, grad_queries)
    grad_w_key = product("rd,re->de", normed, grad_keys)
    grad_w_value = product("rd,re->de", normed, grad_values)
    grad_bias_query = jnp.sum(grad_queries.astype(jnp.float32), axis=0)
    grad_bias_value = jnp.sum(grad_values.astype(jnp.float32), axis=0)
    grad_normed = (
        product("re,de->rd", grad_queries, w_query)
        + product("re,de->rd", grad_keys, w_key)
        + product("re,de->rd", grad_values, w_value)
    )
    grad_in_norm, grad_gain_one, grad_shift_one = norm_back(grad_normed)
    grad_tokens = (grad_middle + grad_in_norm).reshape(images, capacity, model_width) * query_mask
    vector_grad = jnp.concatenate(
        [
            grad_gain_one,
            grad_shift_one,
            grad_bias_query,
            grad_bias_value,
            grad_bias_out,
            grad_gain_two,
            grad_shift_two,
            grad_bias_down,
            grad_up_bias,
        ]
    )
    reduced = (
        lax.psum_scatter(grad_w_query, "seq", scatter_dimension=1, tiled=True),
        lax.psum_scatter(grad_w_key, "seq", scatter_dimension=1, tiled=True),
        lax.psum_scatter(grad_w_value, "seq", scatter_dimension=1, tiled=True),
        lax.psum_scatter(grad_w_out, "seq", scatter_dimension=1, tiled=True),
        lax.psum_scatter(grad_up, "seq", scatter_dimension=1, tiled=True),
        lax.psum_scatter(grad_down, "seq", scatter_dimension=1, tiled=True),
        lax.psum_scatter(vector_grad, "seq", scatter_dimension=0, tiled=True),
    )
    summed = (
        lax.psum(reduced[0].astype(jnp.bfloat16), "dp").astype(jnp.float32),
        lax.psum(reduced[1].astype(jnp.bfloat16), "dp").astype(jnp.float32),
        lax.psum(reduced[2].astype(jnp.bfloat16), "dp").astype(jnp.float32),
        lax.psum(reduced[3].astype(jnp.bfloat16), "dp").astype(jnp.float32),
        lax.psum(reduced[4].astype(jnp.bfloat16), "dp").astype(jnp.float32),
        lax.psum(reduced[5].astype(jnp.bfloat16), "dp").astype(jnp.float32),
        lax.psum(reduced[6].astype(jnp.bfloat16), "dp").astype(jnp.float32),
    )
    grad_slab = jnp.zeros((model_width, slab_width), jnp.float32)
    for matrix in range(6):
        block_piece = summed[matrix]
        grad_slab = jnp.where(
            owner_table[matrix] == dp_index,
            jnp.pad(block_piece, ((0, 0), (0, slab_width - block_piece.shape[1]))),
            grad_slab,
        )
    vector_total = summed[6]
    moment = owned_moments[0, :, 0, :]
    moment_new = momentum_decay * moment + grad_slab
    direction = grad_slab + momentum_decay * moment_new
    orthogonal = orthogonalize(direction)
    update_scale = jnp.zeros((), jnp.float32)
    for matrix in range(6):
        update_scale = jnp.where(
            owner_table[matrix] == dp_index,
            jnp.float32(0.2 * math.sqrt(max(model_width, widths[matrix]))),
            update_scale,
        )
    updated = (
        weight_slab * (1.0 - matrix_rate * matrix_decay) - matrix_rate * update_scale * orthogonal
    )
    owned_first = moment_new[None, :, None, :]
    owned_new = updated[None, :, None, :]
    first_new = beta_first * vector_moments[0] + (1.0 - beta_first) * vector_total
    second_new = beta_second * vector_moments[1] + (1.0 - beta_second) * vector_total * vector_total
    first_fix = 1.0 - beta_first**STEP
    second_fix = 1.0 - beta_second**STEP
    vector_new = vectors - vector_rate * (first_new / first_fix) / (
        jnp.sqrt(second_new / second_fix) + adam_eps
    )
    return (block_out, grad_tokens, owned_first, owned_new, first_new, second_new, vector_new)


def solution(mesh):
    in_specs = (
        P("dp", "seq", None),
        P("dp", "seq", None),
        P("dp", None),
        P(),
        P("dp", None, "seq", None),
        P("dp", None, "seq", None),
        P("seq"),
        P(None, "seq"),
    )
    out_specs = (
        P("dp", "seq", None),
        P("dp", "seq", None),
        P("dp", None, "seq", None),
        P("dp", None, "seq", None),
        P("seq"),
        P("seq"),
        P("seq"),
    )
    return jax.shard_map(local, mesh=mesh, in_specs=in_specs, out_specs=out_specs, check_vma=False)
```

profile of v0, /device:TPU:0, one launch (start us, length us, event | category | flops | bytes accessed | tf_op | source)
XLA Modules:
  0.0 3078.6 jit_solution(2758728626690163982)
XLA Ops:
  12.6 4.3 broadcast_select_fusion.1
  20.2 123.1 %all-reduce.17.cloned.1.call-done = (bf16[1152,288]{0,1:T(8,128)(2,1)}, bf16[1152,288]{0,1:T(8,128)(2,1)}, bf16[1152,288]{0,1:T(8,128)(2,1)}, bf16[1152,288]{0,1...) async-done(((bf16[1152,288]{0,1:T(8,128)(2,1)}, bf16[1152,288]{0,1:T(8,128)(2,1)}, bf16[1152,288]{0,1:T(8,128)(2,1)}, bf16[1152,288]{0,1:T(8,128)(2,1)}, ...) | async-done | bytes 7612432 | tf_op jit(solution)/shard_map/psum | solution.py:30
  146.5 19.7 all-reduce.4
  167.7 33.1 %all-gather.18.cloned.1.call-done = bf16[1152,1152]{0,1:T(8,128)(2,1)} async-done(((bf16[1152,288]{0,1:T(8,128)(2,1)}), bf16[1152,1152]{0,1:T(8,128)(2,1)}) %all-gather.18.cloned.1.call-update) | async-done | bytes 2654224 | tf_op jit(solution)/shard_map/all_gather | solution.py:103
  204.5 51.9 %all-gather.22.cloned.1.call-done = bf16[1152,1152]{0,1:T(8,128)(2,1)} async-done(((bf16[1152,288]{0,1:T(8,128)(2,1)}), bf16[1152,1152]{0,1:T(8,128)(2,1)}) %all-gather.22.cloned.1.call-update) | async-done | bytes 2654224 | tf_op jit(solution)/shard_map/all_gather | solution.py:102
  266.4 45.5 %all-gather.20.cloned.1.call-done = bf16[1152,1152]{0,1:T(8,128)(2,1)} async-done(((bf16[1152,288]{0,1:T(8,128)(2,1)}), bf16[1152,1152]{0,1:T(8,128)(2,1)}) %all-gather.20.cloned.1.call-update) | async-done | bytes 2654224 | tf_op jit(solution)/shard_map/all_gather | solution.py:101
  315.9 47.4 %all-gather.36.cloned.1.call-done = bf16[1024,1152]{1,0:T(8,128)(2,1)} async-done(((bf16[256,1152]{1,0:T(8,128)(2,1)}), bf16[1024,1152]{1,0:T(8,128)(2,1)}) %all-gather.36.cloned.1.call-update) | async-done | bytes 2359312 | tf_op jit(solution)/shard_map/all_gather | solution.py:133
  366.2 48.3 %all-gather.38.cloned.1.call-done = bf16[1024,1152]{1,0:T(8,128)(2,1)} async-done(((bf16[256,1152]{1,0:T(8,128)(2,1)}), bf16[1024,1152]{1,0:T(8,128)(2,1)}) %all-gather.38.cloned.1.call-update) | async-done | bytes 2359312 | tf_op jit(solution)/shard_map/all_gather | solution.py:132
  414.6 4.3 copy.38
  418.8 4.9 fusion.91
  429.8 4.7 fusion.54
  434.5 35.8 %all-gather.24.cloned.1.call-done = bf16[1152,1152]{0,1:T(8,128)(2,1)} async-done(((bf16[1152,288]{0,1:T(8,128)(2,1)}), bf16[1152,1152]{0,1:T(8,128)(2,1)}) %all-gather.24.cloned.1.call-update) | async-done | bytes 2654224 | tf_op jit(solution)/shard_map/all_gather | solution.py:104
  473.8 172.1 %all-gather.40.cloned.1.call-done = bf16[4,1076,1152]{2,1,0:T(8,128)(2,1)} async-done(((bf16[1,1076,1152]{2,1,0:T(8,128)(2,1)}), bf16[4,1076,1152]{2,1,0:T(8,128)(2,1)}) %all-gather.40.cloned.1.call-update) | async-done | bytes 9916432 | tf_op jit(solution)/shard_map/all_gather | solution.py:105
  645.9 11.9 reshape.384
  657.8 9.6 convolution_add_fusion.5
  667.5 153.4 %all-gather.42.cloned.1.call-done = bf16[4,1076,1152]{2,1,0:T(8,128)(2,1)} async-done(((bf16[1,1076,1152]{2,1,0:T(8,128)(2,1)}), bf16[4,1076,1152]{2,1,0:T(8,128)(2,1)}) %all-gather.42.cloned.1.call-update) | async-done | bytes 9916432 | tf_op jit(solution)/shard_map/all_gather | solution.py:106
  820.9 11.3 reshape.386
  832.2 10.7 convert_reduce_fusion
  843.0 3.9 multiply_reduce_fusion.1
  851.5 9.3 fusion.48
  862.4 9.3 fusion.99
  871.7 36.5 %multiply_convert_fusion = bf16[16,72,1024]{2,1,0:T(8,128)(2,1)} fusion(bf16[256,16,72]{0,2,1:T(8,128)(2,1)} %bitcast.182, f32[16,256,1024]{2,1,0:T(8,128)} %fusion.99, f32[16,256,1024]{2,1,0:T(8,128)} %copy-done.2, f32[16,256]{1,0:T(8,128)} %copy-done.47, pred[1024]{0:T(1024)(128)(4,1)S(1)} %copy-done.72), kind=kOutput, calls=%fused_computation.56 | convolution fusion | flops 635704320 | bytes 36520960 | tf_op jit(solution)/shard_map/ghqk,gqhe->gkhe/dot_general | solution.py:49
  913.2 38.8 %convert_reduce_fusion.4 = (f32[16,72]{1,0:T(8,128)}, bf16[16,72,256]{2,1,0:T(8,128)(2,1)}) fusion(bf16[1024,16,72]{0,2,1:T(8,128)(2,1)S(1)} %bitcast.173, f32[16,256,1024]{2,1,0:T(8,128)} %fusion.99, f32[16,256,1024]{2,1,0:T(8,128)} %copy-done.2, f32[16,256]{1,0:T(8,128)} %copy-done.47, pred[1024]{0:T(1024)(128)(4,1)} %fusion.67), kind=kOutput, calls=%fused_computation.99 | convolution fusion | flops 634523520 | bytes 36525568 | tf_op jit(solution)/shard_map/ghqk,gkhe->gqhe/dot_general | solution.py:49
  952.1 4.5 fusion.97
  957.6 13.6 fusion.81
  971.2 4.5 fusion.59
  975.8 573.7 %fusion = f32[1152,1088]{0,1:T(8,128)} fusion(f32[1152,4304]{0,1:T(8,128)} %fusion.81), kind=kCustom, calls=%all-reduce-scatter | all-reduce-scatter fusion | flops 5013505 | bytes 24846848
  1551.8 11.5 fusion.80
  1563.3 4.5 fusion.62
  1567.9 419.3 %fusion.1 = f32[1152,1088]{0,1:T(8,128)} fusion(f32[1152,4304]{0,1:T(8,128)} %fusion.80), kind=kCustom, calls=%all-reduce-scatter.1 | all-reduce-scatter fusion | flops 5013505 | bytes 24846848
  1990.4 13.6 concatenate.4
  2004.0 13.5 concatenate.5
  2017.4 3.9 dynamic-slice_convert_fusion.1
  2036.2 115.9 %all-reduce.15.cloned.1.call-done = (bf16[1152,288]{0,1:T(8,128)(2,1)}, bf16[1152,288]{0,1:T(8,128)(2,1)}, bf16[1152,288]{0,1:T(8,128)(2,1)}, bf16[1152,288]{0,1...) async-done(((bf16[1152,288]{0,1:T(8,128)(2,1)}, bf16[1152,288]{0,1:T(8,128)(2,1)}, bf16[1152,288]{0,1:T(8,128)(2,1)}, bf16[1152,288]{0,1:T(8,128)(2,1)}, ...) | async-done | bytes 7612432 | tf_op jit(solution)/shard_map/psum | solution.py:246
  2152.1 35.8 %convolution_convert_fusion.4 = bf16[1152,1152]{1,0:T(8,128)(2,1)} fusion(f32[1,1152,1,1076]{1,2,3,0:T(1,128)} %param.13, bf16[1152,1076]{0,1:T(8,128)(2,1)} %get-tuple-element.40, bf16[1152,1076]{0,1:T(8,128)(2,1)} %get-tuple-element.41, bf16[1152,288]{0,1:T(8,128)(2,1)} %get-tuple-element.36, bf16[1152,288]{0,1:T(8,128)(2,1)} %get-tuple-element.37, ...), kind=kOutput, calls=%fused_computation.36 | convolution fusion | flops 17156726784 | bytes 15224838 | tf_op jit(solution)/shard_map/dot_general | solution.py:53
  2187.9 52.8 %reduce-scatter.28.cloned.1.call-done = bf16[288,1152]{1,0:T(8,128)(2,1)} async-done(((bf16[1152,1152]{1,0:T(8,128)(2,1)}), bf16[288,1152]{1,0:T(8,128)(2,1)}) %reduce-scatter.28.cloned.1.call-update) | async-done | bytes 663568 | tf_op jit(solution)/shard_map/reduce_scatter | solution.py:54
  2241.2 56.0 %all-gather.26.cloned.1.call-done = bf16[1152,1152]{1,0:T(8,128)(2,1)} async-done(((bf16[288,1152]{1,0:T(8,128)(2,1)}), bf16[1152,1152]{1,0:T(8,128)(2,1)}) %all-gather.26.cloned.1.call-update) | async-done | bytes 2654224 | tf_op jit(solution)/shard_map/all_gather | solution.py:57
  2300.5 26.9 fusion.10
  2327.5 30.9 %convolution_add_fusion.4 = f32[1152,1076]{0,1:T(8,128)S(1)} fusion(f32[1152,1152]{1,0:T(8,128)S(1)} %fusion.10, f32[]{:T(128)S(6)} %div.71, f32[1,1152,1,1076]{1,2,3,0:T(1,128)} %param.13, bf16[1152,288]{0,1:T(8,128)(2,1)S(1)} %copy-done.31, pred[]{:T(512)S(6)} %eq.59, bf16[1152,288]{0,1:T(8,128)(2,1)S(1)} %copy-done.33, pred[]{:T(512)S(6)} %eq.58, ...), kind=kOutput, calls=%fused_computation.21 | convolution fusion | flops 17180190720 | bytes 22837258 | tf_op jit(solution)/shard_map/dot_general | solution.py:73
  2360.6 25.7 convolution_convert_fusion.3
  2386.4 51.5 %reduce-scatter.30.cloned.1.call-done = bf16[288,1152]{1,0:T(8,128)(2,1)} async-done(((bf16[1152,1152]{1,0:T(8,128)(2,1)}), bf16[288,1152]{1,0:T(8,128)(2,1)}) %reduce-scatter.30.cloned.1.call-update) | async-done | bytes 663568 | tf_op jit(solution)/shard_map/reduce_scatter | solution.py:54
  2438.0 56.4 %all-gather.28.cloned.1.call-done = bf16[1152,1152]{1,0:T(8,128)(2,1)} async-done(((bf16[288,1152]{1,0:T(8,128)(2,1)}), bf16[1152,1152]{1,0:T(8,128)(2,1)}) %all-gather.28.cloned.1.call-update) | async-done | bytes 2654224 | tf_op jit(solution)/shard_map/all_gather | solution.py:57
  2494.4 7.6 fusion.11
  2502.0 26.3 convolution_add_fusion.3
  2530.5 25.7 convolution_convert_fusion.2
  2556.3 51.5 %reduce-scatter.32.cloned.1.call-done = bf16[288,1152]{1,0:T(8,128)(2,1)} async-done(((bf16[1152,1152]{1,0:T(8,128)(2,1)}), bf16[288,1152]{1,0:T(8,128)(2,1)}) %reduce-scatter.32.cloned.1.call-update) | async-done | bytes 663568 | tf_op jit(solution)/shard_map/reduce_scatter | solution.py:54
  2607.9 56.6 %all-gather.30.cloned.1.call-done = bf16[1152,1152]{1,0:T(8,128)(2,1)} async-done(((bf16[288,1152]{1,0:T(8,128)(2,1)}), bf16[1152,1152]{1,0:T(8,128)(2,1)}) %all-gather.30.cloned.1.call-update) | async-done | bytes 2654224 | tf_op jit(solution)/shard_map/all_gather | solution.py:57
  2664.4 7.6 fusion.12
  2672.0 26.1 convolution_add_fusion.2
  2700.3 25.9 convolution_convert_fusion.1
  2726.3 51.5 %reduce-scatter.34.cloned.1.call-done = bf16[288,1152]{1,0:T(8,128)(2,1)} async-done(((bf16[1152,1152]{1,0:T(8,128)(2,1)}), bf16[288,1152]{1,0:T(8,128)(2,1)}) %reduce-scatter.34.cloned.1.call-update) | async-done | bytes 663568 | tf_op jit(solution)/shard_map/reduce_scatter | solution.py:54
  2777.9 56.4 %all-gather.32.cloned.1.call-done = bf16[1152,1152]{1,0:T(8,128)(2,1)} async-done(((bf16[288,1152]{1,0:T(8,128)(2,1)}), bf16[1152,1152]{1,0:T(8,128)(2,1)}) %all-gather.32.cloned.1.call-update) | async-done | bytes 2654224 | tf_op jit(solution)/shard_map/all_gather | solution.py:57
  2834.3 7.6 fusion.13
  2841.9 26.1 convolution_add_fusion.1
  2870.3 25.7 convolution_convert_fusion
  2901.2 9.5 fusion.39
  2926.0 21.4 all-reduce.7
  2948.8 13.5 psum.103
  2967.6 5.2 fusion.45
  2972.8 22.2 copy.42
  2995.1 20.7 all-gather.34.cloned.1.call-done
  3015.7 7.3 fusion.14
  3023.1 26.6 fusion.15
  3049.7 22.2 copy.43
  (291 shorter events, 105.6 us)
Async XLA Ops:
  7.2 255.8 %copy-start = (s32[1,4]{1,0:T(1,128)S(1)}, s32[1,4]{1,0:T(1,128)}, u32[]{:S(2)}) copy-start(s32[1,4]{1,0:T(1,128)} %param.10) | copy-start | bytes 52
  7.2 136.1 %all-reduce.17.cloned.1.call-start = ((), (), s32[]{:S(2)}) async-start(), calls=%async_computation.36 | async-start | bytes 15261696 | tf_op jit(solution)/shard_map/psum | solution.py:30
  20.1 124.6 %copy-start.46 = (f32[3380]{0:T(1024)S(1)}, f32[3380]{0:T(1024)}, u32[]{:S(2)}) copy-start(f32[3380]{0:T(1024)} %param.14) | copy-start | bytes 40564
  20.1 124.6 %copy-start.70 = (u32[32]{0:T(128)S(1)}, u32[32]{0:T(128)}, u32[]{:S(2)}) copy-start(u32[32]{0:T(128)} %constant.125) | copy-start | bytes 388
  20.1 126.0 %copy-start.3 = (f32[1,256,1152]{2,1,0:T(8,128)S(1)}, f32[1,256,1152]{2,1,0:T(8,128)}, u32[]{:S(2)}) copy-start(f32[1,256,1152]{2,1,0:T(8,128)} %param.8) | copy-start | bytes 3538948
  20.1 180.7 %all-gather.18.cloned.1.call-start = ((), (), s32[]{:S(2)}) async-start(), calls=%async_computation.11 | async-start | bytes 3317760 | tf_op jit(solution)/shard_map/all_gather | solution.py:103
  143.3 113.1 %all-gather.22.cloned.1.call-start = ((), (), s32[]{:S(2)}) async-start(), calls=%async_computation.13 | async-start | bytes 3317760 | tf_op jit(solution)/shard_map/all_gather | solution.py:102
  144.1 167.9 %all-gather.20.cloned.1.call-start = ((), (), s32[]{:S(2)}) async-start(), calls=%async_computation.12 | async-start | bytes 3317760 | tf_op jit(solution)/shard_map/all_gather | solution.py:101
  144.6 218.6 %all-gather.36.cloned.1.call-start = ((), (), s32[]{:S(2)}) async-start(), calls=%async_computation.31 | async-start | bytes 2949120 | tf_op jit(solution)/shard_map/all_gather | solution.py:133
  167.1 144.9 %copy-start.44 = (f32[256]{0:T(256)}, f32[256]{0:T(256)S(1)}, u32[]{:S(2)}) copy-start(f32[256]{0:T(256)S(1)} %fusion.71) | copy-start | bytes 3076
  167.7 144.3 %copy-start.40 = (f32[1152]{0:T(1024)}, f32[1152]{0:T(1024)S(1)}, u32[]{:S(2)}) copy-start(f32[1152]{0:T(1024)S(1)} %get-tuple-element.74) | copy-start | bytes 13828
  204.5 210.1 %all-gather.38.cloned.1.call-start = ((), (), s32[]{:S(2)}) async-start(), calls=%async_computation.32 | async-start | bytes 2949120 | tf_op jit(solution)/shard_map/all_gather | solution.py:132
  260.1 210.3 %all-gather.24.cloned.1.call-start = ((), (), s32[]{:S(2)}) async-start(), calls=%async_computation.14 | async-start | bytes 3317760 | tf_op jit(solution)/shard_map/all_gather | solution.py:104
  260.8 385.1 %all-gather.40.cloned.1.call-start = ((), (), s32[]{:S(2)}) async-start(), calls=%async_computation.33 | async-start | bytes 12441600 | tf_op jit(solution)/shard_map/all_gather | solution.py:105
  261.6 559.3 %all-gather.42.cloned.1.call-start = ((), (), s32[]{:S(2)}) async-start(), calls=%async_computation.34 | async-start | bytes 12441600 | tf_op jit(solution)/shard_map/all_gather | solution.py:106
  262.3 708.9 %reduce-scatter.18.cloned.1.call-start = ((), (), s32[]{:S(2)}) async-start(), calls=%async_computation.16 | async-start | bytes 2949120 | tf_op jit(solution)/shard_map/reduce_scatter | solution.py:202
  264.3 51.6 %copy-start.64 = (f32[256]{0:T(256)}, f32[256]{0:T(256)S(1)}, u32[]{:S(2)}) copy-start(f32[256]{0:T(256)S(1)} %compare_convert_fusion) | copy-start | bytes 3076
  315.9 102.9 %copy-start.71 = (pred[1024]{0:T(1024)(128)(4,1)S(1)}, pred[1024]{0:T(1024)(128)(4,1)}, u32[]{:S(2)}) copy-start(pred[1024]{0:T(1024)(128)(4,1)} %fusion.67) | copy-start | bytes 3076
  366.2 61.1 %copy-start.7 = (bf16[1024,1152]{0,1:T(8,128)(2,1)}, bf16[1024,1152]{0,1:T(8,128)(2,1)S(1)}, u32[]{:S(2)}) copy-start(bf16[1024,1152]{0,1:T(8,128)(2,1)S(1)} %copy.36) | copy-start | bytes 7077892
  434.5 39.1 %copy-start.39 = (f32[16,256]{1,0:T(8,128)S(1)}, f32[16,256]{1,0:T(8,128)}, u32[]{:S(2)}) copy-start(f32[16,256]{1,0:T(8,128)} %copy-done.38) | copy-start | bytes 49156
  434.5 39.1 %copy-start.49 = (f32[16,256]{1,0:T(8,128)S(1)}, f32[16,256]{1,0:T(8,128)}, u32[]{:S(2)}) copy-start(f32[16,256]{1,0:T(8,128)} %copy-done.48) | copy-start | bytes 49156
  473.4 184.5 %copy-start.4 = (f32[256,1152]{1,0:T(8,128)}, f32[256,1152]{1,0:T(8,128)S(1)}, u32[]{:S(2)}) copy-start(f32[256,1152]{1,0:T(8,128)S(1)} %get-tuple-element.87) | copy-start | bytes 3538948
  473.4 373.6 %copy-start.58 = (f32[256]{0:T(256)}, f32[256]{0:T(256)S(1)}, u32[]{:S(2)}) copy-start(f32[256]{0:T(256)S(1)} %broadcast_multiply_fusion) | copy-start | bytes 3076
  473.7 373.3 %copy-start.62 = (f32[256]{0:T(256)}, f32[256]{0:T(256)S(1)}, u32[]{:S(2)}) copy-start(f32[256]{0:T(256)S(1)} %fusion.72) | copy-start | bytes 3076
  473.7 376.9 %copy-start.47 = (f32[16,256]{1,0:T(8,128)}, f32[16,256]{1,0:T(8,128)S(1)}, u32[]{:S(2)}) copy-start(f32[16,256]{1,0:T(8,128)S(1)} %log_add_fusion) | copy-start | bytes 49156
  473.7 184.1 %copy-start.42 = (f32[1152]{0:T(1024)S(1)}, f32[1152]{0:T(1024)}, u32[]{:S(2)}) copy-start(f32[1152]{0:T(1024)} %get-tuple-element.67) | copy-start | bytes 13828
  473.7 184.1 %copy-start.50 = (f32[1152]{0:T(1024)S(1)}, f32[1152]{0:T(1024)}, u32[]{:S(2)}) copy-start(f32[1152]{0:T(1024)} %get-tuple-element.68) | copy-start | bytes 13828
  473.7 184.1 %copy-start.61 = (f32[4304]{0:T(1024)S(1)}, f32[4304]{0:T(1024)}, u32[]{:S(2)}) copy-start(f32[4304]{0:T(1024)} %slice.112) | copy-start | bytes 51652
  667.5 164.8 %copy-start.28 = (bf16[256,1152]{1,0:T(8,128)(2,1)S(1)}, bf16[256,1152]{1,0:T(8,128)(2,1)}, u32[]{:S(2)}) copy-start(bf16[256,1152]{1,0:T(8,128)(2,1)} %get-tuple-element.54) | copy-start | bytes 1769476
  860.8 702.5 %reduce-scatter.16.cloned.1.call-start = ((), (), s32[]{:S(2)}) async-start(), calls=%async_computation.15 | async-start | bytes 2949120 | tf_op jit(solution)/shard_map/reduce_scatter | solution.py:196
  871.7 36.5 %copy-start.11 = (f32[256,1152]{1,0:T(8,128)S(1)}, f32[256,1152]{1,0:T(8,128)}, u32[]{:S(2)}) copy-start(f32[256,1152]{1,0:T(8,128)} %copy-done.10) | copy-start | bytes 3538948
  871.7 36.5 %copy-start.20 = (bf16[16,72,256]{2,1,0:T(8,128)(2,1)S(1)}, bf16[16,72,256]{2,1,0:T(8,128)(2,1)}, u32[]{:S(2)}) copy-start(bf16[16,72,256]{2,1,0:T(8,128)(2,1)} %fusion.54) | copy-start | bytes 1769476
  908.2 1115.2 %reduce-scatter.20.cloned.1.call-start = ((), (), s32[]{:S(2)}) async-start(), calls=%async_computation.17 | async-start | bytes 6635520 | tf_op jit(solution)/shard_map/reduce_scatter | solution.py:240
  911.6 40.5 %copy-start.45 = (f32[256]{0:T(256)S(1)}, f32[256]{0:T(256)}, u32[]{:S(2)}) copy-start(f32[256]{0:T(256)} %copy-done.44) | copy-start | bytes 3076
  911.6 1114.0 %reduce-scatter.26.cloned.1.call-start = ((), (), s32[]{:S(2)}) async-start(), calls=%async_computation.20 | async-start | bytes 6635520 | tf_op jit(solution)/shard_map/reduce_scatter | solution.py:237
  956.6 1071.3 %reduce-scatter.22.cloned.1.call-start = ((), (), s32[]{:S(2)}) async-start(), calls=%async_computation.18 | async-start | bytes 6635520 | tf_op jit(solution)/shard_map/reduce_scatter | solution.py:239
  975.7 576.0 %copy-start.6 = (f32[256,1152]{1,0:T(8,128)S(1)}, f32[256,1152]{1,0:T(8,128)}, u32[]{:S(2)}) copy-start(f32[256,1152]{1,0:T(8,128)} %copy-done.4) | copy-start | bytes 3538948
  975.8 576.0 %copy-start.43 = (f32[1152]{0:T(1024)S(1)}, f32[1152]{0:T(1024)}, u32[]{:S(2)}) copy-start(f32[1152]{0:T(1024)} %get-tuple-element.67) | copy-start | bytes 13828
  975.8 576.0 %copy-start.51 = (f32[1152]{0:T(1024)S(1)}, f32[1152]{0:T(1024)}, u32[]{:S(2)}) copy-start(f32[1152]{0:T(1024)} %get-tuple-element.68) | copy-start | bytes 13828
  975.8 576.0 %copy-start.59 = (f32[256]{0:T(256)S(1)}, f32[256]{0:T(256)}, u32[]{:S(2)}) copy-start(f32[256]{0:T(256)} %copy-done.58) | copy-start | bytes 3076
  975.8 576.0 %copy-start.63 = (f32[256]{0:T(256)S(1)}, f32[256]{0:T(256)}, u32[]{:S(2)}) copy-start(f32[256]{0:T(256)} %copy-done.62) | copy-start | bytes 3076
  975.8 1054.3 %reduce-scatter.24.cloned.1.call-start = ((), (), s32[]{:S(2)}) async-start(), calls=%async_computation.19 | async-start | bytes 6635520 | tf_op jit(solution)/shard_map/reduce_scatter | solution.py:238
  1550.5 439.9 %collective-permute-start = (bf16[1152,36]{0,1:T(8,128)(2,1)S(1)}, bf16[1152,36]{0,1:T(8,128)(2,1)S(1)}, u32[]{:S(2)}, u32[]{:S(2)}) collective-permute-start(bf16[1152,36]{0,1:T(8,128)(2,1)S(1)} %slice.114), channel_id=1, source_target_pairs={{0,1},{1,2},{2,3},{4,5},{5,6},{6,7},{8,9},{9,10},{10,11},{12,13},{... | collective-permute-start | bytes 248840
  1567.8 584.2 %all-reduce.15.cloned.1.call-start = ((), (), s32[]{:S(2)}) async-start(), calls=%async_computation.35 | async-start | bytes 15261696 | tf_op jit(solution)/shard_map/psum | solution.py:246
  1988.2 15.8 collective-permute-start.1
  2032.3 208.4 %reduce-scatter.28.cloned.1.call-start = ((), (), s32[]{:S(2)}) async-start(), calls=%async_computation.21 | async-start | bytes 3317760 | tf_op jit(solution)/shard_map/reduce_scatter | solution.py:54
  2187.9 109.3 %all-gather.26.cloned.1.call-start = ((), (), s32[]{:S(2)}) async-start(), calls=%async_computation.22 | async-start | bytes 3317760 | tf_op jit(solution)/shard_map/all_gather | solution.py:57
  2240.7 197.2 %reduce-scatter.30.cloned.1.call-start = ((), (), s32[]{:S(2)}) async-start(), calls=%async_computation.23 | async-start | bytes 3317760 | tf_op jit(solution)/shard_map/reduce_scatter | solution.py:54
  2300.5 27.0 copy-start.24
  2300.5 27.0 copy-start.26
  2300.5 27.0 copy-start.31
  2300.5 27.0 copy-start.33
  2300.5 27.0 copy-start.35
  2386.4 108.0 %all-gather.28.cloned.1.call-start = ((), (), s32[]{:S(2)}) async-start(), calls=%async_computation.24 | async-start | bytes 3317760 | tf_op jit(solution)/shard_map/all_gather | solution.py:57
  2438.0 169.8 %reduce-scatter.32.cloned.1.call-start = ((), (), s32[]{:S(2)}) async-start(), calls=%async_computation.25 | async-start | bytes 3317760 | tf_op jit(solution)/shard_map/reduce_scatter | solution.py:54
  2556.2 108.2 %all-gather.30.cloned.1.call-start = ((), (), s32[]{:S(2)}) async-start(), calls=%async_computation.26 | async-start | bytes 3317760 | tf_op jit(solution)/shard_map/all_gather | solution.py:57
  2607.8 170.0 %reduce-scatter.34.cloned.1.call-start = ((), (), s32[]{:S(2)}) async-start(), calls=%async_computation.27 | async-start | bytes 3317760 | tf_op jit(solution)/shard_map/reduce_scatter | solution.py:54
  2726.3 108.0 %all-gather.32.cloned.1.call-start = ((), (), s32[]{:S(2)}) async-start(), calls=%async_computation.28 | async-start | bytes 3317760 | tf_op jit(solution)/shard_map/all_gather | solution.py:57
  2777.9 184.4 %reduce-scatter.36.cloned.1.call-start = ((), (), s32[]{:S(2)}) async-start(), calls=%async_computation.29 | async-start | bytes 3317760 | tf_op jit(solution)/shard_map/reduce_scatter | solution.py:54
  2870.3 27.4 copy-start.69
  2870.3 28.1 copy-start.30
  2896.0 119.7 %all-gather.34.cloned.1.call-start = ((), (), s32[]{:S(2)}) async-start(), calls=%async_computation.30 | async-start | bytes 3317760 | tf_op jit(solution)/shard_map/all_gather | solution.py:57
  2912.7 52.9 %copy-start.12 = (f32[256,1152]{1,0:T(8,128)S(1)}, f32[256,1152]{1,0:T(8,128)}, u32[]{:S(2)}) copy-start(f32[256,1152]{1,0:T(8,128)} %copy-done.10) | copy-start | bytes 3538948
  3023.1 48.8 %copy-start.1 = (s32[1,4]{1,0:T(1,128)S(1)}, s32[1,4]{1,0:T(1,128)}, u32[]{:S(2)}) copy-start(s32[1,4]{1,0:T(1,128)} %param.10) | copy-start | bytes 52
  (44 other events, 301.3 us)
Sparse Core Ops, SparseCore 0:
  20.2 123.0 all-reduce.16
  144.9 55.8 all-gather.17
  202.4 53.9 all-gather.21
  257.8 54.1 all-gather.19
  314.0 49.2 all-gather.35
  365.2 49.2 all-gather.37
  416.1 54.1 all-gather.23
  471.9 173.9 all-gather.39
  647.5 173.3 all-gather.41
  860.9 46.2 reduce-scatter.17
  909.5 47.4 reduce-scatter.15
  959.2 161.7 reduce-scatter.19
  1123.4 181.3 reduce-scatter.25
  1307.0 177.8 reduce-scatter.21
  1567.9 177.8 reduce-scatter.23
  2032.5 119.5 all-reduce.14
  2188.0 52.6 reduce-scatter.27
  2242.1 55.0 all-gather.25
  2386.5 51.3 reduce-scatter.29
  2439.3 55.0 all-gather.27
  2556.4 51.3 reduce-scatter.31
  2609.4 55.0 all-gather.29
  2726.4 51.3 reduce-scatter.33
  2779.3 55.0 all-gather.31
  2896.1 53.3 reduce-scatter.35
  2962.4 53.2 all-gather.33
where the time goes:
time: 3090 us; the launch traced here: 3080 us
  waiting for transfers between devices  1280 us (41%)
  blocking collectives  1050 us (34%)
  matrix products  531 us (17%)
  local copies, waits for them, and re-layouts  148 us (5%)
  other arithmetic  38.6 us (1%)
    unnamed x4, blocking collectives  1030 us
    all_gather x5, waiting for transfers between devices, gram_total(): lax.all_gather(gram_share.astype(jnp.bfloat16), 'seq', axis=0, tiled=True)  246 us
    reduce_scatter x5, waiting for transfers between devices, gram_total(): lax.psum_scatter(partial_gram.astype(jnp.bfloat16), 'seq', scatter_dimens...  207 us
    dot_general x24, matrix products, product(): return jnp.einsum(form, left, right, preferred_element_type=jnp.float32)  199 us
    all_gather x1, waiting for transfers between devices, local(): lax.all_gather(piece_up, 'seq', axis=1, tiled=True)  172 us
    all_gather x1, waiting for transfers between devices, local(): lax.all_gather(piece_down, 'seq', axis=1, tiled=True)  153 us
    dot_general x5, matrix products, gram_total(): partial_gram = jnp.dot(source, source.T, precision=highest)  139 us
    dot_general x5, matrix products, orthogonalize(): jnp.dot(mixing, orthogonal, precision=highest)  136 us
  transfers between devices with their start and end apart: 28, of which 19 were waited for; matrix products, arithmetic and copies ran while one was open for 42% of the time, Pallas kernels for 0%

commit v1 on v0

v1 whole, which is shorter than its diff:
```python
import functools
import math

import jax
import jax.numpy as jnp
from jax import lax
from jax.experimental import pallas as pl
from jax.experimental.pallas import tpu as pltpu
from jax.sharding import PartitionSpec as P

HEADS = 16
FF = 4304
LEN = 729
NS_ITERS = 5
STEP = 10

norm_eps = 1e-06
coef_a = 3.4445
coef_b = -4.775
coef_c = 2.0315
momentum_decay = 0.95
matrix_rate = 0.15
matrix_decay = 0.1
beta_first = 0.9
beta_second = 0.999
vector_rate = 0.5
adam_eps = 1e-08
low = jnp.bfloat16
f32 = jnp.float32


def call(body, name, **kw):
    vmem = kw.pop("vmem", 48)
    return pl.pallas_call(
        body,
        name=name,
        compiler_params=pltpu.CompilerParams(vmem_limit_bytes=vmem * 1024 * 1024),
        **kw,
    )


def dot(left, right, contract):
    return lax.dot_general(
        left, right, ((tuple(contract[:1]), tuple(contract[1:])), ((), ())), preferred_element_type=f32
    )


def split(x):
    top = x.astype(low)
    return top, (x - top.astype(f32)).astype(low)


def prep_square_body(slab_ref, out_ref):
    rows = slab_ref[:, 0, :]
    extra = out_ref.shape[0] - rows.shape[0]
    out_ref[...] = jnp.concatenate([rows, jnp.zeros((extra, rows.shape[1]), f32)], axis=0)


def prep_body(total, square_ref, slab_ref, out_ref):
    rows = slab_ref[:, 0, :]
    at = pl.program_id(0) * rows.shape[0] + lax.broadcasted_iota(jnp.int32, rows.shape, 0)
    rows = jnp.where(at < total, rows, 0.0)
    out_ref[...] = jnp.concatenate([square_ref[...], rows], axis=0).astype(low)


def prep(slab, heads, head_size, head_pad, parts, square_chunk, wide_chunk):
    total, _, width = slab.shape
    square = call(
        prep_square_body,
        "prep_square",
        grid=(heads,),
        in_specs=[pl.BlockSpec((head_size, 1, width), lambda i: (i, 0, 0))],
        out_specs=pl.BlockSpec((head_pad, width), lambda i: (i, 0)),
        out_shape=jax.ShapeDtypeStruct((parts * square_chunk, width), f32),
    )(slab)
    return call(
        functools.partial(prep_body, total),
        "prep",
        grid=(parts,),
        in_specs=[
            pl.BlockSpec((square_chunk, width), lambda i: (i, 0)),
            pl.BlockSpec((wide_chunk, 1, width), lambda i: (i, 0, 0)),
        ],
        out_specs=pl.BlockSpec((square_chunk + wide_chunk, width), lambda i: (i, 0)),
        out_shape=jax.ShapeDtypeStruct((parts * (square_chunk + wide_chunk), width), low),
    )(square, slab)


def momentum_body(total, moment_ref, grad_ref, first_ref, top_ref, rest_ref):
    grad = grad_ref[...].astype(f32)
    first = momentum_decay * moment_ref[:, 0, :] + grad
    first_ref[...] = first.reshape(first_ref.shape)
    at = pl.program_id(0) * grad.shape[0] + lax.broadcasted_iota(jnp.int32, grad.shape, 0)
    top, rest = split(jnp.where(at < total, grad + momentum_decay * first, 0.0))
    top_ref[...] = top
    rest_ref[...] = rest


def momentum(moments, grad):
    total, _, width = moments.shape
    rows_pad = grad.shape[0]
    block = rows_pad // 4
    slab_spec = pl.BlockSpec((block, 1, width), lambda i: (i, 0, 0))
    flat_spec = pl.BlockSpec((block, width), lambda i: (i, 0))
    return call(
        functools.partial(momentum_body, total),
        "momentum",
        grid=(4,),
        in_specs=[slab_spec, flat_spec],
        out_specs=[slab_spec, flat_spec, flat_spec],
        out_shape=[
            jax.ShapeDtypeStruct(moments.shape, f32),
            jax.ShapeDtypeStruct((rows_pad, width), low),
            jax.ShapeDtypeStruct((rows_pad, width), low),
        ],
    )(moments, grad)


def momentum_again_body(total, moment_ref, grad_ref, *refs):
    momentum_body(total, moment_ref, grad_ref, *refs[3:])


def momentum_again(moments, grad, first, top, rest):
    total, _, width = moments.shape
    rows = grad.shape[0]
    slab_spec = pl.BlockSpec((rows, 1, width), lambda i: (i, 0, 0))
    flat_spec = pl.BlockSpec((rows, width), lambda i: (i, 0))
    return call(
        functools.partial(momentum_again_body, total),
        "momentum_again",
        grid=(1,),
        in_specs=[slab_spec, flat_spec] + [pl.BlockSpec(memory_space=pl.ANY)] * 3,
        out_specs=[slab_spec, flat_spec, flat_spec],
        out_shape=[jax.ShapeDtypeStruct(x.shape, x.dtype) for x in (first, top, rest)],
        input_output_aliases={2: 0, 3: 1, 4: 2},
    )(moments, grad, first, top, rest)


def packed_at(column):
    return 128 * (column * (column + 1) // 2)


def gram_body(start, top_ref, rest_ref, *refs):
    base_ref, out_ref = (refs + refs)[:2] if len(refs) == 2 else (None, refs[0])
    width = top_ref.shape[1]
    depth = pl.ds(start, top_ref.shape[0] - start)
    for j in range(0, width, 256):
        wide = min(256, width - j)
        for i in range(0, j + wide, 256):
            tall = min(256, width - i)
            rows, columns = pl.ds(i, tall), pl.ds(j, wide)
            value = (
                dot(top_ref[depth, rows], top_ref[depth, columns], (0, 0))
                + dot(top_ref[depth, rows], rest_ref[depth, columns], (0, 0))
                + dot(rest_ref[depth, rows], top_ref[depth, columns], (0, 0))
            )
            for c in range(j // 128, (j + wide) // 128):
                used = min(tall, 128 * (c + 1) - i)
                lanes = 128 * c - j
                at = pl.ds(packed_at(c) + i, used)
                piece = value[:used, lanes : lanes + 128]
                out_ref[at, :] = piece if base_ref is None else base_ref[at, :] + piece


def gram_of(top, rest, start, depth, base=None):
    width = top.shape[1]
    count = width // 128
    part = pl.BlockSpec((depth, width), lambda i: (0, 0))
    whole = pl.BlockSpec((packed_at(count), 128), lambda i: (0, 0))
    bases = [] if base is None else [base]
    return call(
        functools.partial(gram_body, start),
        "gram" if base is None else "gram_add",
        grid=(1,),
        in_specs=[part, part] + [whole] * len(bases),
        out_specs=whole,
        out_shape=jax.ShapeDtypeStruct((packed_at(count), 128), f32),
    )(top, rest, *bases)


def iterate_body(
    total,
    rate_ref,
    gram_ref,
    top_hbm,
    rest_hbm,
    slab_hbm,
    out_hbm,
    a_top,
    a_rest,
    b_top,
    t_top,
    t_rest,
    x_ref,
    slab_ref,
    sem,
):
    width = a_top.shape[0]
    rows_pad = x_ref.shape[0]
    fetch_top = pltpu.make_async_copy(top_hbm, b_top.at[pl.ds(0, rows_pad)], sem.at[0])
    fetch_rest = pltpu.make_async_copy(rest_hbm, t_top.at[pl.ds(0, rows_pad)], sem.at[1])
    fetch_slab = pltpu.make_async_copy(slab_hbm, slab_ref.at[pl.ds(0, total)], sem.at[2])
    fetch_top.start()
    fetch_rest.start()
    fetch_slab.start()
    count = width // 128
    diagonal = lax.broadcasted_iota(jnp.int32, (128, 128), 0) == lax.broadcasted_iota(
        jnp.int32, (128, 128), 1
    )
    trace = jnp.zeros((128, 128), f32)
    for c in range(count):
        trace = trace + jnp.where(diagonal, gram_ref[pl.ds(packed_at(c) + 128 * c, 128), :], 0.0)
    scaling = 1.0 / (jnp.sqrt(jnp.sum(trace)) + 1e-07)
    squared = scaling * scaling

    def put(top_ref, rest_ref, i, j, value):
        tall, wide = value.shape
        top, rest = split(value)
        top_ref[pl.ds(i, tall), pl.ds(j, wide)] = top
        rest_ref[pl.ds(i, tall), pl.ds(j, wide)] = rest
        if i != j:
            top, rest = split(value.T)
            top_ref[pl.ds(j, wide), pl.ds(i, tall)] = top
            rest_ref[pl.ds(j, wide), pl.ds(i, tall)] = rest

    for c in range(count):
        for r in range(c + 1):
            put(a_top, a_rest, 128 * r, 128 * c, gram_ref[pl.ds(packed_at(c) + 128 * r, 128), :] * squared)

    step = rows_pad // 4
    fetch_top.wait()
    fetch_rest.wait()

    @pl.loop(0, 4)
    def _(r):
        rows = pl.ds(r * step, step)
        x_ref[rows, :] = (b_top[rows, :].astype(f32) + t_top[rows, :].astype(f32)) * scaling

    def both(top_ref, rest_ref, rows, columns):
        return top_ref[rows, columns].astype(f32) + rest_ref[rows, columns].astype(f32)

    def symmetric(left, rights, finish):
        for j in range(0, width, 256):
            wide = min(256, width - j)
            columns = pl.ds(j, wide)
            for i in range(0, j + wide, 256):
                rows = pl.ds(i, min(256, width - i))
                value = dot(left[rows, :], rights[0][:, columns], (1, 0))
                for right in rights[1:]:
                    value = value + dot(left[rows, :], right[:, columns], (1, 0))
                finish(i, j, rows, columns, value)


    def recenter(center):
        total_mean = jnp.zeros((128, 128), f32)
        for c in range(count):
            at = pl.ds(128 * c, 128)
            total_mean = total_mean + jnp.where(diagonal, both(a_top, a_rest, at, at), 0.0)
        mean = jnp.sum(total_mean) / width
        for c in range(count):
            at = pl.ds(128 * c, 128)
            top, rest = split(both(a_top, a_rest, at, at) - jnp.where(diagonal, mean, 0.0))
            a_top[at, at] = top
            a_rest[at, at] = rest
        return center + mean

    def mix(center):
        def finish(i, j, rows, columns, value):
            value = (coef_b + 2.0 * coef_c * center) * both(
                a_top, a_rest, rows, columns
            ) + coef_c * value
            b_top[rows, columns] = value.astype(low)
            if i != j:
                b_top[columns, rows] = value.T.astype(low)

        symmetric(a_top, (a_top,), finish)
        return coef_a + coef_b * center + coef_c * center * center

    def stepped(rows, lead):
        x = x_ref[rows, :]
        return lead * x + dot(x.astype(low), b_top[...], (1, 0))

    def propagate(center, lead, lefts, rights):
        tall = width // 3

        @pl.loop(0, 3)
        def _(r):
            rows = pl.ds(r * tall, tall)
            value = lead * both(a_top, a_rest, rows, slice(None)) + center * b_top[rows, :].astype(f32)
            for left in lefts:
                value = value + dot(left[rows, :], b_top[...], (1, 0))
            top, rest = split(value)
            t_top[rows, :] = top
            t_rest[rows, :] = rest

        def finish(i, j, rows, columns, value):
            carried = lead * both(t_top, t_rest, rows, columns)
            carried = carried + lead * center * b_top[rows, columns].astype(f32)
            put(a_top, a_rest, i, j, carried + value)

        symmetric(b_top, rights, finish)
        return lead * lead * center

    def sweep(center, lefts, rights):
        center = recenter(center)
        lead = mix(center)

        @pl.loop(0, 4)
        def _(r):
            rows = pl.ds(r * step, step)
            x_ref[rows, :] = stepped(rows, lead)

        return propagate(center, lead, lefts, rights)

    def exact(_, center):
        return sweep(center, (a_top, a_rest), (t_top, t_rest))

    center = lax.fori_loop(0, NS_ITERS - 2, exact, jnp.float32(0.0))
    center = sweep(center, (a_top,), (t_top,))
    lead = mix(recenter(center))
    fetch_slab.wait()
    rate = rate_ref[0]

    @pl.loop(0, 4)
    def _(r):
        rows = pl.ds(r * step, step)
        new = slab_ref[rows, 0, :] * (1.0 - matrix_rate * matrix_decay) - rate * stepped(rows, lead)
        slab_ref[rows, :, :] = new.reshape(step, 1, width)

    leave = pltpu.make_async_copy(slab_ref.at[pl.ds(0, total)], out_hbm, sem.at[3])
    leave.start()
    leave.wait()


def iterate(rate, gram, top, rest, slab):
    total, _, width = slab.shape
    rows_pad = top.shape[0]
    square = pltpu.VMEM((width, width), low)
    flops = 2 * width * width * (15 * width + 5 * rows_pad)
    return call(
        functools.partial(iterate_body, total),
        "iterate",
        vmem=56,
        in_specs=[
            pl.BlockSpec(memory_space=pltpu.SMEM),
            pl.BlockSpec(memory_space=pltpu.VMEM),
            pl.BlockSpec(memory_space=pl.ANY),
            pl.BlockSpec(memory_space=pl.ANY),
            pl.BlockSpec(memory_space=pl.ANY),
        ],
        out_specs=pl.BlockSpec(memory_space=pl.ANY),
        out_shape=jax.ShapeDtypeStruct(slab.shape, f32),
        scratch_shapes=[square] * 5
        + [
            pltpu.VMEM((rows_pad, width), f32),
            pltpu.VMEM((rows_pad, 1, width), f32),
            pltpu.SemaphoreType.DMA((4,)),
        ],
        cost_estimate=pl.CostEstimate(flops=flops, bytes_accessed=20_000_000, transcendentals=0),
    )(rate, gram, top, rest, slab)


def attend_body(scale, qkv_ref, context_ref, soft_ref):
    query, key, value = qkv_ref[0, 0], qkv_ref[1, 0], qkv_ref[2, 0]
    scores = dot(key, query, (0, 0)) * scale
    at = lax.broadcasted_iota(jnp.int32, scores.shape, 0)
    scores = jnp.where(at < LEN, scores, -1e30)
    exponent = jnp.exp(scores - jnp.max(scores, axis=0, keepdims=True))
    soft = (exponent / jnp.sum(exponent, axis=0, keepdims=True)).astype(low)
    soft_ref[0] = soft
    context = dot(value, soft, (1, 0))
    context_ref[0] = context[: context_ref.shape[1]].astype(low)


def attend(qkv, head_size, scale):
    _, groups, head_pad, rows = qkv.shape
    return call(
        functools.partial(attend_body, scale),
        "attend",
        grid=(groups,),
        in_specs=[pl.BlockSpec((3, 1, head_pad, rows), lambda h: (0, h, 0, 0))],
        out_specs=[
            pl.BlockSpec((1, head_size, rows), lambda h: (h, 0, 0)),
            pl.BlockSpec((1, rows, rows), lambda h: (h, 0, 0)),
        ],
        out_shape=[
            jax.ShapeDtypeStruct((groups, head_size, rows), low),
            jax.ShapeDtypeStruct((groups, rows, rows), low),
        ],
    )(qkv)


def attend_back_body(scale, qkv_ref, soft_ref, grad_ref, out_ref):
    query, key, value = qkv_ref[0, 0], qkv_ref[1, 0], qkv_ref[2, 0]
    grad, soft = grad_ref[0], soft_ref[0]
    grad_soft = dot(value, grad, (0, 0))
    soft_f32 = soft.astype(f32)
    along = jnp.sum(soft_f32 * grad_soft, axis=0, keepdims=True)
    grad_scores = (soft_f32 * (grad_soft - along)).astype(low)
    out_ref[0, 0] = (dot(key, grad_scores, (1, 0)) * scale).astype(low)
    out_ref[1, 0] = (dot(query, grad_scores, (1, 1)) * scale).astype(low)
    out_ref[2, 0] = dot(grad, soft, (1, 1)).astype(low)


def attend_back(qkv, soft, grad, scale):
    _, groups, head_pad, rows = qkv.shape
    three = pl.BlockSpec((3, 1, head_pad, rows), lambda h: (0, h, 0, 0))
    return call(
        functools.partial(attend_back_body, scale),
        "attend_back",
        grid=(groups,),
        in_specs=[
            three,
            pl.BlockSpec((1, rows, rows), lambda h: (h, 0, 0)),
            pl.BlockSpec((1, head_pad, rows), lambda h: (h, 0, 0)),
        ],
        out_specs=three,
        out_shape=jax.ShapeDtypeStruct(qkv.shape, low),
    )(qkv, soft, grad)


def whiten(inputs):
    average = jnp.mean(inputs, axis=-1, keepdims=True)
    centered = inputs - average
    variance = jnp.mean(centered * centered, axis=-1, keepdims=True)
    inverse = lax.rsqrt(variance + norm_eps)
    return centered * inverse, inverse


def whiten_back(grad, gain_row, hat, inverse):
    scaled = grad * gain_row
    mean_one = jnp.mean(scaled, axis=-1, keepdims=True)
    mean_two = jnp.mean(scaled * hat, axis=-1, keepdims=True)
    return inverse * (scaled - mean_one - hat * mean_two)


def gelu_both(inputs):
    squared = inputs * inputs
    curve = jnp.tanh(0.7978845608028654 * (inputs + 0.044715 * inputs * squared))
    value = 0.5 * inputs * (1.0 + curve)
    slope = 0.5 * (1.0 + curve) + 0.5 * inputs * (1.0 - curve * curve) * 0.7978845608028654 * (
        1.0 + 3.0 * 0.044715 * squared
    )
    return value, slope


def product(form, left, right):
    return jnp.einsum(form, left, right, preferred_element_type=f32)


def flip(x, axis, mask):
    count = lax.axis_size(axis)
    return lax.ppermute(x, axis, [(i, i ^ mask) for i in range(count)])


def gather_chunks(pieces):
    count = lax.axis_size("dp")
    half = count // 2
    me = lax.axis_index("dp")
    pair, core = me >> 1, me & 1
    joined = jnp.concatenate(pieces, axis=0) if len(pieces) > 1 else pieces[0]
    arrived = [joined] + [flip(joined, "dp", mask << 1) for mask in range(1, half)]
    result, at = [], 0
    for piece in pieces:
        whole = jnp.zeros((half, 2) + piece.shape, piece.dtype)
        for mask in range(half):
            part = arrived[mask][at : at + piece.shape[0]]
            whole = lax.dynamic_update_slice(whole, part[None, None], (pair ^ mask, core, 0, 0))
        mine = lax.dynamic_slice_in_dim(whole, core, 1, 1)
        other = flip(mine, "dp", 1)
        whole = lax.dynamic_update_slice_in_dim(whole, other, 1 - core, 1)
        result.append(whole.reshape((count,) + piece.shape))
        at += piece.shape[0]
    return result


def scatter_sum(whole, order):
    count, rows, columns = whole.shape
    bits = count.bit_length() - 1
    me = lax.axis_index("dp")
    whole = whole.reshape((2,) * bits + (rows, columns))
    for bit in order:
        at = bits - 1 - bit
        mine = (me >> bit) & 1
        kept = lax.dynamic_slice_in_dim(whole, mine, 1, at)
        sent = lax.dynamic_slice_in_dim(whole, 1 - mine, 1, at)
        got = flip(sent, "dp", 1 << bit)
        whole = (kept.astype(f32) + got.astype(f32)).astype(low)
    return whole.reshape(rows, columns)


def gather_seq(piece):
    count = lax.axis_size("seq")
    me = lax.axis_index("seq")
    whole = jnp.zeros((count,) + piece.shape, piece.dtype)
    whole = lax.dynamic_update_slice_in_dim(whole, piece[None], me, 0)
    for shift in range(1, count):
        got = lax.ppermute(piece, "seq", [(i, (i + shift) % count) for i in range(count)])
        whole = lax.dynamic_update_slice_in_dim(whole, got[None], (me - shift) % count, 0)
    return whole


def total_sum(x):
    for axis in ("dp", "seq"):
        step = 1
        while step < lax.axis_size(axis):
            x = x + flip(x, axis, step)
            step *= 2
    return x


def after(x, token):
    return x + jnp.minimum(jnp.abs(token), 0.0).astype(x.dtype)


def local(
    tokens, cotangent, counts, owner_table, owned_weights, owned_moments, vectors, vector_moments
):
    seq_count = lax.axis_size("seq")
    dp_count = lax.axis_size("dp")
    bits = dp_count.bit_length() - 1
    seq_index = lax.axis_index("seq")
    dp_index = lax.axis_index("dp")
    capacity = tokens.shape[1]
    width = tokens.shape[2]
    slots = capacity * seq_count
    head_size = width // HEADS
    head_pad = -(-head_size // 16) * 16
    heads = HEADS // seq_count
    score_scale = 1.0 / math.sqrt(head_size)
    widths = (width, width, width, width, FF, FF)
    cols = width // seq_count
    ff_cols = FF // seq_count
    share = -(-LEN // (16 * seq_count)) * 16
    packed = share * seq_count
    square_rows = heads * head_pad
    square_chunk = -(-square_rows // (8 * dp_count)) * 8
    square_total = square_chunk * dp_count
    sent_chunk = -(-(-(-ff_cols // dp_count) + square_chunk) // 16) * 16
    wide_chunk = sent_chunk - square_chunk
    wide_rows = wide_chunk * dp_count
    orders = (tuple(range(bits)), (0,) + tuple(range(bits - 1, 0, -1)))

    rows_in = tokens[0]
    vector_count = vectors.shape[0]
    vector_rows = -(-vector_count // width)
    extra = -(-vector_rows // 16) * 16
    payload = jnp.pad(vectors, (0, extra * width - vector_count)).reshape(extra, width)
    payload = jnp.concatenate([rows_in.astype(low), payload.astype(low)], axis=0)
    gathered = lax.all_gather(payload, "seq", axis=0, tiled=False)
    token_slots = gathered.reshape(seq_count * (capacity + extra), width)

    counts_row = counts[0]
    starts = jnp.cumsum(counts_row) - counts_row

    def rows_of(per):
        ids = jnp.arange(per * seq_count)
        real = (ids % per) < jnp.repeat(counts_row, per)
        return jnp.where(real, jnp.repeat(starts, per) + ids % per, packed)

    def picks(row):
        return (jnp.arange(packed)[:, None] == row[None, :]).astype(low)

    slot_row = rows_of(capacity)
    pick = picks(slot_row)
    token_pick = picks(rows_of(capacity + extra))
    own_row = lax.dynamic_slice_in_dim(slot_row, seq_index * capacity, capacity)
    own_pick = picks(own_row)
    own_valid = (own_row < packed)[:, None].astype(f32)
    cot_own = after((cotangent[0] * own_valid).astype(low), token_slots[0, 0])
    cot_slots = gather_seq(cot_own).reshape(slots, width)

    slab = jnp.transpose(owned_weights[0], (2, 1, 0))
    moments = jnp.transpose(owned_moments[0], (2, 1, 0))

    def send(x):
        return lax.all_to_all(x, "dp", split_axis=0, concat_axis=0, tiled=True)

    sent = prep(slab, heads, head_size, head_pad, dp_count, square_chunk, wide_chunk)
    got = send(sent.reshape(dp_count, sent_chunk, width))
    chunks = [lax.dynamic_index_in_dim(got, owner_table[m], 0, keepdims=False) for m in range(6)]
    squares = [chunk[:square_chunk] for chunk in chunks[:4]]
    (w_qkv,) = gather_chunks([jnp.concatenate(squares[:3], axis=0)])
    w_qkv = w_qkv.reshape(dp_count, 3, square_chunk, width).transpose(1, 0, 2, 3)
    w_qkv = w_qkv.reshape(3, square_total, width)[:, :square_rows].reshape(3 * square_rows, width)
    w_out_part = gather_seq(squares[3]).reshape(seq_count * square_chunk, width)
    w_out_part = after(w_out_part, w_qkv[0, 0])
    w_out, w_up, w_down = gather_chunks(
        [w_out_part, chunks[4][square_chunk:], chunks[5][square_chunk:]]
    )
    w_up = w_up.reshape(wide_rows, width)
    w_down = w_down.reshape(wide_rows, width)
    w_out = w_out.reshape(dp_count, seq_count, square_chunk, width).transpose(1, 0, 2, 3)
    w_out = w_out.reshape(seq_count, square_total, width)[:, :square_rows]
    w_out = w_out.reshape(seq_count * heads, head_pad, width)[:, :head_size].reshape(width, width)
    w_out_own = lax.dynamic_slice_in_dim(w_out, seq_index * cols, cols, axis=1)
    w_out_own = jnp.pad(
        w_out_own.reshape(width, heads, head_size), ((0, 0), (0, 0), (0, head_pad - head_size))
    ).reshape(width, square_rows)

    vector_full = gathered[:, capacity : capacity + vector_rows].reshape(seq_count, -1)
    vector_full = vector_full[:, :vector_count].reshape(-1).astype(f32)
    row_params = vector_full[: 8 * width].reshape(8, width)
    up_bias = lax.dynamic_slice_in_dim(vector_full, 8 * width + seq_index * ff_cols, ff_cols)
    up_bias = jnp.pad(up_bias, (0, wide_rows - ff_cols))

    def head_bias(row):
        own = lax.dynamic_slice_in_dim(row, seq_index * cols, cols).reshape(heads, head_size)
        return jnp.pad(own, ((0, 0), (0, head_pad - head_size))).reshape(square_rows)

    qkv_bias = jnp.concatenate(
        [head_bias(row_params[2]), jnp.zeros((square_rows,), f32), head_bias(row_params[3])]
    )

    token_rows = product("rc,cd->rd", token_pick, token_slots)
    normed = (whiten(token_rows)[0] * row_params[0] + row_params[1]).astype(low)
    qkv = (product("ed,rd->er", w_qkv, normed) + qkv_bias[:, None]).astype(low)
    qkv = qkv.reshape(3, heads, head_pad, packed)
    context_own, soft = attend(qkv, head_size, score_scale)
    context = lax.all_gather(context_own.reshape(cols, packed), "seq", axis=0, tiled=True)
    grad_rows = product("rc,cd->rd", pick, cot_slots).astype(low)
    middle = token_rows + product("er,oe->ro", context, w_out) + after(row_params[4], grad_rows[0, 0])
    hat_two, inverse_two = whiten(middle)
    normed_two = (hat_two * row_params[5] + row_params[6]).astype(low)
    pre_act = product("rd,fd->rf", normed_two, w_up) + up_bias
    hidden_f32, slope = gelu_both(pre_act)
    hidden = hidden_f32.astype(low)

    grad_hidden = product("rd,fd->rf", grad_rows, w_down)
    grad_pre = (slope * grad_hidden).astype(low)
    grad_normed_two_part = product("rf,fd->rd", grad_pre, w_up).astype(low)
    token = grad_normed_two_part[0, 0]
    hidden_late = after(hidden, token)
    grad_pre_late = after(grad_pre, token)
    grad_down = product("rf,rd->fd", hidden_late, grad_rows)
    grad_up = product("rf,rd->fd", grad_pre_late, normed_two)
    grad_up_bias = jnp.sum(grad_pre_late.astype(f32), axis=0)[:ff_cols]

    def parts(x, rows):
        return x.astype(low).reshape(dp_count, rows, width)

    sum_down = scatter_sum(parts(grad_down, wide_chunk), orders[0])
    sum_up = scatter_sum(parts(grad_up, wide_chunk), orders[1])
    grad_normed_two = after(
        lax.psum_scatter(grad_normed_two_part, "seq", scatter_dimension=0, tiled=True),
        sum_down[0, 0] + sum_up[0, 0],
    ).astype(f32)

    def to_owner(pairs):
        total = 0
        for piece, m in pairs:
            here = (jnp.arange(dp_count) == owner_table[m])[:, None, None]
            total = total + jnp.where(here, piece[None], jnp.zeros((), low))
        return total

    back_wide = send(to_owner([(sum_up, 4), (sum_down, 5)])).reshape(wide_rows, width)
    first_moment, top, rest = momentum(moments, back_wide)
    early_gram = gram_of(top, rest, cols, wide_rows)

    def own_share(x):
        return lax.dynamic_slice_in_dim(x, seq_index * share, share)

    own_grad = own_share(grad_rows).astype(f32)
    own_hat = own_share(hat_two)
    grad_bias_down = jnp.sum(own_grad, axis=0)
    grad_gain_two = jnp.sum(grad_normed_two * own_hat, axis=0)
    grad_shift_two = jnp.sum(grad_normed_two, axis=0)
    grad_mid_norm = whiten_back(grad_normed_two, row_params[5], own_hat, own_share(inverse_two))
    grad_attn_own = (own_grad + grad_mid_norm).astype(low)
    grad_bias_out = jnp.sum(grad_attn_own.astype(f32), axis=0)
    grad_attn = lax.all_gather(grad_attn_own, "seq", axis=0, tiled=True)

    grad_context = product("de,rd->er", w_out_own, grad_attn).astype(low)
    grad_qkv = attend_back(qkv, soft, grad_context.reshape(heads, head_pad, packed), score_scale)
    grad_qkv_flat = grad_qkv.reshape(3 * square_rows, packed)
    grad_attn_cols = lax.dynamic_slice_in_dim(grad_attn, seq_index * cols, cols, axis=1)
    grad_w_out = product("rd,er->de", grad_attn_cols, context)
    grad_w_qkv = product("er,rd->ed", grad_qkv_flat, normed)
    grad_qkv_bias = jnp.sum(grad_qkv.astype(f32), axis=3)[:, :, :head_size].reshape(3, cols)

    grad_normed_part = product("er,ed->rd", grad_qkv_flat, w_qkv) + jnp.minimum(
        jnp.abs(grad_w_qkv[0, 0] + grad_w_out[0, 0]), 0.0
    )
    unpick = (slot_row[:, None] == jnp.arange(packed)[None, :]).astype(low)
    grad_normed_slots = product("cr,rd->cd", unpick, grad_normed_part.astype(low)).astype(low)
    grad_normed = lax.psum_scatter(
        grad_normed_slots, "seq", scatter_dimension=0, tiled=True
    ).astype(f32)

    def square_parts(x):
        x = jnp.pad(x.astype(low), ((0, square_total - square_rows), (0, 0)))
        return x.reshape(dp_count, square_chunk, width)

    late = [square_parts(grad_w_qkv[m * square_rows : (m + 1) * square_rows]) for m in range(3)]
    grad_w_out = jnp.pad(
        grad_w_out.reshape(heads, head_size, width), ((0, 0), (0, head_pad - head_size), (0, 0))
    )
    late.append(square_parts(grad_w_out.reshape(square_rows, width)))
    token = back_wide[0, 0]
    sum_qk = scatter_sum(after(jnp.concatenate(late[:2], axis=1), token), orders[0])
    sum_vo = scatter_sum(after(jnp.concatenate(late[2:], axis=1), token), orders[1])
    back_square = send(
        to_owner(
            [
                (sum_qk[:square_chunk], 0),
                (sum_qk[square_chunk:], 1),
                (sum_vo[:square_chunk], 2),
                (sum_vo[square_chunk:], 3),
            ]
        )
    ).reshape(square_total, width)[:square_rows]
    back_square = back_square.reshape(heads, head_pad, width)[:, :head_size].reshape(cols, width)
    first_moment, top, rest = momentum_again(
        moments, back_wide[:cols] + back_square, first_moment, top, rest
    )
    partial_gram = gram_of(top, rest, 0, cols, early_gram)
    partial_gram = after(partial_gram, grad_normed[0, 0])
    gram_share = lax.psum_scatter(partial_gram, "seq", scatter_dimension=0, tiled=True)
    first_gram = lax.all_gather(gram_share, "seq", axis=0, tiled=True)
    token = first_gram[0, 0]
    update_scale = jnp.zeros((), f32)
    for m in range(6):
        update_scale = jnp.where(
            owner_table[m] == dp_index,
            jnp.float32(matrix_rate * 0.2 * math.sqrt(max(width, widths[m]))),
            update_scale,
        )
    updated = iterate(update_scale.reshape(1), first_gram, top, rest, slab)

    placed_middle = jnp.where(
        (jnp.arange(packed) // share == seq_index)[:, None], middle + row_params[7], 0.0
    )
    out_part = (product("rf,fd->rd", hidden, w_down) + placed_middle).astype(low)
    out_slots = after(product("cr,rd->cd", unpick, out_part).astype(low), token)
    block_out = lax.psum_scatter(out_slots, "seq", scatter_dimension=0, tiled=True).astype(f32)
    hat_one, inverse_one = whiten(rows_in)
    grad_gain_one = jnp.sum(grad_normed * hat_one, axis=0)
    grad_shift_one = jnp.sum(grad_normed, axis=0)
    grad_in_norm = whiten_back(grad_normed, row_params[0], hat_one, inverse_one)
    grad_mid_slots = product("rc,rd->cd", own_pick, grad_attn)
    grad_tokens = (grad_mid_slots + grad_in_norm) * own_valid

    def spot(piece):
        return lax.dynamic_update_slice_in_dim(
            jnp.zeros((piece.shape[0] * seq_count,), f32), piece, seq_index * piece.shape[0], 0
        )

    vector_grad = jnp.concatenate(
        [
            grad_gain_one,
            grad_shift_one,
            spot(grad_qkv_bias[0]),
            spot(grad_qkv_bias[2]),
            grad_bias_out,
            grad_gain_two,
            grad_shift_two,
            grad_bias_down,
            spot(grad_up_bias),
        ]
    )
    padded = -(-vector_grad.shape[0] // 1024) * 1024
    vector_grad = jnp.pad(vector_grad, (0, padded - vector_grad.shape[0])).reshape(-1, 128)
    vector_sum = total_sum(vector_grad).reshape(-1)
    vector_total = lax.dynamic_slice_in_dim(vector_sum, seq_index * vector_count, vector_count)

    first_new = beta_first * vector_moments[0] + (1.0 - beta_first) * vector_total
    second_new = beta_second * vector_moments[1] + (1.0 - beta_second) * vector_total * vector_total
    first_fix = 1.0 - beta_first**STEP
    second_fix = 1.0 - beta_second**STEP
    vector_new = vectors - vector_rate * (first_new / first_fix) / (
        jnp.sqrt(second_new / second_fix) + adam_eps
    )
    return (
        block_out[None],
        grad_tokens[None],
        jnp.transpose(first_moment, (2, 1, 0))[None],
        jnp.transpose(updated, (2, 1, 0))[None],
        first_new,
        second_new,
        vector_new,
    )


def solution(mesh):
    in_specs = (
        P("dp", "seq", None),
        P("dp", "seq", None),
        P("dp", None),
        P(),
        P("dp", None, "seq", None),
        P("dp", None, "seq", None),
        P("seq"),
        P(None, "seq"),
    )
    out_specs = (
        P("dp", "seq", None),
        P("dp", "seq", None),
        P("dp", None, "seq", None),
        P("dp", None, "seq", None),
        P("seq"),
        P("seq"),
        P("seq"),
    )
    return jax.shard_map(local, mesh=mesh, in_specs=in_specs, out_specs=out_specs, check_vma=False)
```

time: 3090 us -> 654 us (0.21)
  blocking collectives: 1050 us -> 0 us
  waiting for transfers between devices: 1280 us -> 245 us
  matrix products: 531 us -> 65 us
  Pallas kernels: 0 us -> 142 us
  local copies, waits for them, and re-layouts: 148 us -> 66.6 us
  starting transfers between devices: 4.68 us -> 53.6 us
    unnamed x4 -> x0, blocking collectives: 1030 us -> none
    all_gather x13 -> x4, waiting for transfers between devices: 834 us -> 44.7 us  [the longest x1 28.2 us: local(): first_gram = lax.all_gather(gram_share, 'seq', axis=0, tiled=True)]
    dot_general x39 -> x15, matrix products: 531 us -> 65 us  [product(): return jnp.einsum(form, left, right, preferred_element_type=f32)]
    psum x2 -> x0, waiting for transfers between devices: 239 us -> none  [the longest x1 123 us: spread(): return lax.psum(jnp.where(mine, x, jnp.zeros_like(x)), axis)]
    reduce_scatter x11 -> x4, waiting for transfers between devices: 207 us -> 59.6 us  [the longest x1 55.2 us: local(): lax.psum_scatter(partial_gram, 'seq', scatter_dimension=0, tiled=True)]
    pallas_call x0 -> x9, Pallas kernels: none -> 142 us  [the longest x1 90.9 us: iterate(): call(functools.partial(iterate_body, total), 'iterate', vmem=56, in_specs...]
    unnamed x182 -> x134, local copies, waits for them, and re-layouts: 129 us -> 15.8 us
    ppermute x0 -> x33, waiting for transfers between devices: none -> 90.3 us  [the longest x27 51 us: flip(): return lax.ppermute(x, axis, [(i, i ^ mask) for i in range(count)])]
  transfers between devices with their start and end apart: 28 -> 44, of which waited for: 19 -> 24; matrix products, arithmetic and copies ran while one was open for 42% -> 15% of each run, Pallas kernels for 0% -> 19%
where the time goes in v1:
time: 654 us; the launch traced here: 649 us
  waiting for transfers between devices  245 us (37%)
  Pallas kernels  142 us (22%)
  local copies, waits for them, and re-layouts  66.6 us (10%)
  matrix products  65 us (10%)
  starting transfers between devices  53.6 us (8%)
  other arithmetic  38.7 us (6%)
  between operations  38.1 us (6%)
    pallas_call x1, Pallas kernels, iterate(): call(functools.partial(iterate_body, total), 'iterate', vmem=56, in_specs...  90.9 us
    dot_general x15, matrix products, product(): return jnp.einsum(form, left, right, preferred_element_type=f32)  65 us
    reduce_scatter x1, waiting for transfers between devices, local(): lax.psum_scatter(partial_gram, 'seq', scatter_dimension=0, tiled=True)  55.2 us
    ppermute x27, waiting for transfers between devices, flip(): return lax.ppermute(x, axis, [(i, i ^ mask) for i in range(count)])  51 us
    all_to_all x3, waiting for transfers between devices, send(): return lax.all_to_all(x, 'dp', split_axis=0, concat_axis=0, tiled=True)  50.3 us
    ppermute x6, waiting for transfers between devices, gather_seq(): lax.ppermute(piece, 'seq', [(i, (i + shift) % count) for i in range(count)])  39.2 us
    all_gather x1, waiting for transfers between devices, local(): first_gram = lax.all_gather(gram_share, 'seq', axis=0, tiled=True)  28.2 us
    ppermute x27, starting transfers between devices, flip(): return lax.ppermute(x, axis, [(i, i ^ mask) for i in range(count)])  24 us
  transfers between devices with their start and end apart: 44, of which 24 were waited for; matrix products, arithmetic and copies ran while one was open for 15% of the time, Pallas kernels for 19%

profile of v1, /device:TPU:0, one launch (start us, length us, event | category | flops | bytes accessed | tf_op | source)
XLA Modules:
  0.0 648.8 jit_solution(13824597200628569174)
XLA Ops:
  7.2 2.2 prep_square.1.square_ref
  9.4 6.9 %prep.1 = bf16[1408,1152]{1,0:T(8,128)(2,1)} custom-call(f32[320,1152]{1,0:T(8,128)S(1)} %prep_square.1.square_ref, f32[1076,1,1152]{2,1,0:T(1,128)} %bitcast.217), custom_call_target="tpu_custom_call" | custom-call | tf_op jit(solution)/shard_map/prep/pallas_call | solution.py:76
  16.4 5.3 all-to-all-start
  36.9 23.8 %all-to-all-done = bf16[8,176,1152]{2,1,0:T(8,128)(2,1)} async-done(((bf16[8,176,1152]{2,1,0:T(8,128)(2,1)}), bf16[8,176,1152]{2,1,0:T(8,128)(2,1)}, u32[]{:S(2)}, u32[]{:S(2)}) %all-to-all-start) | async-done | bytes 3244064 | tf_op jit(solution)/shard_map/all_to_all | solution.py:577
  61.8 4.3 collective-permute-start.6
  71.0 2.4 dynamic-slice_bitcast_fusion.1
  73.7 4.9 collective-permute-done.4
  80.1 4.7 collective-permute-done.5
  91.4 6.6 %collective-permute-start.12 = (bf16[256,1152]{1,0:T(8,128)(2,1)}, bf16[256,1152]{1,0:T(8,128)(2,1)}, u32[]{:S(2)}, u32[]{:S(2)}) collective-permute-start(bf16[256,1152]{1,0:T(8,128)(2,1)} %fusion.28), channel_id=1, source_target_pairs={{0,2},{1,3},{2,0},{3,1},{4,6},{5,7},{6,4},{7,5},{8,10},{9,11},{10,... | collective-permute-start | bytes 1769480 | tf_op jit(solution)/shard_map/ppermute | solution.py:498
  98.0 2.5 collective-permute-start.11
  101.5 6.2 fusion.67
  107.8 2.5 multiply_reduce_fusion.1
  114.3 2.7 collective-permute-start.9
  117.8 21.1 %collective-permute-done.11 = bf16[256,1152]{1,0:T(8,128)(2,1)} collective-permute-done((bf16[256,1152]{1,0:T(8,128)(2,1)}, bf16[256,1152]{1,0:T(8,128)(2,1)}, u32[]{:S(2)}, u32[]{:S(2)}) %collective-permute-start.11) | collective-permute-done | bytes 589856 | tf_op jit(solution)/shard_map/ppermute | solution.py:498
  141.6 8.6 %collective-permute-done.12 = bf16[256,1152]{1,0:T(8,128)(2,1)} collective-permute-done((bf16[256,1152]{1,0:T(8,128)(2,1)}, bf16[256,1152]{1,0:T(8,128)(2,1)}, u32[]{:S(2)}, u32[]{:S(2)}) %collective-permute-start.12) | collective-permute-done | bytes 589856 | tf_op jit(solution)/shard_map/ppermute | solution.py:498
  152.5 2.3 convolution_convert_fusion.5
  158.0 4.9 add_convert_fusion.2
  162.9 6.5 attend.1
  169.6 2.0 fusion.42
  171.6 1.9 fusion.41
  174.4 2.7 constant_dynamic-slice_fusion.14
  177.1 2.5 constant_dynamic-slice_fusion.13
  185.3 2.6 constant_dynamic-update-slice_fusion
  187.9 2.5 constant_dynamic-update-slice_fusion.1
  192.5 15.8 %all-gather.6.cloned.1.call-done = bf16[1152,768]{1,0:T(8,128)(2,1)} async-done(((bf16[288,768]{1,0:T(8,128)(2,1)}), bf16[1152,768]{1,0:T(8,128)(2,1)}) %all-gather.6.cloned.1.call-update) | async-done | bytes 1769488 | tf_op jit(solution)/shard_map/all_gather | solution.py:620
  208.3 6.1 fusion.68
  217.9 2.4 convolution_add_fusion
  220.3 3.9 fusion.3
  225.4 2.7 convolution_convert_fusion.4
  229.4 5.0 convolution_convert_fusion.1
  237.3 3.1 convolution_convert_fusion
  243.7 2.1 add_convert_fusion.4
  247.5 1.8 add_convert_fusion.3
  250.7 11.8 %collective-permute-done.17 = bf16[1,2,1,136,1152]{4,3,2,1,0:T(8,128)(2,1)S(1)} collective-permute-done((bf16[1,2,1,136,1152]{4,3,2,1,0:T(8,128)(2,1)S(1)}, bf16[1,2,1,136,1152]{4,3,2,1,0:T(8,128)(2,1)S(1)}, u32[]{:S(2)}, u32[]{:S(2)}) %collective-permute-start.17) | collective-permute-done | bytes 626720 | tf_op jit(solution)/shard_map/ppermute | solution.py:453
  266.3 6.0 collective-permute-done.18
  272.9 1.7 collective-permute-done.21
  276.5 4.3 reduce-scatter.5.cloned.1.call-done
  282.6 2.6 convert_reduce_fusion.5
  285.2 2.2 select_add_fusion
  287.4 4.4 all-to-all-start.1
  296.3 26.5 %all-to-all-done.1 = bf16[8,136,1152]{2,1,0:T(8,128)(2,1)} async-done(((bf16[8,136,1152]{2,1,0:T(8,128)(2,1)}), bf16[8,136,1152]{2,1,0:T(8,128)(2,1)}, u32[]{:S(2)}, u32[]{:S(2)}) %all-to-all-start.1) | async-done | bytes 2506784 | tf_op jit(solution)/shard_map/all_to_all | solution.py:577
  324.7 3.9 fusion.69
  330.1 9.1 %attend_back.1 = bf16[3,4,80,768]{3,2,1,0:T(8,128)(2,1)S(1)} custom-call(bf16[3,4,80,768]{3,2,1,0:T(8,128)(2,1)S(1)} %bitcast.210, bf16[4,768,768]{2,1,0:T(8,128)(2,1)} %get-tuple-element.16.soft_ref, bf16[4,80,768]{2,1,0:T(8,128)(2,1)S(1)} %bitcast.213), custom_call_target="tpu_custom_call" | custom-call | tf_op jit(solution)/shard_map/attend_back/pallas_call | solution.py:408
  339.3 2.3 fusion.70
  345.6 7.5 %convolution_convert_fusion.2 = bf16[1024,1152]{1,0:T(8,128)(2,1)} fusion(s32[1024]{0:T(1024)S(1)} %copy-done.53, bf16[960,768]{1,0:T(8,128)(2,1)S(1)} %bitcast.212, bf16[960,1152]{1,0:T(8,128)(2,1)} %bitcast.245, f32[]{:T(128)} %bitcast.86), kind=kOutput, calls=%fused_computation.8 | convolution fusion | flops 3514368000 | bytes 6049796 | tf_op jit(solution)/shard_map/cr,rd->cd/dot_general | solution.py:448
  360.0 7.2 %collective-permute-done.23 = bf16[2,1,1,80,1152]{4,3,2,1,0:T(8,128)(2,1)S(1)} collective-permute-done((bf16[2,1,1,80,1152]{4,3,2,1,0:T(8,128)(2,1)S(1)}, bf16[2,1,1,80,1152]{4,3,2,1,0:T(8,128)(2,1)S(1)}, u32[]{:S(2)}, u32[]{:S(2)}) %collective-permute-start.23) | collective-permute-done | bytes 368672 | tf_op jit(solution)/shard_map/ppermute | solution.py:453
  370.6 2.7 collective-permute-done.24
  376.1 3.6 all-to-all-start.2
  379.7 7.8 %momentum.1 = (f32[1076,1,1152]{2,1,0:T(1,128)}, bf16[1088,1152]{1,0:T(8,128)(2,1)S(1)}, bf16[1088,1152]{1,0:T(8,128)(2,1)S(1)}) custom-call(f32[1076,1,1152]{2,1,0:T(1,128)} %bitcast.214, bf16[1088,1152]{1,0:T(8,128)(2,1)} %bitcast.67.grad_ref), custom_call_target="tpu_custom_call" | custom-call | tf_op jit(solution)/shard_map/momentum/pallas_call | solution.py:105
  387.5 7.5 %gram.1.refs_0_ = f32[5760,128]{1,0:T(8,128)} custom-call(bf16[1088,1152]{1,0:T(8,128)(2,1)S(1)} %get-tuple-element.18.refs_1_.top_ref, bf16[1088,1152]{1,0:T(8,128)(2,1)S(1)} %get-tuple-element.19.refs_2_.rest_ref), custom_call_target="tpu_custom_call" | custom-call | tf_op jit(solution)/shard_map/gram/pallas_call | solution.py:171
  398.4 3.4 momentum_again.1
  401.9 7.4 %gram_add.1 = f32[5760,128]{1,0:T(8,128)} custom-call(bf16[1088,1152]{1,0:T(8,128)(2,1)S(1)} %get-tuple-element.20.top_ref.top_hbm, bf16[1088,1152]{1,0:T(8,128)(2,1)S(1)} %get-tuple-element.21.rest_ref.rest_hbm, f32[5760,128]{1,0:T(8,128)} %gram.1.refs_0_), custom_call_target="tpu_custom_call" | custom-call | tf_op jit(solution)/shard_map/gram_add/pallas_call | solution.py:171
  412.5 3.6 broadcast_add_fusion
  417.7 55.2 %reduce-scatter.9.cloned.1.call-done = f32[1440,128]{1,0:T(8,128)} async-done(((f32[5760,128]{1,0:T(8,128)}), f32[1440,128]{1,0:T(8,128)}) %reduce-scatter.9.cloned.1.call-update) | async-done | bytes 737296 | tf_op jit(solution)/shard_map/reduce_scatter | solution.py:718
  473.2 1.9 convert_reduce_fusion
  483.6 2.2 collective-permute-done.29
  487.4 2.7 collective-permute-done.30
  491.1 7.4 %collective-permute-done.31 = f32[112,128]{1,0:T(8,128)S(1)} collective-permute-done((f32[112,128]{1,0:T(8,128)S(1)}, f32[112,128]{1,0:T(8,128)S(1)}, u32[]{:S(2)}, u32[]{:S(2)}) %collective-permute-start.31) | collective-permute-done | bytes 57376 | tf_op jit(solution)/shard_map/ppermute | solution.py:453
  498.9 4.1 fusion.7
  502.9 5.2 collective-permute-done.32
  508.9 28.2 %all-gather.10.cloned.1.call-done.gram_ref = f32[5760,128]{1,0:T(8,128)} async-done(((f32[1440,128]{1,0:T(8,128)}), f32[5760,128]{1,0:T(8,128)}) %all-gather.10.cloned.1.call-update) | async-done | bytes 2949136 | tf_op jit(solution)/shard_map/all_gather | solution.py:719
  539.0 9.7 %fusion.5 = bf16[1024,1152]{1,0:T(8,128)(2,1)} fusion(s32[1024]{0:T(1024)} %copy-done.52, bf16[]{:T(256)} %bitcast.88, f32[768,1152]{1,0:T(8,128)S(1)} %copy-done.11, bf16[1088,1152]{1,0:T(8,128)(2,1)} %bitcast.224, f32[1152]{0:T(1024)} %get-tuple-element.63, pred[768]{0:T(1024)(128)(4,1)} %fusion.49, f32[768,1088]{0,1:T(8,128)} %copy-done.58), kind=kOutput, calls=%fused_computation.25 | convolution fusion | flops 3754868736 | bytes 11756802 | tf_op jit(solution)/shard_map/cr,rd->cd/dot_general | solution.py:448
  548.6 90.9 %iterate.1 = f32[1076,1,1152]{2,1,0:T(1,128)} custom-call(f32[1]{0:T(128)} %bitcast.93.rate_ref, f32[5760,128]{1,0:T(8,128)} %all-gather.10.cloned.1.call-done.gram_ref, bf16[1088,1152]{1,0:T(8,128)(2,1)} %copy-done, bf16[1088,1152]{1,0:T(8,128)(2,1)} %copy-done.3, f32[1076,1,1152]{2,1,0:T(1,128)} %bitcast.218), custom_call_target="tpu_custom_call" | custom-call | flops 60303605760 | bytes 20000000 | tf_op jit(solution)/shard_map/iterate/pallas_call | solution.py:340
  639.6 2.2 bitcast_convert_fusion.1
  (355 shorter events, 99.9 us)
Async XLA Ops:
  16.4 44.3 %all-to-all-start = ((bf16[8,176,1152]{2,1,0:T(8,128)(2,1)}), bf16[8,176,1152]{2,1,0:T(8,128)(2,1)}, u32[]{:S(2)}, u32[]{:S(2)}) async-start(bf16[8,176,1152]{2,1,0:T(8,128)(2,1)} %bitcast.6), calls=%async_computation | async-start | bytes 6488064 | tf_op jit(solution)/shard_map/all_to_all | solution.py:577
  21.7 10.1 %copy-start.57 = (s32[1,4]{1,0:T(1,128)S(1)}, s32[1,4]{1,0:T(1,128)}, u32[]{:S(2)}) copy-start(s32[1,4]{1,0:T(1,128)} %param.10) | copy-start | bytes 52
  21.7 66.0 %all-gather.12.cloned.1.call-start = ((), (), s32[]{:S(2)}) async-start(), calls=%async_computation.14 | async-start | bytes 3133440 | tf_op jit(solution)/shard_map/all_gather | solution.py:550
  23.5 184.8 %all-gather.6.cloned.1.call-start = ((), (), s32[]{:S(2)}) async-start(), calls=%async_computation.7 | async-start | bytes 2211840 | tf_op jit(solution)/shard_map/all_gather | solution.py:620
  36.2 116.3 %copy-start.52 = (s32[1024]{0:T(1024)}, s32[1024]{0:T(1024)S(1)}, u32[]{:S(2)}) copy-start(s32[1024]{0:T(1024)S(1)} %add_select_fusion.4) | copy-start | bytes 12292
  36.9 74.2 %copy-start.47 = (f32[256]{0:T(256)}, f32[256]{0:T(256)S(1)}, u32[]{:S(2)}) copy-start(f32[256]{0:T(256)S(1)} %get-tuple-element.38) | copy-start | bytes 3076
  61.8 23.0 %collective-permute-start.6 = (bf16[40,1152]{1,0:T(8,128)(2,1)S(1)}, bf16[40,1152]{1,0:T(8,128)(2,1)S(1)}, u32[]{:S(2)}, u32[]{:S(2)}) collective-permute-start(bf16[40,1152]{1,0:T(8,128)(2,1)S(1)} %get-tuple-element.41), channel_id=1, source_target_pairs={{0,3},{1,0},{2,1},{3,2},{4,7},{5,4},{6,5},{7,6},{8,11},{9,8},{10,9... | collective-permute-start | bytes 276488 | tf_op jit(solution)/shard_map/ppermute | solution.py:498
  66.1 18.7 %collective-permute-start.5 = (bf16[40,1152]{1,0:T(8,128)(2,1)S(1)}, bf16[40,1152]{1,0:T(8,128)(2,1)S(1)}, u32[]{:S(2)}, u32[]{:S(2)}) collective-permute-start(bf16[40,1152]{1,0:T(8,128)(2,1)S(1)} %get-tuple-element.41), channel_id=1, source_target_pairs={{0,2},{1,3},{2,0},{3,1},{4,6},{5,7},{6,4},{7,5},{8,10},{9,11},{10,... | collective-permute-start | bytes 276488 | tf_op jit(solution)/shard_map/ppermute | solution.py:498
  66.1 12.4 %collective-permute-start.4 = (bf16[40,1152]{1,0:T(8,128)(2,1)S(1)}, bf16[40,1152]{1,0:T(8,128)(2,1)S(1)}, u32[]{:S(2)}, u32[]{:S(2)}) collective-permute-start(bf16[40,1152]{1,0:T(8,128)(2,1)S(1)} %get-tuple-element.41), channel_id=1, source_target_pairs={{0,1},{1,2},{2,3},{3,0},{4,5},{5,6},{6,7},{7,4},{8,9},{9,10},{10,1... | collective-permute-start | bytes 276488 | tf_op jit(solution)/shard_map/ppermute | solution.py:498
  67.2 17.7 %collective-permute-start.1 = (bf16[120,1152]{1,0:T(8,128)(2,1)S(1)}, bf16[120,1152]{1,0:T(8,128)(2,1)S(1)}, u32[]{:S(2)}, u32[]{:S(2)}) collective-permute-start(bf16[120,1152]{1,0:T(8,128)(2,1)S(1)} %pad_maximum_fusion.2), channel_id=1, source_target_pairs={{0,16},{4,20},{8,24},{12,28},{16,0},{20,4},{24,8},{28,12},{1,17},{... | collective-permute-start | bytes 829448 | tf_op jit(solution)/shard_map/ppermute | solution.py:453
  67.8 17.1 %collective-permute-start = (bf16[120,1152]{1,0:T(8,128)(2,1)S(1)}, bf16[120,1152]{1,0:T(8,128)(2,1)S(1)}, u32[]{:S(2)}, u32[]{:S(2)}) collective-permute-start(bf16[120,1152]{1,0:T(8,128)(2,1)S(1)} %pad_maximum_fusion.2), channel_id=1, source_target_pairs={{0,8},{4,12},{8,0},{12,4},{16,24},{20,28},{24,16},{28,20},{1,9},{5... | collective-permute-start | bytes 829448 | tf_op jit(solution)/shard_map/ppermute | solution.py:453
  71.0 13.9 %copy-start.17 = (bf16[4,2,136,1152]{3,2,1,0:T(8,128)(2,1)}, bf16[4,2,136,1152]{3,2,1,0:T(8,128)(2,1)S(1)}, u32[]{:S(2)}) copy-start(bf16[4,2,136,1152]{3,2,1,0:T(8,128)(2,1)S(1)} %bitcast_dynamic-update-slice_fusion.3) | copy-start | bytes 7520260
  73.6 15.9 %copy-start.19 = (f32[1,256,1152]{2,1,0:T(8,128)S(1)}, f32[1,256,1152]{2,1,0:T(8,128)}, u32[]{:S(2)}) copy-start(f32[1,256,1152]{2,1,0:T(8,128)} %param.9) | copy-start | bytes 3538948
  78.5 7.4 %collective-permute-start.2 = (bf16[120,1152]{1,0:T(8,128)(2,1)S(1)}, bf16[120,1152]{1,0:T(8,128)(2,1)S(1)}, u32[]{:S(2)}, u32[]{:S(2)}) collective-permute-start(bf16[120,1152]{1,0:T(8,128)(2,1)S(1)} %pad_maximum_fusion.2), channel_id=1, source_target_pairs={{0,24},{4,28},{8,16},{12,20},{16,8},{20,12},{24,0},{28,4},{1,25},{... | collective-permute-start | bytes 829448 | tf_op jit(solution)/shard_map/ppermute | solution.py:453
  87.1 24.2 %collective-permute-start.3 = (bf16[4,1,120,1152]{3,2,1,0:T(8,128)(2,1)}, bf16[4,1,120,1152]{3,2,1,0:T(8,128)(2,1)}, u32[]{:S(2)}, u32[]{:S(2)}) collective-permute-start(bf16[4,1,120,1152]{3,2,1,0:T(8,128)(2,1)} %constant_dynamic-slice_fusion.16), channel_id=1, source_target_pairs={{0,4},{4,0},{8,12},{12,8},{16,20},{20,16},{24,28},{28,24},{1,5},{5... | collective-permute-start | bytes 3317768 | tf_op jit(solution)/shard_map/ppermute | solution.py:453
  90.5 60.8 %collective-permute-start.13 = (bf16[256,1152]{1,0:T(8,128)(2,1)}, bf16[256,1152]{1,0:T(8,128)(2,1)}, u32[]{:S(2)}, u32[]{:S(2)}) collective-permute-start(bf16[256,1152]{1,0:T(8,128)(2,1)} %fusion.28), channel_id=1, source_target_pairs={{0,3},{1,0},{2,1},{3,2},{4,7},{5,4},{6,5},{7,6},{8,11},{9,8},{10,9... | collective-permute-start | bytes 1769480 | tf_op jit(solution)/shard_map/ppermute | solution.py:498
  91.4 58.8 %collective-permute-start.12 = (bf16[256,1152]{1,0:T(8,128)(2,1)}, bf16[256,1152]{1,0:T(8,128)(2,1)}, u32[]{:S(2)}, u32[]{:S(2)}) collective-permute-start(bf16[256,1152]{1,0:T(8,128)(2,1)} %fusion.28), channel_id=1, source_target_pairs={{0,2},{1,3},{2,0},{3,1},{4,6},{5,7},{6,4},{7,5},{8,10},{9,11},{10,... | collective-permute-start | bytes 1769480 | tf_op jit(solution)/shard_map/ppermute | solution.py:498
  98.0 40.9 %collective-permute-start.11 = (bf16[256,1152]{1,0:T(8,128)(2,1)}, bf16[256,1152]{1,0:T(8,128)(2,1)}, u32[]{:S(2)}, u32[]{:S(2)}) collective-permute-start(bf16[256,1152]{1,0:T(8,128)(2,1)} %fusion.28), channel_id=1, source_target_pairs={{0,1},{1,2},{2,3},{3,0},{4,5},{5,6},{6,7},{7,4},{8,9},{9,10},{10,1... | collective-permute-start | bytes 1769480 | tf_op jit(solution)/shard_map/ppermute | solution.py:498
  114.3 59.2 %collective-permute-start.9 = (bf16[432,1152]{1,0:T(8,128)(2,1)S(1)}, bf16[432,1152]{1,0:T(8,128)(2,1)S(1)}, u32[]{:S(2)}, u32[]{:S(2)}) collective-permute-start(bf16[432,1152]{1,0:T(8,128)(2,1)S(1)} %pad_maximum_fusion), channel_id=1, source_target_pairs={{0,24},{4,28},{8,16},{12,20},{16,8},{20,12},{24,0},{28,4},{1,25},{... | collective-permute-start | bytes 2985992 | tf_op jit(solution)/shard_map/ppermute | solution.py:453
  117.0 54.5 %collective-permute-start.8 = (bf16[432,1152]{1,0:T(8,128)(2,1)S(1)}, bf16[432,1152]{1,0:T(8,128)(2,1)}, u32[]{:S(2)}, u32[]{:S(2)}) collective-permute-start(bf16[432,1152]{1,0:T(8,128)(2,1)S(1)} %pad_maximum_fusion), channel_id=1, source_target_pairs={{0,16},{4,20},{8,24},{12,28},{16,0},{20,4},{24,8},{28,12},{1,17},{... | collective-permute-start | bytes 2985992 | tf_op jit(solution)/shard_map/ppermute | solution.py:453
  117.8 37.1 %copy-start.6 = (bf16[4,2,160,1152]{3,2,1,0:T(8,128)(2,1)}, bf16[4,2,160,1152]{3,2,1,0:T(8,128)(2,1)S(1)}, u32[]{:S(2)}) copy-start(bf16[4,2,160,1152]{3,2,1,0:T(8,128)(2,1)S(1)} %constant_dynamic-update-slice_fusion.3) | copy-start | bytes 8847364
  138.9 30.7 %collective-permute-start.7 = (bf16[432,1152]{1,0:T(8,128)(2,1)S(1)}, bf16[432,1152]{1,0:T(8,128)(2,1)}, u32[]{:S(2)}, u32[]{:S(2)}) collective-permute-start(bf16[432,1152]{1,0:T(8,128)(2,1)S(1)} %pad_maximum_fusion), channel_id=1, source_target_pairs={{0,8},{4,12},{8,0},{12,4},{16,24},{20,28},{24,16},{28,20},{1,9},{5... | collective-permute-start | bytes 2985992 | tf_op jit(solution)/shard_map/ppermute | solution.py:453
  169.4 111.5 %reduce-scatter.5.cloned.1.call-start = ((), (), s32[]{:S(2)}) async-start(), calls=%async_computation.8 | async-start | bytes 2211840 | tf_op jit(solution)/shard_map/reduce_scatter | solution.py:645
  179.6 5.7 collective-permute-start.15
  179.6 8.3 %collective-permute-start.14 = (bf16[4,1,136,1152]{3,2,1,0:T(8,128)(2,1)}, bf16[4,1,136,1152]{3,2,1,0:T(8,128)(2,1)}, u32[]{:S(2)}, u32[]{:S(2)}) collective-permute-start(bf16[4,1,136,1152]{3,2,1,0:T(8,128)(2,1)} %constant_dynamic-slice_fusion.14), channel_id=1, source_target_pairs={{0,4},{4,0},{8,12},{12,8},{16,20},{20,16},{24,28},{28,24},{1,5},{5... | collective-permute-start | bytes 3760136 | tf_op jit(solution)/shard_map/ppermute | solution.py:453
  185.2 5.2 collective-permute-start.10
  190.8 17.4 %copy-start.51 = (f32[1152]{0:T(1024)S(1)}, f32[1152]{0:T(1024)}, u32[]{:S(2)}) copy-start(f32[1152]{0:T(1024)} %get-tuple-element.66) | copy-start | bytes 13828
  229.4 6.9 %copy-start.59 = (f32[768,1088]{0,1:T(8,128)S(1)}, f32[768,1088]{0,1:T(8,128)}, u32[]{:S(2)}) copy-start(f32[768,1088]{0,1:T(8,128)} %copy-done.58) | copy-start | bytes 10027012
  236.4 7.4 %collective-permute-start.16 = (bf16[2,2,1,136,1152]{4,3,2,1,0:T(8,128)(2,1)}, bf16[2,2,1,136,1152]{4,3,2,1,0:T(8,128)(2,1)}, u32[]{:S(2)}, u32[]{:S(2)}) collective-permute-start(bf16[2,2,1,136,1152]{4,3,2,1,0:T(8,128)(2,1)} %constant_dynamic-slice_fusion.12), channel_id=1, source_target_pairs={{0,4},{4,0},{8,12},{12,8},{16,20},{20,16},{24,28},{28,24},{1,5},{5... | collective-permute-start | bytes 3760136 | tf_op jit(solution)/shard_map/ppermute | solution.py:453
  241.9 5.5 collective-permute-start.19
  243.4 81.4 %all-gather.8.cloned.1.call-start = ((), (), s32[]{:S(2)}) async-start(), calls=%async_computation.9 | async-start | bytes 2211840 | tf_op jit(solution)/shard_map/all_gather | solution.py:671
  245.9 16.6 %collective-permute-start.17 = (bf16[1,2,1,136,1152]{4,3,2,1,0:T(8,128)(2,1)S(1)}, bf16[1,2,1,136,1152]{4,3,2,1,0:T(8,128)(2,1)S(1)}, u32[]{:S(2)}, u32[]{:S(2)}) collective-permute-start(bf16[1,2,1,136,1152]{4,3,2,1,0:T(8,128)(2,1)S(1)} %constant_dynamic-slice_fusion.11), channel_id=1, source_target_pairs={{0,16},{4,20},{8,24},{12,28},{16,0},{20,4},{24,8},{28,12},{1,17},{... | collective-permute-start | bytes 1880072 | tf_op jit(solution)/shard_map/ppermute | solution.py:453
  249.3 16.6 %collective-permute-start.20 = (bf16[2,1,1,136,1152]{4,3,2,1,0:T(8,128)(2,1)S(1)}, bf16[2,1,1,136,1152]{4,3,2,1,0:T(8,128)(2,1)S(1)}, u32[]{:S(2)}, u32[]{:S(2)}) collective-permute-start(bf16[2,1,1,136,1152]{4,3,2,1,0:T(8,128)(2,1)S(1)} %constant_dynamic-slice_fusion.8), channel_id=1, source_target_pairs={{0,8},{4,12},{8,0},{12,4},{16,24},{20,28},{24,16},{28,20},{1,9},{5... | collective-permute-start | bytes 1880072 | tf_op jit(solution)/shard_map/ppermute | solution.py:453
  262.7 9.6 %collective-permute-start.18 = (bf16[1,1,1,136,1152]{4,3,2,1,0:T(8,128)(2,1)S(1)}, bf16[1,1,1,136,1152]{4,3,2,1,0:T(8,128)(2,1)S(1)}, u32[]{:S(2)}, u32[]{:S(2)}) collective-permute-start(bf16[1,1,1,136,1152]{4,3,2,1,0:T(8,128)(2,1)S(1)} %constant_dynamic-slice_fusion.10), channel_id=1, source_target_pairs={{0,8},{4,12},{8,0},{12,4},{16,24},{20,28},{24,16},{28,20},{1,9},{5... | collective-permute-start | bytes 940040 | tf_op jit(solution)/shard_map/ppermute | solution.py:453
  266.1 8.5 %collective-permute-start.21 = (bf16[1,1,1,136,1152]{4,3,2,1,0:T(8,128)(2,1)S(1)}, bf16[1,1,1,136,1152]{4,3,2,1,0:T(8,128)(2,1)S(1)}, u32[]{:S(2)}, u32[]{:S(2)}) collective-permute-start(bf16[1,1,1,136,1152]{4,3,2,1,0:T(8,128)(2,1)S(1)} %constant_dynamic-slice_fusion.7), channel_id=1, source_target_pairs={{0,16},{4,20},{8,24},{12,28},{16,0},{20,4},{24,8},{28,12},{1,17},{... | collective-permute-start | bytes 940040 | tf_op jit(solution)/shard_map/ppermute | solution.py:453
  287.4 35.4 %all-to-all-start.1 = ((bf16[8,136,1152]{2,1,0:T(8,128)(2,1)}), bf16[8,136,1152]{2,1,0:T(8,128)(2,1)}, u32[]{:S(2)}, u32[]{:S(2)}) async-start(bf16[8,136,1152]{2,1,0:T(8,128)(2,1)} %select_add_fusion), calls=%async_computation.1 | async-start | bytes 5013504 | tf_op jit(solution)/shard_map/all_to_all | solution.py:577
  291.7 119.0 %reduce-scatter.7.cloned.1.call-start = ((), (), s32[]{:S(2)}) async-start(), calls=%async_computation.10 | async-start | bytes 2949120 | tf_op jit(solution)/shard_map/reduce_scatter | solution.py:686
  330.0 9.2 %copy-start.20 = (f32[768,1152]{1,0:T(8,128)S(1)}, f32[768,1152]{1,0:T(8,128)}, u32[]{:S(2)}) copy-start(f32[768,1152]{1,0:T(8,128)} %get-tuple-element.80) | copy-start | bytes 10616836
  330.0 9.2 %copy-start.42 = (f32[1152]{0:T(1024)S(1)}, f32[1152]{0:T(1024)}, u32[]{:S(2)}) copy-start(f32[1152]{0:T(1024)} %copy-done.41) | copy-start | bytes 13828
  330.0 9.2 %copy-start.46 = (f32[768]{0:T(1024)S(1)}, f32[768]{0:T(1024)}, u32[]{:S(2)}) copy-start(f32[768]{0:T(1024)} %copy-done.45) | copy-start | bytes 9220
  330.1 9.2 %copy-start.49 = (f32[1152]{0:T(1024)S(1)}, f32[1152]{0:T(1024)}, u32[]{:S(2)}) copy-start(f32[1152]{0:T(1024)} %get-tuple-element.69) | copy-start | bytes 13828
  330.1 9.2 %copy-start.56 = (f32[768]{0:T(1024)S(1)}, f32[768]{0:T(1024)}, u32[]{:S(2)}) copy-start(f32[768]{0:T(1024)} %add_rsqrt_fusion.1) | copy-start | bytes 9220
  345.6 9.7 %collective-permute-start.22 = (bf16[2,2,1,80,1152]{4,3,2,1,0:T(8,128)(2,1)}, bf16[2,2,1,80,1152]{4,3,2,1,0:T(8,128)(2,1)}, u32[]{:S(2)}, u32[]{:S(2)}) collective-permute-start(bf16[2,2,1,80,1152]{4,3,2,1,0:T(8,128)(2,1)} %constant_dynamic-slice_fusion.5), channel_id=1, source_target_pairs={{0,4},{4,0},{8,12},{12,8},{16,20},{20,16},{24,28},{28,24},{1,5},{5... | collective-permute-start | bytes 2211848 | tf_op jit(solution)/shard_map/ppermute | solution.py:453
  354.8 3.5 collective-permute-start.25
  356.7 10.6 %collective-permute-start.23 = (bf16[2,1,1,80,1152]{4,3,2,1,0:T(8,128)(2,1)S(1)}, bf16[2,1,1,80,1152]{4,3,2,1,0:T(8,128)(2,1)S(1)}, u32[]{:S(2)}, u32[]{:S(2)}) collective-permute-start(bf16[2,1,1,80,1152]{4,3,2,1,0:T(8,128)(2,1)S(1)} %constant_dynamic-slice_fusion.4), channel_id=1, source_target_pairs={{0,8},{4,12},{8,0},{12,4},{16,24},{20,28},{24,16},{28,20},{1,9},{5... | collective-permute-start | bytes 1105928 | tf_op jit(solution)/shard_map/ppermute | solution.py:453
  358.5 10.5 %collective-permute-start.26 = (bf16[1,2,1,80,1152]{4,3,2,1,0:T(8,128)(2,1)S(1)}, bf16[1,2,1,80,1152]{4,3,2,1,0:T(8,128)(2,1)S(1)}, u32[]{:S(2)}, u32[]{:S(2)}) collective-permute-start(bf16[1,2,1,80,1152]{4,3,2,1,0:T(8,128)(2,1)S(1)} %constant_dynamic-slice_fusion.1), channel_id=1, source_target_pairs={{0,16},{4,20},{8,24},{12,28},{16,0},{20,4},{24,8},{28,12},{1,17},{... | collective-permute-start | bytes 1105928 | tf_op jit(solution)/shard_map/ppermute | solution.py:453
  367.4 5.9 collective-permute-start.24
  369.1 5.6 collective-permute-start.27
  376.1 20.4 %all-to-all-start.2 = ((bf16[8,40,1152]{2,1,0:T(8,128)(2,1)}), bf16[8,40,1152]{2,1,0:T(8,128)(2,1)S(1)}, u32[]{:S(2)}, u32[]{:S(2)}) async-start(bf16[8,40,1152]{2,1,0:T(8,128)(2,1)} %select_add_fusion.1), calls=%async_computation.3 | async-start | bytes 1474560 | tf_op jit(solution)/shard_map/all_to_all | solution.py:577
  379.7 93.2 %reduce-scatter.9.cloned.1.call-start = ((), (), s32[]{:S(2)}) async-start(), calls=%async_computation.11 | async-start | bytes 3686400 | tf_op jit(solution)/shard_map/reduce_scatter | solution.py:718
  401.8 7.4 %copy-start = (bf16[1088,1152]{1,0:T(8,128)(2,1)}, bf16[1088,1152]{1,0:T(8,128)(2,1)S(1)}, u32[]{:S(2)}) copy-start(bf16[1088,1152]{1,0:T(8,128)(2,1)S(1)} %get-tuple-element.20.top_ref.top_hbm) | copy-start | bytes 7520260
  416.2 59.0 %copy-start.5 = (bf16[3,4,80,768]{3,2,1,0:T(8,128)(2,1)S(1)}, bf16[3,4,80,768]{3,2,1,0:T(8,128)(2,1)}, u32[]{:S(2)}) copy-start(bf16[3,4,80,768]{3,2,1,0:T(8,128)(2,1)} %copy-done.4) | copy-start | bytes 4423684
  416.2 120.9 %all-gather.10.cloned.1.call-start = ((), (), s32[]{:S(2)}) async-start(), calls=%async_computation.12 | async-start | bytes 3686400 | tf_op jit(solution)/shard_map/all_gather | solution.py:719
  417.4 58.8 %copy-start.48 = (f32[256]{0:T(256)}, f32[256]{0:T(256)S(1)}, u32[]{:S(2)}) copy-start(f32[256]{0:T(256)S(1)} %broadcast_multiply_fusion.4) | copy-start | bytes 3076
  417.4 58.8 %copy-start.33 = (bf16[256,1152]{1,0:T(8,128)(2,1)S(1)}, bf16[256,1152]{1,0:T(8,128)(2,1)}, u32[]{:S(2)}) copy-start(bf16[256,1152]{1,0:T(8,128)(2,1)} %reduce-scatter.7.cloned.1.call-done) | copy-start | bytes 1769476
  472.9 166.7 %reduce-scatter.11.cloned.1.call-start = ((), (), s32[]{:S(2)}) async-start(), calls=%async_computation.13 | async-start | bytes 2949120 | tf_op jit(solution)/shard_map/reduce_scatter | solution.py:735
  476.9 4.5 collective-permute-start.28
  481.5 4.4 collective-permute-start.29
  485.9 4.2 collective-permute-start.30
  490.1 8.3 %collective-permute-start.31 = (f32[112,128]{1,0:T(8,128)S(1)}, f32[112,128]{1,0:T(8,128)S(1)}, u32[]{:S(2)}, u32[]{:S(2)}) collective-permute-start(f32[112,128]{1,0:T(8,128)S(1)} %add.625), channel_id=1, source_target_pairs={{0,1},{1,0},{2,3},{3,2},{4,5},{5,4},{6,7},{7,6},{8,9},{9,8},{10,11... | collective-permute-start | bytes 172040 | tf_op jit(solution)/shard_map/ppermute | solution.py:453
  498.5 9.7 %collective-permute-start.32 = (f32[112,128]{1,0:T(8,128)S(1)}, f32[112,128]{1,0:T(8,128)S(1)}, u32[]{:S(2)}, u32[]{:S(2)}) collective-permute-start(f32[112,128]{1,0:T(8,128)S(1)} %add.626), channel_id=1, source_target_pairs={{0,2},{1,3},{2,0},{3,1},{4,6},{5,7},{6,4},{7,5},{8,10},{9,11},{10,... | collective-permute-start | bytes 172040 | tf_op jit(solution)/shard_map/ppermute | solution.py:453
  498.9 9.3 %copy-start.39 = (f32[3380]{0:T(1024)S(1)}, f32[3380]{0:T(1024)}, u32[]{:S(2)}) copy-start(f32[3380]{0:T(1024)} %get-tuple-element.31) | copy-start | bytes 40564
  498.9 9.3 %copy-start.40 = (f32[3380]{0:T(1024)S(1)}, f32[3380]{0:T(1024)}, u32[]{:S(2)}) copy-start(f32[3380]{0:T(1024)} %get-tuple-element.32) | copy-start | bytes 40564
  498.9 40.1 %copy-start.11 = (f32[768,1152]{1,0:T(8,128)S(1)}, f32[768,1152]{1,0:T(8,128)}, u32[]{:S(2)}) copy-start(f32[768,1152]{1,0:T(8,128)} %copy-done.10) | copy-start | bytes 10616836
  (40 other events, 116.3 us)
Sparse Core Ops, SparseCore 0:
  24.7 62.9 all-gather.11
  169.5 38.7 all-gather.5
  243.5 37.3 reduce-scatter.4
  285.3 39.3 all-gather.7
  353.3 47.0 reduce-scatter.6
  416.3 56.5 reduce-scatter.8
  474.5 62.5 all-gather.9
  548.8 46.6 reduce-scatter.10

commit v2 on v1

v2 whole, which is shorter than its diff:
```python
import functools
import math

import jax
import jax.numpy as jnp
from jax import lax
from jax.experimental import pallas as pl
from jax.experimental.pallas import tpu as pltpu
from jax.sharding import PartitionSpec as P

HEADS = 16
FF = 4304
LEN = 729
NS_ITERS = 5
STEP = 10

norm_eps = 1e-06
coef_a = 3.4445
coef_b = -4.775
coef_c = 2.0315
momentum_decay = 0.95
matrix_rate = 0.15
matrix_decay = 0.1
beta_first = 0.9
beta_second = 0.999
vector_rate = 0.5
adam_eps = 1e-08
low = jnp.bfloat16
f32 = jnp.float32


def call(body, name, **kw):
    vmem = kw.pop("vmem", 48)
    return pl.pallas_call(
        body,
        name=name,
        compiler_params=pltpu.CompilerParams(vmem_limit_bytes=vmem * 1024 * 1024),
        **kw,
    )


def dot(left, right, contract):
    return lax.dot_general(
        left, right, ((tuple(contract[:1]), tuple(contract[1:])), ((), ())), preferred_element_type=f32
    )


def split(x):
    top = x.astype(low)
    return top, (x - top.astype(f32)).astype(low)


def prep_square_body(slab_ref, first_ref, out_ref):
    rows = slab_ref[:, 0, :]
    extra = out_ref.shape[0] - rows.shape[0]
    padded = jnp.concatenate([rows, jnp.zeros((extra, rows.shape[1]), f32)], axis=0)
    out_ref[...] = padded.astype(low)


def prep_square(slab, first, heads, head_size, head_pad):
    width = slab.shape[2]
    return call(
        prep_square_body,
        "prep_square",
        grid=(heads,),
        in_specs=[
            pl.BlockSpec((head_size, 1, width), lambda i: (i, 0, 0)),
            pl.BlockSpec(memory_space=pl.ANY),
        ],
        out_specs=pl.BlockSpec((head_pad, width), lambda i: (i, 0)),
        out_shape=jax.ShapeDtypeStruct((heads * head_pad, width), low),
    )(slab, first)


def prep_wide_body(total, slab_ref, out_ref):
    rows = slab_ref[:, 0, :]
    at = pl.program_id(0) * rows.shape[0] + lax.broadcasted_iota(jnp.int32, rows.shape, 0)
    out_ref[...] = jnp.where(at < total, rows, 0.0).astype(low)


def prep_wide(slab, rows_pad):
    total, _, width = slab.shape
    block = rows_pad // 4
    return call(
        functools.partial(prep_wide_body, total),
        "prep_wide",
        grid=(4,),
        in_specs=[pl.BlockSpec((block, 1, width), lambda i: (i, 0, 0))],
        out_specs=pl.BlockSpec((block, width), lambda i: (i, 0)),
        out_shape=jax.ShapeDtypeStruct((rows_pad, width), low),
    )(slab)


def momentum_body(total, moment_ref, grad_ref, first_ref, top_ref, rest_ref):
    grad = grad_ref[...].astype(f32)
    first = momentum_decay * moment_ref[:, 0, :] + grad
    first_ref[...] = first.reshape(first_ref.shape)
    at = pl.program_id(0) * grad.shape[0] + lax.broadcasted_iota(jnp.int32, grad.shape, 0)
    top, rest = split(jnp.where(at < total, grad + momentum_decay * first, 0.0))
    top_ref[...] = top
    rest_ref[...] = rest


def momentum(moments, grad):
    total, _, width = moments.shape
    rows_pad = grad.shape[0]
    block = rows_pad // 4
    slab_spec = pl.BlockSpec((block, 1, width), lambda i: (i, 0, 0))
    flat_spec = pl.BlockSpec((block, width), lambda i: (i, 0))
    return call(
        functools.partial(momentum_body, total),
        "momentum",
        grid=(4,),
        in_specs=[slab_spec, flat_spec],
        out_specs=[slab_spec, flat_spec, flat_spec],
        out_shape=[
            jax.ShapeDtypeStruct(moments.shape, f32),
            jax.ShapeDtypeStruct((rows_pad, width), low),
            jax.ShapeDtypeStruct((rows_pad, width), low),
        ],
    )(moments, grad)


def momentum_again_body(total, moment_ref, grad_ref, *refs):
    momentum_body(total, moment_ref, grad_ref, *refs[-3:])


def momentum_again(moments, grad, first, top, rest, *others):
    total, _, width = moments.shape
    rows = grad.shape[0]
    slab_spec = pl.BlockSpec((rows, 1, width), lambda i: (i, 0, 0))
    flat_spec = pl.BlockSpec((rows, width), lambda i: (i, 0))
    return call(
        functools.partial(momentum_again_body, total),
        "momentum_again",
        grid=(1,),
        in_specs=[slab_spec, flat_spec] + [pl.BlockSpec(memory_space=pl.ANY)] * (3 + len(others)),
        out_specs=[slab_spec, flat_spec, flat_spec],
        out_shape=[jax.ShapeDtypeStruct(x.shape, x.dtype) for x in (first, top, rest)],
        input_output_aliases={2: 0, 3: 1, 4: 2},
    )(moments, grad, first, top, rest, *others)


def packed_at(column):
    return 128 * (column * (column + 1) // 2)


def upper(width):
    for j in range(0, width, 256):
        for i in range(0, min(j + 256, width), 256):
            yield i, j, pl.ds(i, min(256, width - i)), pl.ds(j, min(256, width - j))


def gram_body(top_ref, rest_ref, out_ref):
    for i, j, rows, columns in upper(top_ref.shape[1]):
        value = (
            dot(top_ref[:, rows], top_ref[:, columns], (0, 0))
            + dot(top_ref[:, rows], rest_ref[:, columns], (0, 0))
            + dot(rest_ref[:, rows], top_ref[:, columns], (0, 0))
        )
        for c in range(j // 128, (j + value.shape[1]) // 128):
            used = min(value.shape[0], 128 * (c + 1) - i)
            lanes = 128 * c - j
            out_ref[pl.ds(packed_at(c) + i, used), :] = value[:used, lanes : lanes + 128]


def gram_of(top, rest):
    count = top.shape[1] // 128
    return call(
        gram_body,
        "gram",
        in_specs=[pl.BlockSpec(memory_space=pltpu.VMEM)] * 2,
        out_specs=pl.BlockSpec(memory_space=pltpu.VMEM),
        out_shape=jax.ShapeDtypeStruct((packed_at(count), 128), f32),
    )(top, rest)


class Iterate:
    def __init__(self, a_top, a_rest, b_top, t_top, t_rest, x_ref):
        self.a = a_top, a_rest
        self.b = b_top
        self.t = t_top, t_rest
        self.x = x_ref
        self.width = a_top.shape[0]
        self.step = x_ref.shape[0] // 4
        self.diagonal = lax.broadcasted_iota(jnp.int32, (128, 128), 0) == lax.broadcasted_iota(
            jnp.int32, (128, 128), 1
        )

    def put(self, i, j, value):
        tall, wide = value.shape
        for x, rows, columns in ((value, pl.ds(i, tall), pl.ds(j, wide)),) + (
            ((value.T, pl.ds(j, wide), pl.ds(i, tall)),) if i != j else ()
        ):
            top, rest = split(x)
            self.a[0][rows, columns] = top
            self.a[1][rows, columns] = rest

    def both(self, pair, rows, columns):
        return pair[0][rows, columns].astype(f32) + pair[1][rows, columns].astype(f32)

    def symmetric(self, left, rights, finish):
        for i, j, rows, columns in upper(self.width):
            value = dot(left[rows, :], rights[0][:, columns], (1, 0))
            for right in rights[1:]:
                value = value + dot(left[rows, :], right[:, columns], (1, 0))
            finish(i, j, rows, columns, value)

    def recenter(self, center):
        total = jnp.zeros((128, 128), f32)
        for c in range(0, self.width, 128):
            at = pl.ds(c, 128)
            total = total + jnp.where(self.diagonal, self.both(self.a, at, at), 0.0)
        mean = jnp.sum(total) / self.width
        for c in range(0, self.width, 128):
            at = pl.ds(c, 128)
            top, rest = split(self.both(self.a, at, at) - jnp.where(self.diagonal, mean, 0.0))
            self.a[0][at, at] = top
            self.a[1][at, at] = rest
        return center + mean

    def mix(self, center):
        def finish(i, j, rows, columns, value):
            value = (coef_b + 2.0 * coef_c * center) * self.both(
                self.a, rows, columns
            ) + coef_c * value
            self.b[rows, columns] = value.astype(low)
            if i != j:
                self.b[columns, rows] = value.T.astype(low)

        self.symmetric(self.a[0], (self.a[0],), finish)
        return coef_a + coef_b * center + coef_c * center * center

    def stepped(self, rows, lead):
        x = self.x[rows, :]
        return lead * x + dot(x.astype(low), self.b[...], (1, 0))

    def propagate(self, center, lead, passes):
        tall = self.width // 3

        @pl.loop(0, 3)
        def _(r):
            rows = pl.ds(r * tall, tall)
            value = lead * self.both(self.a, rows, slice(None)) + center * self.b[rows, :].astype(f32)
            for left in self.a[:passes]:
                value = value + dot(left[rows, :], self.b[...], (1, 0))
            top, rest = split(value)
            self.t[0][rows, :] = top
            self.t[1][rows, :] = rest

        def finish(i, j, rows, columns, value):
            carried = lead * self.both(self.t, rows, columns)
            carried = carried + lead * center * self.b[rows, columns].astype(f32)
            self.put(i, j, carried + value)

        self.symmetric(self.b, self.t[:passes], finish)
        return lead * lead * center

    def sweep(self, center, passes=2):
        center = self.recenter(center)
        lead = self.mix(center)

        @pl.loop(0, 4)
        def _(r):
            rows = pl.ds(r * self.step, self.step)
            self.x[rows, :] = self.stepped(rows, lead)

        return self.propagate(center, lead, passes)


def iterate_body(
    total,
    square_ref,
    rate_ref,
    gram_ref,
    full_hbm,
    top_hbm,
    rest_hbm,
    slab_hbm,
    first_ref,
    out_hbm,
    a_top,
    a_rest,
    b_top,
    t_top,
    t_rest,
    x_ref,
    slab_ref,
    sem,
):
    state = Iterate(a_top, a_rest, b_top, t_top, t_rest, x_ref)
    width, step = state.width, state.step
    rows_pad = x_ref.shape[0]
    fetch_full = pltpu.make_async_copy(full_hbm, t_rest, sem.at[0])
    fetch_top = pltpu.make_async_copy(top_hbm, b_top.at[pl.ds(0, rows_pad)], sem.at[1])
    fetch_rest = pltpu.make_async_copy(rest_hbm, t_top.at[pl.ds(0, rows_pad)], sem.at[2])
    fetch_slab = pltpu.make_async_copy(slab_hbm, slab_ref.at[pl.ds(0, total)], sem.at[3])
    for fetch in (fetch_full, fetch_top, fetch_rest, fetch_slab):
        fetch.start()
    is_square = square_ref[0] == 1
    trace = jnp.zeros((128, 128), f32)
    for c in range(width // 128):
        block = gram_ref[pl.ds(packed_at(c) + 128 * c, 128), :]
        trace = trace + jnp.where(state.diagonal, block, 0.0)
    fetch_full.wait()

    def add_squares(r, sums):
        part = t_rest[pl.ds(r * 128, 128), :].astype(f32)
        return sums + jnp.sum(part * part, axis=0, keepdims=True)

    squares = lax.fori_loop(0, width // 128, add_squares, jnp.zeros((1, width), f32))
    norm = jnp.sqrt(jnp.where(is_square, jnp.sum(squares), jnp.sum(trace)))
    scaling = 1.0 / (norm + 1e-07)
    scale_two = scaling * scaling

    @pl.when(is_square)
    def _():
        for i, j, rows, columns in upper(width):
            state.put(i, j, dot(t_rest[:, rows], t_rest[:, columns], (0, 0)) * scale_two)

    @pl.when(jnp.logical_not(is_square))
    def _():
        for c in range(width // 128):
            for r in range(c + 1):
                block = gram_ref[pl.ds(packed_at(c) + 128 * r, 128), :]
                state.put(128 * r, 128 * c, block * scale_two)

    fetch_top.wait()
    fetch_rest.wait()
    rest_scaling = jnp.where(is_square, 0.0, scaling)

    @pl.loop(0, 4)
    def _(r):
        rows = pl.ds(r * step, step)
        x_ref[rows, :] = b_top[rows, :].astype(f32) * scaling + t_top[rows, :].astype(f32) * rest_scaling

    center = lax.fori_loop(
        0, NS_ITERS - 2, lambda _, center: state.sweep(center), jnp.float32(0.0)
    )
    center = state.sweep(center, 1)
    lead = state.mix(state.recenter(center))
    fetch_slab.wait()
    rate = rate_ref[0]

    @pl.loop(0, 4)
    def _(r):
        rows = pl.ds(r * step, step)
        new = slab_ref[rows, 0, :] * (1.0 - matrix_rate * matrix_decay) - rate * state.stepped(rows, lead)
        slab_ref[rows, :, :] = new.reshape(step, 1, width)

    leave = pltpu.make_async_copy(slab_ref.at[pl.ds(0, total)], out_hbm, sem.at[0])
    leave.start()
    leave.wait()


def iterate(square, rate, gram, full, top, rest, slab, first):
    total, _, width = slab.shape
    rows_pad = top.shape[0]
    vmem, smem = pl.BlockSpec(memory_space=pltpu.VMEM), pl.BlockSpec(memory_space=pltpu.SMEM)
    far = pl.BlockSpec(memory_space=pl.ANY)
    return call(
        functools.partial(iterate_body, total),
        "iterate",
        vmem=56,
        in_specs=[smem, smem, vmem] + [far] * 5,
        out_specs=far,
        out_shape=jax.ShapeDtypeStruct(slab.shape, f32),
        scratch_shapes=[pltpu.VMEM((width, width), low)] * 5
        + [
            pltpu.VMEM((rows_pad, width), f32),
            pltpu.VMEM((rows_pad, 1, width), f32),
            pltpu.SemaphoreType.DMA((4,)),
        ],
        cost_estimate=pl.CostEstimate(
            flops=80_000_000_000, bytes_accessed=20_000_000, transcendentals=0
        ),
    )(square, rate, gram, full, top, rest, slab, first)


def attend_body(scale, qkv_ref, context_ref, soft_ref):
    query, key, value = qkv_ref[0, 0], qkv_ref[1, 0], qkv_ref[2, 0]
    scores = dot(key, query, (0, 0)) * scale
    at = lax.broadcasted_iota(jnp.int32, scores.shape, 0)
    scores = jnp.where(at < LEN, scores, -1e30)
    exponent = jnp.exp(scores - jnp.max(scores, axis=0, keepdims=True))
    soft = (exponent / jnp.sum(exponent, axis=0, keepdims=True)).astype(low)
    soft_ref[0] = soft
    context = dot(value, soft, (1, 0))
    context_ref[0] = context[: context_ref.shape[1]].astype(low)


def attend(qkv, head_size, scale):
    _, groups, head_pad, rows = qkv.shape
    return call(
        functools.partial(attend_body, scale),
        "attend",
        grid=(groups,),
        in_specs=[pl.BlockSpec((3, 1, head_pad, rows), lambda h: (0, h, 0, 0))],
        out_specs=[
            pl.BlockSpec((1, head_size, rows), lambda h: (h, 0, 0)),
            pl.BlockSpec((1, rows, rows), lambda h: (h, 0, 0)),
        ],
        out_shape=[
            jax.ShapeDtypeStruct((groups, head_size, rows), low),
            jax.ShapeDtypeStruct((groups, rows, rows), low),
        ],
    )(qkv)


def attend_back_body(scale, qkv_ref, soft_ref, grad_ref, first_ref, other_ref, out_ref):
    query, key, value = qkv_ref[0, 0], qkv_ref[1, 0], qkv_ref[2, 0]
    grad, soft = grad_ref[0], soft_ref[0]
    grad_soft = dot(value, grad, (0, 0))
    soft_f32 = soft.astype(f32)
    along = jnp.sum(soft_f32 * grad_soft, axis=0, keepdims=True)
    grad_scores = (soft_f32 * (grad_soft - along)).astype(low)
    out_ref[0, 0] = (dot(key, grad_scores, (1, 0)) * scale).astype(low)
    out_ref[1, 0] = (dot(query, grad_scores, (1, 1)) * scale).astype(low)
    out_ref[2, 0] = dot(grad, soft, (1, 1)).astype(low)


def attend_back(qkv, soft, grad, first, other, scale):
    _, groups, head_pad, rows = qkv.shape
    three = pl.BlockSpec((3, 1, head_pad, rows), lambda h: (0, h, 0, 0))
    return call(
        functools.partial(attend_back_body, scale),
        "attend_back",
        grid=(groups,),
        in_specs=[
            three,
            pl.BlockSpec((1, rows, rows), lambda h: (h, 0, 0)),
            pl.BlockSpec((1, head_pad, rows), lambda h: (h, 0, 0)),
            pl.BlockSpec(memory_space=pl.ANY),
            pl.BlockSpec(memory_space=pl.ANY),
        ],
        out_specs=three,
        out_shape=jax.ShapeDtypeStruct(qkv.shape, low),
    )(qkv, soft, grad, first, other)


def whiten(inputs):
    average = jnp.mean(inputs, axis=-1, keepdims=True)
    centered = inputs - average
    variance = jnp.mean(centered * centered, axis=-1, keepdims=True)
    inverse = lax.rsqrt(variance + norm_eps)
    return centered * inverse, inverse


def whiten_back(grad, gain_row, hat, inverse):
    scaled = grad * gain_row
    mean_one = jnp.mean(scaled, axis=-1, keepdims=True)
    mean_two = jnp.mean(scaled * hat, axis=-1, keepdims=True)
    return inverse * (scaled - mean_one - hat * mean_two)


def gelu_both(inputs):
    squared = inputs * inputs
    curve = jnp.tanh(0.7978845608028654 * (inputs + 0.044715 * inputs * squared))
    value = 0.5 * inputs * (1.0 + curve)
    slope = 0.5 * (1.0 + curve) + 0.5 * inputs * (1.0 - curve * curve) * 0.7978845608028654 * (
        1.0 + 3.0 * 0.044715 * squared
    )
    return value, slope


def product(form, left, right):
    return jnp.einsum(form, left, right, preferred_element_type=f32)


def flip(x, axis, mask):
    count = lax.axis_size(axis)
    return lax.ppermute(x, axis, [(i, i ^ mask) for i in range(count)])


def gather_chunks(piece, first):
    count = lax.axis_size("dp")
    half = count // 2
    me = lax.axis_index("dp")
    pair, core = me >> 1, me & 1
    whole = jnp.zeros((half, 2) + piece.shape, piece.dtype)
    for mask, part in enumerate(exchange(piece, first)):
        whole = lax.dynamic_update_slice(whole, part[None, None], (pair ^ mask, core, 0, 0))
    mine = lax.dynamic_slice_in_dim(whole, core, 1, 1)
    other = flip(mine, "dp", 1)
    whole = lax.dynamic_update_slice_in_dim(whole, other, 1 - core, 1)
    return whole.reshape((count,) + piece.shape)


def scatter_sum(whole, order):
    count, rows, columns = whole.shape
    bits = count.bit_length() - 1
    me = lax.axis_index("dp")
    whole = whole.reshape((2,) * bits + (rows, columns))
    for bit in order:
        at = bits - 1 - bit
        mine = (me >> bit) & 1
        kept = lax.dynamic_slice_in_dim(whole, mine, 1, at)
        sent = lax.dynamic_slice_in_dim(whole, 1 - mine, 1, at)
        got = flip(sent, "dp", 1 << bit)
        whole = (kept.astype(f32) + got.astype(f32)).astype(low)
    return whole.reshape(rows, columns)


def arrivals(piece):
    count = lax.axis_size("seq")
    return [
        lax.ppermute(piece, "seq", [(i, (i + shift) % count) for i in range(count)])
        for shift in range(1, count)
    ]


def gather_seq(piece):
    count = lax.axis_size("seq")
    me = lax.axis_index("seq")
    whole = jnp.zeros((count,) + piece.shape, piece.dtype)
    for shift, part in enumerate([piece] + arrivals(piece)):
        whole = lax.dynamic_update_slice_in_dim(whole, part[None], (me - shift) % count, 0)
    return whole


def total_sum(x):
    for axis in ("dp", "seq"):
        step = 1
        while step < lax.axis_size(axis):
            x = x + flip(x, axis, step)
            step *= 2
    return x


def zero_of(token):
    return jnp.minimum(jnp.abs(token), 0.0)


def after(x, token):
    return x + zero_of(token).astype(x.dtype)


def touch_body(*refs):
    pass


def touch(arrays, *others):
    far = pl.BlockSpec(memory_space=pl.ANY)
    count = len(arrays)
    return call(
        touch_body,
        "touch",
        in_specs=[far] * (count + len(others)),
        out_specs=[far] * count,
        out_shape=[jax.ShapeDtypeStruct(x.shape, x.dtype) for x in arrays],
        input_output_aliases={i: i for i in range(count)},
    )(*arrays, *others)


def relative(me, count):
    place = jnp.arange(count)
    half = count // 2
    return me ^ ((place % half) * 2 + place // half)


def exchange(piece, first):
    half = lax.axis_size("dp") // 2
    arrived = [flip(piece, "dp", mask << 1) for mask in range(1, half)]
    return [piece] + [after(x, first) for x in arrived]


def gather_relative(pieces, first):
    arrived = exchange(jnp.concatenate(pieces, axis=0), first)
    result, at = [], 0
    for piece in pieces:
        rows = piece.shape[0]
        mine = jnp.concatenate([x[at : at + rows] for x in arrived], axis=0)
        result.append(jnp.concatenate([mine, flip(mine, "dp", 1)], axis=0))
        at += rows
    return result


def scatter_relative(whole, order):
    count = lax.axis_size("dp")
    bits = count.bit_length() - 1
    rows, columns = whole.shape[0] // count, whole.shape[1]
    whole = whole.reshape((2,) * bits + (rows, columns))
    for bit in order:
        at = 0 if bit == 0 else bits - bit
        kept = lax.slice_in_dim(whole, 0, 1, axis=at)
        got = flip(lax.slice_in_dim(whole, 1, 2, axis=at), "dp", 1 << bit)
        whole = (kept.astype(f32) + got.astype(f32)).astype(low)
    return whole.reshape(rows, columns)


def local(
    tokens, cotangent, counts, owner_table, owned_weights, owned_moments, vectors, vector_moments
):
    seq_count = lax.axis_size("seq")
    dp_count = lax.axis_size("dp")
    bits = dp_count.bit_length() - 1
    seq_index = lax.axis_index("seq")
    dp_index = lax.axis_index("dp")
    capacity = tokens.shape[1]
    width = tokens.shape[2]
    slots = capacity * seq_count
    head_size = width // HEADS
    head_pad = -(-head_size // 16) * 16
    heads = HEADS // seq_count
    score_scale = 1.0 / math.sqrt(head_size)
    widths = (width, width, width, width, FF, FF)
    cols = width // seq_count
    ff_cols = FF // seq_count
    share = -(-LEN // (16 * seq_count)) * 16
    packed = share * seq_count
    square_rows = heads * head_pad
    square_chunk = -(-square_rows // (8 * dp_count)) * 8
    square_total = square_chunk * dp_count
    wide_chunk = -(-ff_cols // (8 * dp_count)) * 8
    wide_rows = wide_chunk * dp_count
    orders = (tuple(range(bits)), (0,) + tuple(range(bits - 1, 0, -1)))

    rows_in = tokens[0]
    vector_count = vectors.shape[0]
    vector_rows = -(-vector_count // width)
    extra = -(-vector_rows // 16) * 16
    payload = jnp.pad(vectors, (0, extra * width - vector_count)).reshape(extra, width)
    own_ids = jnp.arange(capacity)[:, None]
    own_valid = (own_ids < lax.dynamic_index_in_dim(counts[0], seq_index, 0)).astype(f32)
    cot_own = (cotangent[0] * own_valid).astype(low)
    payload = jnp.concatenate([rows_in.astype(low), payload.astype(low), cot_own], axis=0)
    gathered = lax.all_gather(payload, "seq", axis=0, tiled=False)
    token_slots = gathered[:, : capacity + extra].reshape(seq_count * (capacity + extra), width)
    cot_slots = gathered[:, capacity + extra :].reshape(slots, width)

    counts_row = counts[0]
    starts = jnp.cumsum(counts_row) - counts_row

    def rows_of(per):
        ids = jnp.arange(per * seq_count)
        real = (ids % per) < jnp.repeat(counts_row, per)
        return jnp.where(real, jnp.repeat(starts, per) + ids % per, packed)

    def picks(row):
        return (jnp.arange(packed)[:, None] == row[None, :]).astype(low)

    slot_row = rows_of(capacity)
    token_pick = picks(rows_of(capacity + extra))
    own_row = lax.dynamic_slice_in_dim(slot_row, seq_index * capacity, capacity)
    own_pick = picks(own_row)
    grad_rows = product("rc,cd->rd", picks(slot_row), cot_slots).astype(low)

    slab = jnp.transpose(owned_weights[0], (2, 1, 0))
    moments = jnp.transpose(owned_moments[0], (2, 1, 0))

    def send(x):
        return lax.all_to_all(x, "dp", split_axis=0, concat_axis=0, tiled=True)

    square_own = prep_square(slab, payload, heads, head_size, head_pad)
    near = jnp.stack(exchange(square_own, gathered[0, 0, 0]))
    far = flip(near, "dp", 1)
    squares = []
    for m in range(4):
        away = owner_table[m] ^ dp_index
        from_near = lax.dynamic_index_in_dim(near, away >> 1, 0, keepdims=False)
        from_far = lax.dynamic_index_in_dim(far, away >> 1, 0, keepdims=False)
        squares.append(jnp.where((away & 1) == 0, from_near, from_far))
    w_qkv = jnp.concatenate(squares[:3], axis=0)
    w_out_piece = jnp.pad(squares[3], ((0, square_total - square_rows), (0, 0)))
    w_out_piece = lax.dynamic_slice_in_dim(w_out_piece, dp_index * square_chunk, square_chunk)
    w_out_part = gather_seq(w_out_piece).reshape(seq_count * square_chunk, width)
    wide_sent = prep_wide(slab, wide_rows).reshape(dp_count, wide_chunk, width)
    got_wide = send(wide_sent)
    wide_pieces = [lax.dynamic_index_in_dim(got_wide, owner_table[m], 0, keepdims=False) for m in (4, 5)]

    w_up, w_down = gather_relative(wide_pieces, gathered[0, 0, 0])

    vector_full = gathered[:, capacity : capacity + vector_rows].reshape(seq_count, -1)
    vector_full = vector_full[:, :vector_count].reshape(-1).astype(f32)
    row_params = vector_full[: 8 * width].reshape(8, width)
    up_bias = lax.dynamic_slice_in_dim(vector_full, 8 * width + seq_index * ff_cols, ff_cols)
    up_bias = jnp.pad(up_bias, (0, wide_rows - ff_cols)).reshape(dp_count, wide_chunk)
    up_bias = jnp.take(up_bias, relative(dp_index, dp_count), axis=0).reshape(wide_rows)

    def head_bias(row):
        own = lax.dynamic_slice_in_dim(row, seq_index * cols, cols).reshape(heads, head_size)
        return jnp.pad(own, ((0, 0), (0, head_pad - head_size))).reshape(square_rows)

    qkv_bias = jnp.concatenate(
        [head_bias(row_params[2]), jnp.zeros((square_rows,), f32), head_bias(row_params[3])]
    )

    token_rows = product("rc,cd->rd", token_pick, token_slots)
    hat_packed = whiten(token_rows)[0]
    normed = (hat_packed * row_params[0] + row_params[1]).astype(low)
    qkv_bias = after(qkv_bias, w_up[0, 0] + w_down[0, 0] + grad_rows[0, 0] + w_out_part[0, 0])
    qkv = (product("ed,rd->er", w_qkv, normed) + qkv_bias[:, None]).astype(low)
    qkv = qkv.reshape(3, heads, head_pad, packed)
    context_own, soft = attend(qkv, head_size, score_scale)
    token = context_own[0, 0, 0]
    w_out = gather_chunks(w_out_part, token)
    w_out = w_out.reshape(dp_count, seq_count, square_chunk, width).transpose(1, 0, 2, 3)
    w_out = w_out.reshape(seq_count, square_total, width)[:, :square_rows]
    w_out = w_out.reshape(seq_count * heads, head_pad, width)[:, :head_size].reshape(width, width)
    w_out_own = lax.dynamic_slice_in_dim(w_out, seq_index * cols, cols, axis=1)
    w_out_own = jnp.pad(
        w_out_own.reshape(width, heads, head_size), ((0, 0), (0, 0), (0, head_pad - head_size))
    ).reshape(width, square_rows)
    context = lax.all_gather(context_own.reshape(cols, packed), "seq", axis=0, tiled=True)
    middle = token_rows + product("er,oe->ro", context, w_out) + row_params[4]
    hat_two, inverse_two = whiten(middle)
    normed_two = (hat_two * row_params[5] + row_params[6]).astype(low)
    pre_act = product("rd,fd->rf", normed_two, w_up) + up_bias
    hidden_f32, slope = gelu_both(pre_act)
    hidden = hidden_f32.astype(low)

    grad_hidden = product("rd,fd->rf", grad_rows, w_down)
    grad_pre = (slope * grad_hidden).astype(low)
    grad_down = product("rf,rd->fd", hidden, grad_rows).astype(low)
    grad_up = product("rf,rd->fd", grad_pre, normed_two).astype(low)
    grad_normed_two_part = (
        product("rf,fd->rd", grad_pre, w_up) + zero_of(grad_down[0, 0] + grad_up[0, 0]).astype(f32)
    ).astype(low)
    grad_up_bias = jnp.sum(grad_pre.astype(f32), axis=0).reshape(dp_count, wide_chunk)
    back = jnp.arange(dp_count) ^ dp_index
    grad_up_bias = jnp.take(grad_up_bias, (back & 1) * (dp_count // 2) + (back >> 1), axis=0)
    grad_up_bias = grad_up_bias.reshape(wide_rows)[:ff_cols]

    sum_down = scatter_relative(grad_down, orders[0])
    sum_up = scatter_relative(grad_up, orders[1])
    def to_owner(pairs):
        total = 0
        for piece, m in pairs:
            here = (jnp.arange(dp_count) == owner_table[m])[:, None, None]
            total = total + jnp.where(here, piece[None], jnp.zeros((), low))
        return total

    wide_back = to_owner([(sum_up, 4), (sum_down, 5)])
    grad_normed_two = after(
        lax.psum_scatter(grad_normed_two_part, "seq", scatter_dimension=0, tiled=True),
        wide_back[0, 0, 0],
    ).astype(f32)
    back_wide = send(wide_back).reshape(wide_rows, width)
    def own_share(x):
        return lax.dynamic_slice_in_dim(x, seq_index * share, share)

    own_grad = own_share(grad_rows).astype(f32)
    own_hat = own_share(hat_two)
    grad_bias_down = jnp.sum(own_grad, axis=0)
    grad_gain_two = jnp.sum(grad_normed_two * own_hat, axis=0)
    grad_shift_two = jnp.sum(grad_normed_two, axis=0)
    grad_mid_norm = whiten_back(grad_normed_two, row_params[5], own_hat, own_share(inverse_two))
    grad_attn_own = (own_grad + grad_mid_norm).astype(low)
    grad_bias_out = jnp.sum(grad_attn_own.astype(f32), axis=0)
    grad_attn = lax.all_gather(grad_attn_own, "seq", axis=0, tiled=True)
    unpick = (slot_row[:, None] == jnp.arange(packed)[None, :]).astype(low)
    placed_middle = jnp.where(
        (jnp.arange(packed) // share == seq_index)[:, None], middle + row_params[7], 0.0
    )
    out_part = (
        product("rf,fd->rd", hidden, w_down) + placed_middle + zero_of(grad_attn_own[0, 0]).astype(f32)
    ).astype(low)
    out_slots = product("cr,rd->cd", unpick, out_part).astype(low)
    first_moment, top, rest = momentum(moments, back_wide)
    wide_gram = gram_of(top, rest)
    gram_share = lax.psum_scatter(wide_gram, "seq", scatter_dimension=0, tiled=True)
    first_gram = lax.all_gather(gram_share, "seq", axis=0, tiled=True)


    grad_context = product("de,rd->er", w_out_own, grad_attn).astype(low)
    grad_qkv = attend_back(qkv, soft, grad_context.reshape(heads, head_pad, packed), wide_gram, out_slots, score_scale)
    grad_qkv_flat = grad_qkv.reshape(3 * square_rows, packed)
    grad_attn_cols = lax.dynamic_slice_in_dim(grad_attn, seq_index * cols, cols, axis=1)
    grad_w_out = product("rd,er->de", grad_attn_cols, context)
    grad_w_qkv = product("er,rd->ed", grad_qkv_flat, normed)
    grad_qkv_bias = jnp.sum(grad_qkv.astype(f32), axis=3)[:, :, :head_size].reshape(3, cols)

    grad_normed_part = product("er,ed->rd", grad_qkv_flat, w_qkv)
    grad_gain_one = jnp.sum(grad_normed_part * hat_packed, axis=0)
    grad_shift_one = jnp.sum(grad_normed_part, axis=0)
    grad_normed_slots = product("cr,rd->cd", unpick, grad_normed_part.astype(low)).astype(low)

    grad_mid_slots = product("rc,rd->cd", own_pick, grad_attn)

    def square_parts(x):
        x = jnp.pad(x.astype(low), ((0, square_total - square_rows), (0, 0)))
        return x.reshape(dp_count, square_chunk, width)

    late = [square_parts(grad_w_qkv[m * square_rows : (m + 1) * square_rows]) for m in range(3)]
    grad_w_out = jnp.pad(
        grad_w_out.reshape(heads, head_size, width), ((0, 0), (0, head_pad - head_size), (0, 0))
    )
    late.append(square_parts(grad_w_out.reshape(square_rows, width)))
    sum_qk = scatter_sum(jnp.concatenate(late[:2], axis=1), orders[0])
    sum_vo = scatter_sum(jnp.concatenate(late[2:], axis=1), orders[1])
    square_back = to_owner(
        [
            (sum_qk[:square_chunk], 0),
            (sum_qk[square_chunk:], 1),
            (sum_vo[:square_chunk], 2),
            (sum_vo[square_chunk:], 3),
        ]
    )
    back_square = send(after(square_back, gram_share[0, 0])).reshape(square_total, width)[:square_rows]
    back_square = back_square.reshape(heads, head_pad, width)[:, :head_size].reshape(cols, width)
    first_moment, top, rest = momentum_again(
        moments, back_wide[:cols] + back_square, first_moment, top, rest, grad_normed_slots, grad_mid_slots
    )
    def spot(piece):
        return lax.dynamic_update_slice_in_dim(
            jnp.zeros((piece.shape[0] * seq_count,), f32), piece, seq_index * piece.shape[0], 0
        )

    vector_grad = jnp.concatenate(
        [
            grad_gain_one,
            grad_shift_one,
            spot(grad_qkv_bias[0]),
            spot(grad_qkv_bias[2]),
            grad_bias_out,
            grad_gain_two,
            grad_shift_two,
            grad_bias_down,
            spot(grad_up_bias),
        ]
    )
    padded = -(-vector_grad.shape[0] // 1024) * 1024
    vector_grad = jnp.pad(vector_grad, (0, padded - vector_grad.shape[0])).reshape(-1, 128)
    vector_block = total_sum(after(vector_grad, top[0, 0].astype(f32)))
    (direction,) = touch([top[:cols]], first_gram, vector_block)
    direction = lax.all_gather(direction, "seq", axis=0, tiled=True)
    is_square = jnp.any(owner_table[:4] == dp_index).astype(jnp.int32).reshape(1)
    grad_normed_slots, out_slots = touch([grad_normed_slots, out_slots], direction, first_gram)
    update_scale = jnp.zeros((), f32)
    for m in range(6):
        update_scale = jnp.where(
            owner_table[m] == dp_index,
            jnp.float32(matrix_rate * 0.2 * math.sqrt(max(width, widths[m]))),
            update_scale,
        )

    grad_normed = lax.psum_scatter(
        grad_normed_slots, "seq", scatter_dimension=0, tiled=True
    ).astype(f32)
    block_out = lax.psum_scatter(
        out_slots, "seq", scatter_dimension=0, tiled=True
    ).astype(f32)
    hat_one, inverse_one = whiten(rows_in)
    grad_in_norm = whiten_back(grad_normed, row_params[0], hat_one, inverse_one)
    grad_tokens = (grad_mid_slots + grad_in_norm) * own_valid

    vector_total = lax.dynamic_slice_in_dim(
        vector_block.reshape(-1), seq_index * vector_count, vector_count
    )
    updated = iterate(
        is_square, update_scale.reshape(1), first_gram, direction, top, rest, slab, vector_block
    )

    first_new = beta_first * vector_moments[0] + (1.0 - beta_first) * vector_total
    second_new = beta_second * vector_moments[1] + (1.0 - beta_second) * vector_total * vector_total
    first_fix = 1.0 - beta_first**STEP
    second_fix = 1.0 - beta_second**STEP
    vector_new = vectors - vector_rate * (first_new / first_fix) / (
        jnp.sqrt(second_new / second_fix) + adam_eps
    )
    return (
        block_out[None],
        grad_tokens[None],
        jnp.transpose(first_moment, (2, 1, 0))[None],
        jnp.transpose(updated, (2, 1, 0))[None],
        first_new,
        second_new,
        vector_new,
    )


def solution(mesh):
    in_specs = (
        P("dp", "seq", None),
        P("dp", "seq", None),
        P("dp", None),
        P(),
        P("dp", None, "seq", None),
        P("dp", None, "seq", None),
        P("seq"),
        P(None, "seq"),
    )
    out_specs = (
        P("dp", "seq", None),
        P("dp", "seq", None),
        P("dp", None, "seq", None),
        P("dp", None, "seq", None),
        P("seq"),
        P("seq"),
        P("seq"),
    )
    return jax.shard_map(local, mesh=mesh, in_specs=in_specs, out_specs=out_specs, check_vma=False)
```

time: 654 us -> 664 us (1.015)
  other arithmetic: 38.7 us -> 58.8 us
  waiting for transfers between devices: 245 us -> 230 us
  starting transfers between devices: 53.6 us -> 40 us
  local copies, waits for them, and re-layouts: 66.6 us -> 77.8 us
  matrix products: 65 us -> 75.6 us
    all_gather x0 -> x1, waiting for transfers between devices: none -> 54.3 us  [local(): direction = lax.all_gather(direction, 'seq', axis=0, tiled=True)]
    all_gather x1, waiting for transfers between devices: 0.6 us -> 46.2 us  [local(): gathered = lax.all_gather(payload, 'seq', axis=0, tiled=False)]
    reduce_scatter x1, waiting for transfers between devices: 55.2 us -> 10.1 us  [local(): lax.psum_scatter(wide_gram, 'seq', scatter_dimension=0, tiled=True)]
    ppermute x6 -> x3, waiting for transfers between devices: 39.2 us -> 2.43 us  [arrivals(): lax.ppermute(piece, 'seq', [(i, (i + shift) % count) for i in range(count)])]
    all_gather x1, waiting for transfers between devices: 28.2 us -> 4.15 us  [local(): first_gram = lax.all_gather(gram_share, 'seq', axis=0, tiled=True)]
    all_to_all x3, waiting for transfers between devices: 50.3 us -> 27.5 us  [send(): return lax.all_to_all(x, 'dp', split_axis=0, concat_axis=0, tiled=True)]
    ppermute x6 -> x3, starting transfers between devices: 15.3 us -> 3.01 us  [arrivals(): lax.ppermute(piece, 'seq', [(i, (i + shift) % count) for i in range(count)])]
    dot_general x15 -> x16, matrix products: 65 us -> 75.6 us  [product(): return jnp.einsum(form, left, right, preferred_element_type=f32)]
  transfers between devices with their start and end apart: 44 -> 45, of which waited for: 24 -> 24; matrix products, arithmetic and copies ran while one was open for 15% -> 23% of each run, Pallas kernels for 19% -> 21%
where the time goes in v2:
time: 664 us; the launch traced here: 654 us
  waiting for transfers between devices  230 us (35%)
  Pallas kernels  137 us (21%)
  local copies, waits for them, and re-layouts  77.8 us (12%)
  matrix products  75.6 us (11%)
  other arithmetic  58.8 us (9%)
  starting transfers between devices  40 us (6%)
  between operations  34.8 us (5%)
    pallas_call x1, Pallas kernels, iterate(): call(functools.partial(iterate_body, total), 'iterate', vmem=56, in_specs...  95.5 us
    dot_general x16, matrix products, product(): return jnp.einsum(form, left, right, preferred_element_type=f32)  75.6 us
    ppermute x30, waiting for transfers between devices, flip(): return lax.ppermute(x, axis, [(i, i ^ mask) for i in range(count)])  58 us
    all_gather x1, waiting for transfers between devices, local(): direction = lax.all_gather(direction, 'seq', axis=0, tiled=True)  54.3 us
    all_gather x1, waiting for transfers between devices, local(): gathered = lax.all_gather(payload, 'seq', axis=0, tiled=False)  46.2 us
    all_to_all x3, waiting for transfers between devices, send(): return lax.all_to_all(x, 'dp', split_axis=0, concat_axis=0, tiled=True)  27.5 us
    ppermute x30, starting transfers between devices, flip(): return lax.ppermute(x, axis, [(i, i ^ mask) for i in range(count)])  23.1 us
    all_gather x1, waiting for transfers between devices, local(): lax.all_gather(context_own.reshape(cols, packed), 'seq', axis=0, tiled=True)  22.9 us
  transfers between devices with their start and end apart: 45, of which 24 were waited for; matrix products, arithmetic and copies ran while one was open for 23% of the time, Pallas kernels for 21%

profile of v2, /device:TPU:0, one launch (start us, length us, event | category | flops | bytes accessed | tf_op | source)
XLA Modules:
  0.0 654.0 jit_solution(2165467610928299323)
XLA Ops:
  10.0 2.0 fusion.62
  13.3 3.6 prep_wide.1
  18.4 5.3 all-to-all-start
  23.8 2.3 prep_square.1
  26.1 3.2 collective-permute-start.2
  38.4 17.1 %all-to-all-done = bf16[8,136,1152]{2,1,0:T(8,128)(2,1)} async-done(((bf16[8,136,1152]{2,1,0:T(8,128)(2,1)}), bf16[8,136,1152]{2,1,0:T(8,128)(2,1)}, u32[]{:S(2)}, u32[]{:S(2)}) %all-to-all-start) | async-done | bytes 2506784 | tf_op jit(solution)/shard_map/all_to_all | solution.py:652
  55.5 2.0 constant_dynamic-update-slice_fusion.9
  61.9 46.2 %all-gather.15.cloned.1.call-done = bf16[2112,1152]{1,0:T(8,128)(2,1)} async-done(((bf16[528,1152]{1,0:T(8,128)(2,1)}), bf16[2112,1152]{1,0:T(8,128)(2,1)}) %all-gather.15.cloned.1.call-update) | async-done | bytes 4866064 | tf_op jit(solution)/shard_map/all_gather | solution.py:627
  113.7 1.8 pad_maximum_fusion
  117.4 3.6 convolution_convert_fusion.5
  123.7 3.1 collective-permute-done.11
  138.0 2.9 fusion.69
  145.4 2.3 collective-permute-start.4
  147.7 3.7 select_bitcast_fusion.2
  151.4 2.1 collective-permute-done.4
  156.9 2.6 collective-permute-start.9
  161.9 3.8 add_convert_fusion.2
  165.7 6.5 attend.1
  184.2 2.6 constant_dynamic-update-slice_fusion.5
  193.5 22.9 %all-gather.7.cloned.1.call-done = bf16[1152,768]{1,0:T(8,128)(2,1)} async-done(((bf16[288,768]{1,0:T(8,128)(2,1)}), bf16[1152,768]{1,0:T(8,128)(2,1)}) %all-gather.7.cloned.1.call-update) | async-done | bytes 1769488 | tf_op jit(solution)/shard_map/all_gather | solution.py:704
  216.4 6.2 fusion.70
  225.1 2.4 convolution_add_fusion
  227.6 4.2 convert_reduce_fusion
  231.7 13.7 %convolution_convert_fusion = bf16[1088,1152]{1,0:T(8,128)(2,1)S(1)} fusion(bf16[768,1088]{0,1:T(8,128)(2,1)S(1)} %get-tuple-element.102, f32[768,1152]{1,0:T(8,128)S(1)} %subtract_multiply_fusion, f32[1152]{0:T(1024)S(1)} %copy-done.46, f32[1152]{0:T(1024)S(1)} %get-tuple-element.82), kind=kOutput, calls=%fused_computation.2 | convolution fusion | flops 1929093120 | bytes 7726080 | tf_op jit(solution)/shard_map/rf,rd->fd/dot_general | solution.py:467
  245.5 1.9 fusion.59
  247.8 3.0 convolution_convert_fusion.1
  257.2 6.1 fusion.4
  263.4 2.1 fusion.7
  272.9 8.7 %collective-permute-done.17 = bf16[1,1,2,136,1152]{4,3,2,1,0:T(8,128)(2,1)S(1)} collective-permute-done((bf16[1,1,2,136,1152]{4,3,2,1,0:T(8,128)(2,1)S(1)}, bf16[1,1,2,136,1152]{4,3,2,1,0:T(8,128)(2,1)S(1)}, u32[]{:S(2)}, u32[]{:S(2)}) %collective-permute-start.17) | collective-permute-done | bytes 626720 | tf_op jit(solution)/shard_map/ppermute | solution.py:472
  283.3 1.9 collective-permute-done.20
  285.5 5.7 collective-permute-done.18
  296.3 4.4 reduce-scatter.5.cloned.1.call-done
  300.7 2.3 fusion.24
  303.0 3.2 convert_reduce_fusion.4
  311.1 4.4 all-to-all-start.1
  315.5 1.9 iota_compare_fusion.9
  317.4 2.5 constant_dynamic-slice_fusion.4
  320.0 2.3 copy.24
  322.3 2.0 pad.32
  332.3 9.7 %convolution_convert_fusion.3.other_ref.refs_1_ = bf16[1024,1152]{1,0:T(8,128)(2,1)} fusion(s32[1024]{0:T(1024)} %copy-done.49, f32[768,1152]{1,0:T(8,128)S(1)} %get-tuple-element.99, bf16[1088,1152]{1,0:T(8,128)(2,1)} %constant_dynamic-update-slice_fusion.5, f32[]{:T(128)S(6)} %convert.28, f32[1152]{0:T(1024)} %get-tuple-element.80, ...), kind=kOutput, calls=%fused_computation.12 | convolution fusion | flops 3751034880 | bytes 11756804 | tf_op jit(solution)/shard_map/cr,rd->cd/dot_general | solution.py:467
  342.0 4.5 all-to-all-done.1
  346.5 7.8 %momentum.1 = (f32[1076,1,1152]{2,1,0:T(1,128)}, bf16[1088,1152]{1,0:T(8,128)(2,1)S(1)}, bf16[1088,1152]{1,0:T(8,128)(2,1)S(1)}) custom-call(f32[1076,1,1152]{2,1,0:T(1,128)} %bitcast.177, bf16[1088,1152]{1,0:T(8,128)(2,1)} %bitcast.59.grad_ref), custom_call_target="tpu_custom_call" | custom-call | tf_op jit(solution)/shard_map/momentum/pallas_call | solution.py:110
  354.3 9.0 %gram.1.first_ref = f32[5760,128]{1,0:T(8,128)} custom-call(bf16[1088,1152]{1,0:T(8,128)(2,1)S(1)} %get-tuple-element.20.top_ref.refs_1_, bf16[1088,1152]{1,0:T(8,128)(2,1)S(1)} %get-tuple-element.21.rest_ref.refs_2_), custom_call_target="tpu_custom_call" | custom-call | tf_op jit(solution)/shard_map/gram/pallas_call | solution.py:169
  366.3 2.5 convolution_convert_fusion.6
  370.2 8.8 %attend_back.1 = bf16[3,4,80,768]{3,2,1,0:T(8,128)(2,1)S(1)} custom-call(bf16[3,4,80,768]{3,2,1,0:T(8,128)(2,1)S(1)} %bitcast.171, bf16[4,768,768]{2,1,0:T(8,128)(2,1)} %get-tuple-element.18.soft_ref, bf16[4,80,768]{2,1,0:T(8,128)(2,1)S(1)} %bitcast.175, f32[5760,128]{1,0:T(8,128)} %gram.1.first_ref, ...), custom_call_target="tpu_custom_call" | custom-call | tf_op jit(solution)/shard_map/attend_back/pallas_call | solution.py:425
  379.4 4.3 convolution_convert_fusion.4
  387.7 6.5 fusion.56
  399.5 7.9 %collective-permute-done.23 = bf16[2,1,1,80,1152]{4,3,2,1,0:T(8,128)(2,1)S(1)} collective-permute-done((bf16[2,1,1,80,1152]{4,3,2,1,0:T(8,128)(2,1)S(1)}, bf16[2,1,1,80,1152]{4,3,2,1,0:T(8,128)(2,1)S(1)}, u32[]{:S(2)}, u32[]{:S(2)}) %collective-permute-start.23) | collective-permute-done | bytes 368672 | tf_op jit(solution)/shard_map/ppermute | solution.py:472
  409.6 10.1 %reduce-scatter.7.cloned.1.call-done = f32[1440,128]{1,0:T(8,128)} async-done(((f32[5760,128]{1,0:T(8,128)}), f32[1440,128]{1,0:T(8,128)}) %reduce-scatter.7.cloned.1.call-update) | async-done | bytes 737296 | tf_op jit(solution)/shard_map/reduce_scatter | solution.py:761
  421.3 4.7 collective-permute-done.27
  429.3 3.6 all-to-all-start.2
  433.9 5.2 convolution_convert_fusion.2.refs_3_.refs_0_
  439.1 5.9 all-to-all-done.2
  446.2 3.5 momentum_again.1
  453.4 3.7 collective-permute-done.29
  457.7 3.6 collective-permute-done.30
  462.5 8.2 %collective-permute-done.31 = f32[112,128]{1,0:T(8,128)S(1)} collective-permute-done((f32[112,128]{1,0:T(8,128)S(1)}, f32[112,128]{1,0:T(8,128)S(1)}, u32[]{:S(2)}, u32[]{:S(2)}) %collective-permute-start.31) | collective-permute-done | bytes 57376 | tf_op jit(solution)/shard_map/ppermute | solution.py:472
  470.8 2.0 slice.306.refs_0_
  472.8 6.6 %collective-permute-done.32 = f32[112,128]{1,0:T(8,128)S(1)} collective-permute-done((f32[112,128]{1,0:T(8,128)S(1)}, f32[112,128]{1,0:T(8,128)S(1)}, u32[]{:S(2)}, u32[]{:S(2)}) %collective-permute-start.32) | collective-permute-done | bytes 57376 | tf_op jit(solution)/shard_map/ppermute | solution.py:472
  479.4 4.1 all-gather.11.cloned.1.call-done.refs_1_.refs_3_.gram_ref
  483.6 1.8 copy-done.1
  485.5 54.3 %all-gather.13.cloned.1.call-done.refs_2_.full_hbm = bf16[1152,1152]{1,0:T(8,128)(2,1)} async-done(((bf16[288,1152]{1,0:T(8,128)(2,1)}), bf16[1152,1152]{1,0:T(8,128)(2,1)}) %all-gather.13.cloned.1.call-update) | async-done | bytes 2654224 | tf_op jit(solution)/shard_map/all_gather | solution.py:826
  546.3 95.5 %iterate.1 = f32[1076,1,1152]{2,1,0:T(1,128)} custom-call(s32[1]{0:T(128)} %bitcast.81.square_ref, f32[1]{0:T(128)} %bitcast.82.rate_ref, f32[5760,128]{1,0:T(8,128)} %all-gather.11.cloned.1.call-done.refs_1_.refs_3_.gram_ref, bf16[1152,1152]{1,0:T(8,128)(2,1)} %all-gather.13.cloned.1.call-done.refs_2_.full_hbm, ...), custom_call_target="tpu_custom_call" | custom-call | flops 80000000000 | bytes 20000000 | tf_op jit(solution)/shard_map/iterate/pallas_call | solution.py:361
  643.4 2.2 bitcast_convert_fusion.1
  (372 shorter events, 125.0 us)
Async XLA Ops:
  7.2 100.8 %all-gather.15.cloned.1.call-start = ((), (), s32[]{:S(2)}) async-start(), calls=%async_computation.15 | async-start | bytes 6082560 | tf_op jit(solution)/shard_map/all_gather | solution.py:627
  18.4 37.1 %all-to-all-start = ((bf16[8,136,1152]{2,1,0:T(8,128)(2,1)}), bf16[8,136,1152]{2,1,0:T(8,128)(2,1)}, u32[]{:S(2)}, u32[]{:S(2)}) async-start(bf16[8,136,1152]{2,1,0:T(8,128)(2,1)} %bitcast.169), calls=%async_computation | async-start | bytes 5013504 | tf_op jit(solution)/shard_map/all_to_all | solution.py:652
  23.7 12.1 %copy-start.59 = (s32[1,4]{1,0:T(1,128)S(1)}, s32[1,4]{1,0:T(1,128)}, u32[]{:S(2)}) copy-start(s32[1,4]{1,0:T(1,128)} %param.12) | copy-start | bytes 52
  23.7 192.6 %all-gather.7.cloned.1.call-start = ((), (), s32[]{:S(2)}) async-start(), calls=%async_computation.7 | async-start | bytes 2211840 | tf_op jit(solution)/shard_map/all_gather | solution.py:704
  26.1 84.7 %collective-permute-start.2 = (bf16[320,1152]{1,0:T(8,128)(2,1)S(1)}, bf16[320,1152]{1,0:T(8,128)(2,1)}, u32[]{:S(2)}, u32[]{:S(2)}) collective-permute-start(bf16[320,1152]{1,0:T(8,128)(2,1)S(1)} %prep_square.1), channel_id=1, source_target_pairs={{0,24},{4,28},{8,16},{12,20},{16,8},{20,12},{24,0},{28,4},{1,25},{... | collective-permute-start | bytes 2211848 | tf_op jit(solution)/shard_map/ppermute | solution.py:472
  29.3 84.2 %collective-permute-start.1 = (bf16[320,1152]{1,0:T(8,128)(2,1)S(1)}, bf16[320,1152]{1,0:T(8,128)(2,1)S(1)}, u32[]{:S(2)}, u32[]{:S(2)}) collective-permute-start(bf16[320,1152]{1,0:T(8,128)(2,1)S(1)} %prep_square.1), channel_id=1, source_target_pairs={{0,16},{4,20},{8,24},{12,28},{16,0},{20,4},{24,8},{28,12},{1,17},{... | collective-permute-start | bytes 2211848 | tf_op jit(solution)/shard_map/ppermute | solution.py:472
  29.8 83.8 %collective-permute-start = (bf16[320,1152]{1,0:T(8,128)(2,1)S(1)}, bf16[320,1152]{1,0:T(8,128)(2,1)S(1)}, u32[]{:S(2)}, u32[]{:S(2)}) collective-permute-start(bf16[320,1152]{1,0:T(8,128)(2,1)S(1)} %prep_square.1), channel_id=1, source_target_pairs={{0,8},{4,12},{8,0},{12,4},{16,24},{20,28},{24,16},{28,20},{1,9},{5... | collective-permute-start | bytes 2211848 | tf_op jit(solution)/shard_map/ppermute | solution.py:472
  37.8 79.6 %copy-start.49 = (s32[1024]{0:T(1024)}, s32[1024]{0:T(1024)S(1)}, u32[]{:S(2)}) copy-start(s32[1024]{0:T(1024)S(1)} %add_select_fusion.4) | copy-start | bytes 12292
  58.6 64.0 %collective-permute-start.13 = (bf16[272,1152]{1,0:T(8,128)(2,1)S(1)}, bf16[272,1152]{1,0:T(8,128)(2,1)}, u32[]{:S(2)}, u32[]{:S(2)}) collective-permute-start(bf16[272,1152]{1,0:T(8,128)(2,1)S(1)} %pad_maximum_fusion.7), channel_id=1, source_target_pairs={{0,24},{4,28},{8,16},{12,20},{16,8},{20,12},{24,0},{28,4},{1,25},{... | collective-permute-start | bytes 1880072 | tf_op jit(solution)/shard_map/ppermute | solution.py:472
  59.1 68.8 %collective-permute-start.12 = (bf16[272,1152]{1,0:T(8,128)(2,1)S(1)}, bf16[272,1152]{1,0:T(8,128)(2,1)}, u32[]{:S(2)}, u32[]{:S(2)}) collective-permute-start(bf16[272,1152]{1,0:T(8,128)(2,1)S(1)} %pad_maximum_fusion.7), channel_id=1, source_target_pairs={{0,16},{4,20},{8,24},{12,28},{16,0},{20,4},{24,8},{28,12},{1,17},{... | collective-permute-start | bytes 1880072 | tf_op jit(solution)/shard_map/ppermute | solution.py:472
  110.8 16.0 %collective-permute-start.11 = (bf16[272,1152]{1,0:T(8,128)(2,1)S(1)}, bf16[272,1152]{1,0:T(8,128)(2,1)S(1)}, u32[]{:S(2)}, u32[]{:S(2)}) collective-permute-start(bf16[272,1152]{1,0:T(8,128)(2,1)S(1)} %pad_maximum_fusion.7), channel_id=1, source_target_pairs={{0,8},{4,12},{8,0},{12,4},{16,24},{20,28},{24,16},{28,20},{1,9},{5... | collective-permute-start | bytes 1880072 | tf_op jit(solution)/shard_map/ppermute | solution.py:472
  122.6 19.8 %collective-permute-start.3 = (bf16[4,320,1152]{2,1,0:T(8,128)(2,1)}, bf16[4,320,1152]{2,1,0:T(8,128)(2,1)}, u32[]{:S(2)}, u32[]{:S(2)}) collective-permute-start(bf16[4,320,1152]{2,1,0:T(8,128)(2,1)} %pad_maximum_fusion), channel_id=1, source_target_pairs={{0,4},{4,0},{8,12},{12,8},{16,20},{20,16},{24,28},{28,24},{1,5},{5... | collective-permute-start | bytes 8847368 | tf_op jit(solution)/shard_map/ppermute | solution.py:472
  135.6 48.6 %collective-permute-start.15 = (bf16[544,1152]{1,0:T(8,128)(2,1)}, bf16[544,1152]{1,0:T(8,128)(2,1)}, u32[]{:S(2)}, u32[]{:S(2)}) collective-permute-start(bf16[544,1152]{1,0:T(8,128)(2,1)} %pad_maximum_fusion.3), channel_id=1, source_target_pairs={{0,4},{4,0},{8,12},{12,8},{16,20},{20,16},{24,28},{28,24},{1,5},{5... | collective-permute-start | bytes 3760136 | tf_op jit(solution)/shard_map/ppermute | solution.py:472
  136.8 50.0 %collective-permute-start.14 = (bf16[544,1152]{1,0:T(8,128)(2,1)}, bf16[544,1152]{1,0:T(8,128)(2,1)}, u32[]{:S(2)}, u32[]{:S(2)}) collective-permute-start(bf16[544,1152]{1,0:T(8,128)(2,1)} %pad_maximum_fusion.2), channel_id=1, source_target_pairs={{0,4},{4,0},{8,12},{12,8},{16,20},{20,16},{24,28},{28,24},{1,5},{5... | collective-permute-start | bytes 3760136 | tf_op jit(solution)/shard_map/ppermute | solution.py:472
  140.8 21.1 %copy-start.17 = (f32[768,1152]{1,0:T(8,128)}, f32[768,1152]{1,0:T(8,128)S(1)}, u32[]{:S(2)}) copy-start(f32[768,1152]{1,0:T(8,128)S(1)} %get-tuple-element.97) | copy-start | bytes 10616836
  144.7 10.4 %collective-permute-start.6 = (bf16[40,1152]{1,0:T(8,128)(2,1)S(1)}, bf16[40,1152]{1,0:T(8,128)(2,1)S(1)}, u32[]{:S(2)}, u32[]{:S(2)}) collective-permute-start(bf16[40,1152]{1,0:T(8,128)(2,1)S(1)} %get-tuple-element.50), channel_id=1, source_target_pairs={{0,3},{1,0},{2,1},{3,2},{4,7},{5,4},{6,5},{7,6},{8,11},{9,8},{10,9... | collective-permute-start | bytes 276488 | tf_op jit(solution)/shard_map/ppermute | solution.py:507
  145.3 9.1 %collective-permute-start.5 = (bf16[40,1152]{1,0:T(8,128)(2,1)S(1)}, bf16[40,1152]{1,0:T(8,128)(2,1)S(1)}, u32[]{:S(2)}, u32[]{:S(2)}) collective-permute-start(bf16[40,1152]{1,0:T(8,128)(2,1)S(1)} %get-tuple-element.50), channel_id=1, source_target_pairs={{0,2},{1,3},{2,0},{3,1},{4,6},{5,7},{6,4},{7,5},{8,10},{9,11},{10,... | collective-permute-start | bytes 276488 | tf_op jit(solution)/shard_map/ppermute | solution.py:507
  145.4 8.0 %collective-permute-start.4 = (bf16[40,1152]{1,0:T(8,128)(2,1)S(1)}, bf16[40,1152]{1,0:T(8,128)(2,1)S(1)}, u32[]{:S(2)}, u32[]{:S(2)}) collective-permute-start(bf16[40,1152]{1,0:T(8,128)(2,1)S(1)} %get-tuple-element.50), channel_id=1, source_target_pairs={{0,1},{1,2},{2,3},{3,0},{4,5},{5,6},{6,7},{7,4},{8,9},{9,10},{10,1... | collective-permute-start | bytes 276488 | tf_op jit(solution)/shard_map/ppermute | solution.py:507
  156.9 21.7 %collective-permute-start.9 = (bf16[160,1152]{1,0:T(8,128)(2,1)}, bf16[160,1152]{1,0:T(8,128)(2,1)}, u32[]{:S(2)}, u32[]{:S(2)}) collective-permute-start(bf16[160,1152]{1,0:T(8,128)(2,1)} %bitcast.33), channel_id=1, source_target_pairs={{0,24},{4,28},{8,16},{12,20},{16,8},{20,12},{24,0},{28,4},{1,25},{... | collective-permute-start | bytes 1105928 | tf_op jit(solution)/shard_map/ppermute | solution.py:472
  159.5 18.0 %collective-permute-start.8 = (bf16[160,1152]{1,0:T(8,128)(2,1)}, bf16[160,1152]{1,0:T(8,128)(2,1)}, u32[]{:S(2)}, u32[]{:S(2)}) collective-permute-start(bf16[160,1152]{1,0:T(8,128)(2,1)} %bitcast.33), channel_id=1, source_target_pairs={{0,16},{4,20},{8,24},{12,28},{16,0},{20,4},{24,8},{28,12},{1,17},{... | collective-permute-start | bytes 1105928 | tf_op jit(solution)/shard_map/ppermute | solution.py:472
  160.1 16.4 %collective-permute-start.7 = (bf16[160,1152]{1,0:T(8,128)(2,1)}, bf16[160,1152]{1,0:T(8,128)(2,1)}, u32[]{:S(2)}, u32[]{:S(2)}) collective-permute-start(bf16[160,1152]{1,0:T(8,128)(2,1)} %bitcast.33), channel_id=1, source_target_pairs={{0,8},{4,12},{8,0},{12,4},{16,24},{20,28},{24,16},{28,20},{1,9},{5... | collective-permute-start | bytes 1105928 | tf_op jit(solution)/shard_map/ppermute | solution.py:472
  175.2 125.6 %reduce-scatter.5.cloned.1.call-start = ((), (), s32[]{:S(2)}) async-start(), calls=%async_computation.8 | async-start | bytes 2211840 | tf_op jit(solution)/shard_map/reduce_scatter | solution.py:735
  181.0 8.9 %collective-permute-start.10 = (bf16[4,1,160,1152]{3,2,1,0:T(8,128)(2,1)}, bf16[4,1,160,1152]{3,2,1,0:T(8,128)(2,1)}, u32[]{:S(2)}, u32[]{:S(2)}) collective-permute-start(bf16[4,1,160,1152]{3,2,1,0:T(8,128)(2,1)} %constant_dynamic-slice_fusion.5), channel_id=1, source_target_pairs={{0,4},{4,0},{8,12},{12,8},{16,20},{20,16},{24,28},{28,24},{1,5},{5... | collective-permute-start | bytes 4423688 | tf_op jit(solution)/shard_map/ppermute | solution.py:472
  227.5 20.2 %copy-start.61 = (f32[768,1088]{0,1:T(8,128)}, f32[768,1088]{0,1:T(8,128)S(1)}, u32[]{:S(2)}) copy-start(f32[768,1088]{0,1:T(8,128)S(1)} %convolution_add_fusion) | copy-start | bytes 10027012
  231.7 13.7 %copy-start.62 = (bf16[768,1088]{0,1:T(8,128)(2,1)}, bf16[768,1088]{0,1:T(8,128)(2,1)S(1)}, u32[]{:S(2)}) copy-start(bf16[768,1088]{0,1:T(8,128)(2,1)S(1)} %get-tuple-element.102) | copy-start | bytes 5013508
  247.8 15.6 %collective-permute-start.16 = (bf16[1,2,2,136,1152]{4,3,2,1,0:T(8,128)(2,1)}, bf16[1,2,2,136,1152]{4,3,2,1,0:T(8,128)(2,1)}, u32[]{:S(2)}, u32[]{:S(2)}) collective-permute-start(bf16[1,2,2,136,1152]{4,3,2,1,0:T(8,128)(2,1)} %bitcast.50), channel_id=1, source_target_pairs={{0,4},{4,0},{8,12},{12,8},{16,20},{20,16},{24,28},{28,24},{1,5},{5... | collective-permute-start | bytes 3760136 | tf_op jit(solution)/shard_map/ppermute | solution.py:472
  253.0 14.0 %collective-permute-start.19 = (bf16[1,2,2,136,1152]{4,3,2,1,0:T(8,128)(2,1)}, bf16[1,2,2,136,1152]{4,3,2,1,0:T(8,128)(2,1)}, u32[]{:S(2)}, u32[]{:S(2)}) collective-permute-start(bf16[1,2,2,136,1152]{4,3,2,1,0:T(8,128)(2,1)} %bitcast.53), channel_id=1, source_target_pairs={{0,4},{4,0},{8,12},{12,8},{16,20},{20,16},{24,28},{28,24},{1,5},{5... | collective-permute-start | bytes 3760136 | tf_op jit(solution)/shard_map/ppermute | solution.py:472
  263.3 101.6 %all-gather.9.cloned.1.call-start = ((), (), s32[]{:S(2)}) async-start(), calls=%async_computation.9 | async-start | bytes 2211840 | tf_op jit(solution)/shard_map/all_gather | solution.py:750
  265.5 16.1 %collective-permute-start.17 = (bf16[1,1,2,136,1152]{4,3,2,1,0:T(8,128)(2,1)S(1)}, bf16[1,1,2,136,1152]{4,3,2,1,0:T(8,128)(2,1)S(1)}, u32[]{:S(2)}, u32[]{:S(2)}) collective-permute-start(bf16[1,1,2,136,1152]{4,3,2,1,0:T(8,128)(2,1)S(1)} %slice.346), channel_id=1, source_target_pairs={{0,16},{4,20},{8,24},{12,28},{16,0},{20,4},{24,8},{28,12},{1,17},{... | collective-permute-start | bytes 1880072 | tf_op jit(solution)/shard_map/ppermute | solution.py:472
  268.7 16.5 %collective-permute-start.20 = (bf16[1,2,1,136,1152]{4,3,2,1,0:T(8,128)(2,1)S(1)}, bf16[1,2,1,136,1152]{4,3,2,1,0:T(8,128)(2,1)S(1)}, u32[]{:S(2)}, u32[]{:S(2)}) collective-permute-start(bf16[1,2,1,136,1152]{4,3,2,1,0:T(8,128)(2,1)S(1)} %slice.352), channel_id=1, source_target_pairs={{0,8},{4,12},{8,0},{12,4},{16,24},{20,28},{24,16},{28,20},{1,9},{5... | collective-permute-start | bytes 1880072 | tf_op jit(solution)/shard_map/ppermute | solution.py:472
  281.8 9.4 %collective-permute-start.18 = (bf16[1,1,1,136,1152]{4,3,2,1,0:T(8,128)(2,1)S(1)}, bf16[1,1,1,136,1152]{4,3,2,1,0:T(8,128)(2,1)S(1)}, u32[]{:S(2)}, u32[]{:S(2)}) collective-permute-start(bf16[1,1,1,136,1152]{4,3,2,1,0:T(8,128)(2,1)S(1)} %slice.348), channel_id=1, source_target_pairs={{0,8},{4,12},{8,0},{12,4},{16,24},{20,28},{24,16},{28,20},{1,9},{5... | collective-permute-start | bytes 940040 | tf_op jit(solution)/shard_map/ppermute | solution.py:472
  285.4 7.5 %collective-permute-start.21 = (bf16[1,1,1,136,1152]{4,3,2,1,0:T(8,128)(2,1)S(1)}, bf16[1,1,1,136,1152]{4,3,2,1,0:T(8,128)(2,1)S(1)}, u32[]{:S(2)}, u32[]{:S(2)}) collective-permute-start(bf16[1,1,1,136,1152]{4,3,2,1,0:T(8,128)(2,1)S(1)} %slice.354), channel_id=1, source_target_pairs={{0,16},{4,20},{8,24},{12,28},{16,0},{20,4},{24,8},{28,12},{1,17},{... | collective-permute-start | bytes 940040 | tf_op jit(solution)/shard_map/ppermute | solution.py:472
  311.1 35.4 %all-to-all-start.1 = ((bf16[8,136,1152]{2,1,0:T(8,128)(2,1)}), bf16[8,136,1152]{2,1,0:T(8,128)(2,1)}, u32[]{:S(2)}, u32[]{:S(2)}) async-start(bf16[8,136,1152]{2,1,0:T(8,128)(2,1)} %copy-done.9), calls=%async_computation.2 | async-start | bytes 5013504 | tf_op jit(solution)/shard_map/all_to_all | solution.py:652
  315.5 104.1 %reduce-scatter.7.cloned.1.call-start = ((), (), s32[]{:S(2)}) async-start(), calls=%async_computation.10 | async-start | bytes 3686400 | tf_op jit(solution)/shard_map/reduce_scatter | solution.py:761
  354.3 9.0 %copy-start = (bf16[1088,1152]{1,0:T(8,128)(2,1)}, bf16[1088,1152]{1,0:T(8,128)(2,1)S(1)}, u32[]{:S(2)}) copy-start(bf16[1088,1152]{1,0:T(8,128)(2,1)S(1)} %get-tuple-element.20.top_ref.refs_1_) | copy-start | bytes 7520260
  364.8 118.7 %all-gather.11.cloned.1.call-start = ((), (), s32[]{:S(2)}) async-start(), calls=%async_computation.11 | async-start | bytes 3686400 | tf_op jit(solution)/shard_map/all_gather | solution.py:762
  370.2 9.3 %copy-start.43 = (f32[768]{0:T(1024)S(1)}, f32[768]{0:T(1024)}, u32[]{:S(2)}) copy-start(f32[768]{0:T(1024)} %copy-done.42) | copy-start | bytes 9220
  370.2 9.3 %copy-start.45 = (f32[1152]{0:T(1024)S(1)}, f32[1152]{0:T(1024)}, u32[]{:S(2)}) copy-start(f32[1152]{0:T(1024)} %get-tuple-element.86) | copy-start | bytes 13828
  370.2 9.3 %copy-start.52 = (f32[768]{0:T(1024)S(1)}, f32[768]{0:T(1024)}, u32[]{:S(2)}) copy-start(f32[768]{0:T(1024)} %add_rsqrt_fusion.1) | copy-start | bytes 9220
  385.8 9.3 %collective-permute-start.22 = (bf16[2,2,1,80,1152]{4,3,2,1,0:T(8,128)(2,1)}, bf16[2,2,1,80,1152]{4,3,2,1,0:T(8,128)(2,1)}, u32[]{:S(2)}, u32[]{:S(2)}) collective-permute-start(bf16[2,2,1,80,1152]{4,3,2,1,0:T(8,128)(2,1)} %fusion.28), channel_id=1, source_target_pairs={{0,4},{4,0},{8,12},{12,8},{16,20},{20,16},{24,28},{28,24},{1,5},{5... | collective-permute-start | bytes 2211848 | tf_op jit(solution)/shard_map/ppermute | solution.py:472
  386.7 11.1 %collective-permute-start.25 = (bf16[2,2,1,80,1152]{4,3,2,1,0:T(8,128)(2,1)}, bf16[2,2,1,80,1152]{4,3,2,1,0:T(8,128)(2,1)}, u32[]{:S(2)}, u32[]{:S(2)}) collective-permute-start(bf16[2,2,1,80,1152]{4,3,2,1,0:T(8,128)(2,1)} %fusion.26), channel_id=1, source_target_pairs={{0,4},{4,0},{8,12},{12,8},{16,20},{20,16},{24,28},{28,24},{1,5},{5... | collective-permute-start | bytes 2211848 | tf_op jit(solution)/shard_map/ppermute | solution.py:472
  396.9 10.6 %collective-permute-start.23 = (bf16[2,1,1,80,1152]{4,3,2,1,0:T(8,128)(2,1)S(1)}, bf16[2,1,1,80,1152]{4,3,2,1,0:T(8,128)(2,1)S(1)}, u32[]{:S(2)}, u32[]{:S(2)}) collective-permute-start(bf16[2,1,1,80,1152]{4,3,2,1,0:T(8,128)(2,1)S(1)} %constant_dynamic-slice_fusion.3), channel_id=1, source_target_pairs={{0,8},{4,12},{8,0},{12,4},{16,24},{20,28},{24,16},{28,20},{1,9},{5... | collective-permute-start | bytes 1105928 | tf_op jit(solution)/shard_map/ppermute | solution.py:472
  399.1 28.9 %copy-start.55 = (pred[8]{0:T(512)(128)(4,1)S(1)}, pred[8]{0:T(512)(128)(4,1)}, u32[]{:S(2)}) copy-start(pred[8]{0:T(512)(128)(4,1)} %get-tuple-element.111) | copy-start | bytes 28
  399.1 28.9 %copy-start.56 = (pred[8]{0:T(512)(128)(4,1)S(1)}, pred[8]{0:T(512)(128)(4,1)}, u32[]{:S(2)}) copy-start(pred[8]{0:T(512)(128)(4,1)} %get-tuple-element.112) | copy-start | bytes 28
  399.1 28.9 %copy-start.57 = (pred[8]{0:T(512)(128)(4,1)S(1)}, pred[8]{0:T(512)(128)(4,1)}, u32[]{:S(2)}) copy-start(pred[8]{0:T(512)(128)(4,1)} %get-tuple-element.109) | copy-start | bytes 28
  399.1 28.9 %copy-start.58 = (pred[8]{0:T(512)(128)(4,1)S(1)}, pred[8]{0:T(512)(128)(4,1)}, u32[]{:S(2)}) copy-start(pred[8]{0:T(512)(128)(4,1)} %get-tuple-element.110) | copy-start | bytes 28
  399.1 10.3 %collective-permute-start.26 = (bf16[1,2,1,80,1152]{4,3,2,1,0:T(8,128)(2,1)S(1)}, bf16[1,2,1,80,1152]{4,3,2,1,0:T(8,128)(2,1)S(1)}, u32[]{:S(2)}, u32[]{:S(2)}) collective-permute-start(bf16[1,2,1,80,1152]{4,3,2,1,0:T(8,128)(2,1)S(1)} %constant_dynamic-slice_fusion.1), channel_id=1, source_target_pairs={{0,16},{4,20},{8,24},{12,28},{16,0},{20,4},{24,8},{28,12},{1,17},{... | collective-permute-start | bytes 1105928 | tf_op jit(solution)/shard_map/ppermute | solution.py:472
  407.6 13.6 %collective-permute-start.24 = (bf16[1,1,1,80,1152]{4,3,2,1,0:T(8,128)(2,1)S(1)}, bf16[1,1,1,80,1152]{4,3,2,1,0:T(8,128)(2,1)S(1)}, u32[]{:S(2)}, u32[]{:S(2)}) collective-permute-start(bf16[1,1,1,80,1152]{4,3,2,1,0:T(8,128)(2,1)S(1)} %constant_dynamic-slice_fusion.2), channel_id=1, source_target_pairs={{0,16},{4,20},{8,24},{12,28},{16,0},{20,4},{24,8},{28,12},{1,17},{... | collective-permute-start | bytes 552968 | tf_op jit(solution)/shard_map/ppermute | solution.py:472
  419.7 13.5 %copy-start.34 = (f32[1152]{0:T(1024)S(1)}, f32[1152]{0:T(1024)}, u32[]{:S(2)}) copy-start(f32[1152]{0:T(1024)} %get-tuple-element.61) | copy-start | bytes 13828
  419.7 14.2 %copy-start.50 = (s32[1024]{0:T(1024)S(1)}, s32[1024]{0:T(1024)}, u32[]{:S(2)}) copy-start(s32[1024]{0:T(1024)} %copy-done.49) | copy-start | bytes 12292
  419.7 6.3 collective-permute-start.27
  429.3 15.7 %all-to-all-start.2 = ((bf16[8,40,1152]{2,1,0:T(8,128)(2,1)}), bf16[8,40,1152]{2,1,0:T(8,128)(2,1)S(1)}, u32[]{:S(2)}, u32[]{:S(2)}) async-start(bf16[8,40,1152]{2,1,0:T(8,128)(2,1)} %add_add_fusion), calls=%async_computation.4 | async-start | bytes 1474560 | tf_op jit(solution)/shard_map/all_to_all | solution.py:652
  432.9 106.9 %all-gather.13.cloned.1.call-start = ((), (), s32[]{:S(2)}) async-start(), calls=%async_computation.12 | async-start | bytes 3317760 | tf_op jit(solution)/shard_map/all_gather | solution.py:826
  451.5 1.3 collective-permute-start.28
  452.8 4.2 collective-permute-start.29
  457.1 4.2 collective-permute-start.30
  461.3 9.4 %collective-permute-start.31 = (f32[112,128]{1,0:T(8,128)S(1)}, f32[112,128]{1,0:T(8,128)S(1)}, u32[]{:S(2)}, u32[]{:S(2)}) collective-permute-start(f32[112,128]{1,0:T(8,128)S(1)} %add.625), channel_id=1, source_target_pairs={{0,1},{1,0},{2,3},{3,2},{4,5},{5,4},{6,7},{7,6},{8,9},{9,8},{10,11... | collective-permute-start | bytes 172040 | tf_op jit(solution)/shard_map/ppermute | solution.py:472
  470.7 8.6 %collective-permute-start.32 = (f32[112,128]{1,0:T(8,128)S(1)}, f32[112,128]{1,0:T(8,128)S(1)}, u32[]{:S(2)}, u32[]{:S(2)}) collective-permute-start(f32[112,128]{1,0:T(8,128)S(1)} %add.626), channel_id=1, source_target_pairs={{0,2},{1,3},{2,0},{3,1},{4,6},{5,7},{6,4},{7,5},{8,10},{9,11},{10,... | collective-permute-start | bytes 172040 | tf_op jit(solution)/shard_map/ppermute | solution.py:472
  479.4 66.2 %copy-start.7 = (f32[112,128]{1,0:T(8,128)}, f32[112,128]{1,0:T(8,128)S(1)}, u32[]{:S(2)}) copy-start(f32[112,128]{1,0:T(8,128)S(1)} %add.627.refs_2_.first_ref) | copy-start | bytes 172036
  485.4 58.4 %copy-start.41 = (s32[6]{0:T(128)S(1)}, s32[6]{0:T(128)}, u32[]{:S(2)}) copy-start(s32[6]{0:T(128)} %param.13) | copy-start | bytes 76
  485.4 59.7 %copy-start.38 = (f32[2,3380]{1,0:T(2,128)S(1)}, f32[2,3380]{1,0:T(2,128)}, u32[]{:S(2)}) copy-start(f32[2,3380]{1,0:T(2,128)} %param.17) | copy-start | bytes 81124
  485.4 59.8 %copy-start.51 = (f32[256]{0:T(256)S(1)}, f32[256]{0:T(256)}, u32[]{:S(2)}) copy-start(f32[256]{0:T(256)} %get-tuple-element.62) | copy-start | bytes 3076
  485.4 156.4 %reduce-scatter.11.cloned.1.call-start = ((), (), s32[]{:S(2)}) async-start(), calls=%async_computation.14 | async-start | bytes 2949120 | tf_op jit(solution)/shard_map/reduce_scatter | solution.py:837
  539.8 103.6 %reduce-scatter.9.cloned.1.call-start = ((), (), s32[]{:S(2)}) async-start(), calls=%async_computation.13 | async-start | bytes 2949120 | tf_op jit(solution)/shard_map/reduce_scatter | solution.py:840
  (44 other events, 154.5 us)
Sparse Core Ops, SparseCore 0:
  13.4 94.5 all-gather.14
  175.3 41.0 all-gather.6
  263.4 37.2 reduce-scatter.4
  306.4 39.4 all-gather.8
  364.9 54.6 reduce-scatter.6
  421.1 62.4 all-gather.10
  485.7 54.0 all-gather.12
  542.1 46.7 reduce-scatter.10
  591.2 47.5 reduce-scatter.8

commit v3 on v2

--- a/solution.py
+++ b/solution.py
@@ -558,13 +558,13 @@
     return me ^ ((place % half) * 2 + place // half)
 
 
-def exchange(piece, first):
+def exchange(piece, first=None):
     half = lax.axis_size("dp") // 2
     arrived = [flip(piece, "dp", mask << 1) for mask in range(1, half)]
-    return [piece] + [after(x, first) for x in arrived]
-
-
-def gather_relative(pieces, first):
+    return [piece] + ([after(x, first) for x in arrived] if first is not None else arrived)
+
+
+def gather_relative(pieces, first=None):
     arrived = exchange(jnp.concatenate(pieces, axis=0), first)
     result, at = [], 0
     for piece in pieces:
@@ -652,7 +652,7 @@
         return lax.all_to_all(x, "dp", split_axis=0, concat_axis=0, tiled=True)
 
     square_own = prep_square(slab, payload, heads, head_size, head_pad)
-    near = jnp.stack(exchange(square_own, gathered[0, 0, 0]))
+    near = jnp.stack(exchange(square_own))
     far = flip(near, "dp", 1)
     squares = []
     for m in range(4):
@@ -668,7 +668,7 @@
     got_wide = send(wide_sent)
     wide_pieces = [lax.dynamic_index_in_dim(got_wide, owner_table[m], 0, keepdims=False) for m in (4, 5)]
 
-    w_up, w_down = gather_relative(wide_pieces, gathered[0, 0, 0])
+    w_up, w_down = gather_relative(wide_pieces)
 
     vector_full = gathered[:, capacity : capacity + vector_rows].reshape(seq_count, -1)
     vector_full = vector_full[:, :vector_count].reshape(-1).astype(f32)

time: 664 us -> 644 us (0.970)
  matrix products: 75.6 us -> 66.1 us
  other arithmetic: 58.8 us -> 50.2 us
    ppermute x30, waiting for transfers between devices: 58 us -> 123 us  [flip(): return lax.ppermute(x, axis, [(i, i ^ mask) for i in range(count)])]
    all_gather x1, waiting for transfers between devices: 46.2 us -> 0.02 us  [local(): gathered = lax.all_gather(payload, 'seq', axis=0, tiled=False)]
    all_to_all x3, waiting for transfers between devices: 27.5 us -> 10.5 us  [send(): return lax.all_to_all(x, 'dp', split_axis=0, concat_axis=0, tiled=True)]
    dot_general x16, matrix products: 75.6 us -> 66.1 us  [product(): return jnp.einsum(form, left, right, preferred_element_type=f32)]
    unnamed x142 -> x143, local copies, waits for them, and re-layouts: 21.6 us -> 21.2 us
  transfers between devices with their start and end apart: 45 -> 45, of which waited for: 24 -> 26; matrix products, arithmetic and copies ran while one was open for 23% -> 23% of each run, Pallas kernels for 21% -> 21%
where the time goes in v3:
time: 644 us; the launch traced here: 638 us
  waiting for transfers between devices  233 us (36%)
  Pallas kernels  138 us (21%)
  local copies, waits for them, and re-layouts  74.2 us (12%)
  matrix products  66.1 us (10%)
  other arithmetic  50.2 us (8%)
  starting transfers between devices  42.9 us (7%)
  between operations  33.3 us (5%)
    ppermute x30, waiting for transfers between devices, flip(): return lax.ppermute(x, axis, [(i, i ^ mask) for i in range(count)])  123 us
    pallas_call x1, Pallas kernels, iterate(): call(functools.partial(iterate_body, total), 'iterate', vmem=56, in_specs...  95.6 us
    dot_general x16, matrix products, product(): return jnp.einsum(form, left, right, preferred_element_type=f32)  66.1 us
    all_gather x1, waiting for transfers between devices, local(): direction = lax.all_gather(direction, 'seq', axis=0, tiled=True)  54.3 us
    ppermute x30, starting transfers between devices, flip(): return lax.ppermute(x, axis, [(i, i ^ mask) for i in range(count)])  23.2 us
    all_gather x1, waiting for transfers between devices, local(): lax.all_gather(context_own.reshape(cols, packed), 'seq', axis=0, tiled=True)  22.7 us
    unnamed x143, local copies, waits for them, and re-layouts  21.2 us
    all_to_all x3, starting transfers between devices, send(): return lax.all_to_all(x, 'dp', split_axis=0, concat_axis=0, tiled=True)  13.4 us
  transfers between devices with their start and end apart: 45, of which 26 were waited for; matrix products, arithmetic and copies ran while one was open for 23% of the time, Pallas kernels for 21%

profile of v3, /device:TPU:0, one launch (start us, length us, event | category | flops | bytes accessed | tf_op | source)
XLA Modules:
  0.0 638.2 jit_solution(15409628190753300491)
XLA Ops:
  7.2 4.9 prep_wide.1
  12.1 5.3 all-to-all-start
  22.2 2.2 prep_square.1
  24.5 3.1 collective-permute-start.2
  32.9 31.9 %collective-permute-done.2 = bf16[320,1152]{1,0:T(8,128)(2,1)S(1)} collective-permute-done((bf16[320,1152]{1,0:T(8,128)(2,1)S(1)}, bf16[320,1152]{1,0:T(8,128)(2,1)S(1)}, u32[]{:S(2)}, u32[]{:S(2)}) %collective-permute-start.2) | collective-permute-done | bytes 737312 | tf_op jit(solution)/shard_map/ppermute | solution.py:472
  64.8 14.2 %collective-permute-done.1 = bf16[320,1152]{1,0:T(8,128)(2,1)S(1)} collective-permute-done((bf16[320,1152]{1,0:T(8,128)(2,1)S(1)}, bf16[320,1152]{1,0:T(8,128)(2,1)S(1)}, u32[]{:S(2)}, u32[]{:S(2)}) %collective-permute-start.1) | collective-permute-done | bytes 737312 | tf_op jit(solution)/shard_map/ppermute | solution.py:472
  81.0 2.0 constant_dynamic-update-slice_fusion.9
  91.9 8.1 %collective-permute-done.11 = bf16[272,1152]{1,0:T(8,128)(2,1)S(1)} collective-permute-done((bf16[272,1152]{1,0:T(8,128)(2,1)S(1)}, bf16[272,1152]{1,0:T(8,128)(2,1)S(1)}, u32[]{:S(2)}, u32[]{:S(2)}) %collective-permute-start.11) | collective-permute-done | bytes 626720 | tf_op jit(solution)/shard_map/ppermute | solution.py:472
  100.9 13.7 %collective-permute-done.12 = bf16[272,1152]{1,0:T(8,128)(2,1)S(1)} collective-permute-done((bf16[272,1152]{1,0:T(8,128)(2,1)S(1)}, bf16[272,1152]{1,0:T(8,128)(2,1)S(1)}, u32[]{:S(2)}, u32[]{:S(2)}) %collective-permute-start.12) | collective-permute-done | bytes 626720 | tf_op jit(solution)/shard_map/ppermute | solution.py:472
  120.2 4.3 collective-permute-start.6
  125.7 3.7 select_bitcast_fusion.2
  129.3 2.2 collective-permute-done.4
  138.3 3.3 slice.322
  141.6 3.4 slice.313
  146.2 4.1 convolution_convert_fusion.5
  151.6 2.9 fusion.69
  158.1 4.9 add_convert_fusion.2
  163.0 6.5 %attend.1 = (bf16[4,72,768]{2,1,0:T(8,128)(2,1)}, bf16[4,768,768]{2,1,0:T(8,128)(2,1)}) custom-call(bf16[3,4,80,768]{3,2,1,0:T(8,128)(2,1)S(1)} %bitcast.163), custom_call_target="tpu_custom_call" | custom-call | tf_op jit(solution)/shard_map/attend/pallas_call | solution.py:394
  178.5 2.5 constant_dynamic-update-slice_fusion.5
  189.0 22.7 %all-gather.7.cloned.1.call-done = bf16[1152,768]{1,0:T(8,128)(2,1)} async-done(((bf16[288,768]{1,0:T(8,128)(2,1)}), bf16[1152,768]{1,0:T(8,128)(2,1)}) %all-gather.7.cloned.1.call-update) | async-done | bytes 1769488 | tf_op jit(solution)/shard_map/all_gather | solution.py:704
  211.8 6.2 fusion.70
  220.5 2.4 convolution_add_fusion
  222.9 4.2 convert_reduce_fusion
  227.1 2.6 convolution_convert_fusion
  229.7 1.9 fusion.59
  232.0 3.0 convolution_convert_fusion.1
  241.3 6.1 fusion.4
  247.6 2.1 fusion.7
  257.0 8.8 %collective-permute-done.17 = bf16[1,1,2,136,1152]{4,3,2,1,0:T(8,128)(2,1)S(1)} collective-permute-done((bf16[1,1,2,136,1152]{4,3,2,1,0:T(8,128)(2,1)S(1)}, bf16[1,1,2,136,1152]{4,3,2,1,0:T(8,128)(2,1)S(1)}, u32[]{:S(2)}, u32[]{:S(2)}) %collective-permute-start.17) | collective-permute-done | bytes 626720 | tf_op jit(solution)/shard_map/ppermute | solution.py:472
  267.5 1.9 collective-permute-done.20
  269.7 5.7 collective-permute-done.18
  280.5 4.4 reduce-scatter.5.cloned.1.call-done
  284.9 2.3 fusion.24
  287.2 3.2 convert_reduce_fusion.4
  292.3 1.9 iota_compare_fusion.11
  295.4 4.4 all-to-all-start.1
  301.5 2.5 constant_dynamic-slice_fusion.4
  304.1 2.3 copy.27
  306.4 2.0 pad.32
  316.4 9.7 %convolution_convert_fusion.3.other_ref.refs_1_ = bf16[1024,1152]{1,0:T(8,128)(2,1)} fusion(s32[1024]{0:T(1024)} %copy-done.49, f32[768,1152]{1,0:T(8,128)S(1)} %get-tuple-element.99, bf16[1088,1152]{1,0:T(8,128)(2,1)} %constant_dynamic-update-slice_fusion.5, f32[]{:T(128)S(6)} %convert.28, f32[1152]{0:T(1024)} %get-tuple-element.80, ...), kind=kOutput, calls=%fused_computation.12 | convolution fusion | flops 3751034880 | bytes 11756804 | tf_op jit(solution)/shard_map/cr,rd->cd/dot_general | solution.py:467
  326.2 4.7 all-to-all-done.1
  330.8 7.8 %momentum.1 = (f32[1076,1,1152]{2,1,0:T(1,128)}, bf16[1088,1152]{1,0:T(8,128)(2,1)S(1)}, bf16[1088,1152]{1,0:T(8,128)(2,1)S(1)}) custom-call(f32[1076,1,1152]{2,1,0:T(1,128)} %bitcast.170, bf16[1088,1152]{1,0:T(8,128)(2,1)} %bitcast.59.grad_ref), custom_call_target="tpu_custom_call" | custom-call | tf_op jit(solution)/shard_map/momentum/pallas_call | solution.py:110
  338.6 9.0 %gram.1.first_ref = f32[5760,128]{1,0:T(8,128)} custom-call(bf16[1088,1152]{1,0:T(8,128)(2,1)S(1)} %get-tuple-element.20.top_ref.refs_1_, bf16[1088,1152]{1,0:T(8,128)(2,1)S(1)} %get-tuple-element.21.rest_ref.refs_2_), custom_call_target="tpu_custom_call" | custom-call | tf_op jit(solution)/shard_map/gram/pallas_call | solution.py:169
  350.6 2.5 convolution_convert_fusion.6
  354.5 8.8 %attend_back.1 = bf16[3,4,80,768]{3,2,1,0:T(8,128)(2,1)S(1)} custom-call(bf16[3,4,80,768]{3,2,1,0:T(8,128)(2,1)S(1)} %bitcast.164, bf16[4,768,768]{2,1,0:T(8,128)(2,1)} %get-tuple-element.18.soft_ref, bf16[4,80,768]{2,1,0:T(8,128)(2,1)S(1)} %bitcast.168, f32[5760,128]{1,0:T(8,128)} %gram.1.first_ref, ...), custom_call_target="tpu_custom_call" | custom-call | tf_op jit(solution)/shard_map/attend_back/pallas_call | solution.py:425
  363.7 4.3 convolution_convert_fusion.4
  372.0 6.5 %fusion.56 = (f32[1152]{0:T(1024)S(1)}, f32[1152]{0:T(1024)S(1)}, bf16[768,1152]{1,0:T(8,128)(2,1)}) fusion(f32[768]{0:T(1024)S(1)} %copy-done.53, f32[768,1152]{1,0:T(8,128)} %copy-done.16, f32[768]{0:T(1024)S(1)} %copy-done.43, bf16[960,768]{1,0:T(8,128)(2,1)S(1)} %bitcast.166, bf16[320,1152]{1,0:T(8,128)(2,1)} %get-tuple-element.48, ...), kind=kOutput, calls=%fused_computation.226 | convolution fusion | flops 1710634752 | bytes 9010176 | tf_op jit(solution)/shard_map/er,ed->rd/dot_general | solution.py:467
  383.8 7.9 %collective-permute-done.23 = bf16[2,1,1,80,1152]{4,3,2,1,0:T(8,128)(2,1)S(1)} collective-permute-done((bf16[2,1,1,80,1152]{4,3,2,1,0:T(8,128)(2,1)S(1)}, bf16[2,1,1,80,1152]{4,3,2,1,0:T(8,128)(2,1)S(1)}, u32[]{:S(2)}, u32[]{:S(2)}) %collective-permute-start.23) | collective-permute-done | bytes 368672 | tf_op jit(solution)/shard_map/ppermute | solution.py:472
  393.8 10.1 %reduce-scatter.7.cloned.1.call-done = f32[1440,128]{1,0:T(8,128)} async-done(((f32[5760,128]{1,0:T(8,128)}), f32[1440,128]{1,0:T(8,128)}) %reduce-scatter.7.cloned.1.call-update) | async-done | bytes 737296 | tf_op jit(solution)/shard_map/reduce_scatter | solution.py:761
  405.6 4.7 collective-permute-done.27
  413.6 3.6 all-to-all-start.2
  418.2 5.2 convolution_convert_fusion.2.refs_3_.refs_0_
  423.4 5.9 all-to-all-done.2
  430.5 3.5 momentum_again.1
  437.7 3.7 collective-permute-done.29
  442.0 3.6 collective-permute-done.30
  446.8 8.2 %collective-permute-done.31 = f32[112,128]{1,0:T(8,128)S(1)} collective-permute-done((f32[112,128]{1,0:T(8,128)S(1)}, f32[112,128]{1,0:T(8,128)S(1)}, u32[]{:S(2)}, u32[]{:S(2)}) %collective-permute-start.31) | collective-permute-done | bytes 57376 | tf_op jit(solution)/shard_map/ppermute | solution.py:472
  455.1 2.0 slice.301.refs_0_
  457.1 6.6 %collective-permute-done.32 = f32[112,128]{1,0:T(8,128)S(1)} collective-permute-done((f32[112,128]{1,0:T(8,128)S(1)}, f32[112,128]{1,0:T(8,128)S(1)}, u32[]{:S(2)}, u32[]{:S(2)}) %collective-permute-start.32) | collective-permute-done | bytes 57376 | tf_op jit(solution)/shard_map/ppermute | solution.py:472
  463.7 4.2 all-gather.11.cloned.1.call-done.refs_1_.refs_3_.gram_ref
  467.9 1.8 copy-done.1
  469.8 54.3 %all-gather.13.cloned.1.call-done.refs_2_.full_hbm = bf16[1152,1152]{1,0:T(8,128)(2,1)} async-done(((bf16[288,1152]{1,0:T(8,128)(2,1)}), bf16[1152,1152]{1,0:T(8,128)(2,1)}) %all-gather.13.cloned.1.call-update) | async-done | bytes 2654224 | tf_op jit(solution)/shard_map/all_gather | solution.py:826
  530.5 95.6 %iterate.1 = f32[1076,1,1152]{2,1,0:T(1,128)} custom-call(s32[1]{0:T(128)} %bitcast.81.square_ref, f32[1]{0:T(128)} %bitcast.82.rate_ref, f32[5760,128]{1,0:T(8,128)} %all-gather.11.cloned.1.call-done.refs_1_.refs_3_.gram_ref, bf16[1152,1152]{1,0:T(8,128)(2,1)} %all-gather.13.cloned.1.call-done.refs_2_.full_hbm, ...), custom_call_target="tpu_custom_call" | custom-call | flops 80000000000 | bytes 20000000 | tf_op jit(solution)/shard_map/iterate/pallas_call | solution.py:361
  627.7 2.2 bitcast_convert_fusion.1
  (367 shorter events, 114.9 us)
Async XLA Ops:
  12.1 68.9 %all-to-all-start = ((bf16[8,136,1152]{2,1,0:T(8,128)(2,1)}), bf16[8,136,1152]{2,1,0:T(8,128)(2,1)}, u32[]{:S(2)}, u32[]{:S(2)}) async-start(bf16[8,136,1152]{2,1,0:T(8,128)(2,1)} %bitcast.22), calls=%async_computation | async-start | bytes 5013504 | tf_op jit(solution)/shard_map/all_to_all | solution.py:652
  17.4 120.0 %all-gather.15.cloned.1.call-start = ((), (), s32[]{:S(2)}) async-start(), calls=%async_computation.15 | async-start | bytes 6082560 | tf_op jit(solution)/shard_map/all_gather | solution.py:627
  20.9 190.9 %all-gather.7.cloned.1.call-start = ((), (), s32[]{:S(2)}) async-start(), calls=%async_computation.7 | async-start | bytes 2211840 | tf_op jit(solution)/shard_map/all_gather | solution.py:704
  24.5 40.4 %collective-permute-start.2 = (bf16[320,1152]{1,0:T(8,128)(2,1)S(1)}, bf16[320,1152]{1,0:T(8,128)(2,1)S(1)}, u32[]{:S(2)}, u32[]{:S(2)}) collective-permute-start(bf16[320,1152]{1,0:T(8,128)(2,1)S(1)} %prep_square.1), channel_id=1, source_target_pairs={{0,24},{4,28},{8,16},{12,20},{16,8},{20,12},{24,0},{28,4},{1,25},{... | collective-permute-start | bytes 2211848 | tf_op jit(solution)/shard_map/ppermute | solution.py:472
  27.6 51.5 %collective-permute-start.1 = (bf16[320,1152]{1,0:T(8,128)(2,1)S(1)}, bf16[320,1152]{1,0:T(8,128)(2,1)S(1)}, u32[]{:S(2)}, u32[]{:S(2)}) collective-permute-start(bf16[320,1152]{1,0:T(8,128)(2,1)S(1)} %prep_square.1), channel_id=1, source_target_pairs={{0,16},{4,20},{8,24},{12,28},{16,0},{20,4},{24,8},{28,12},{1,17},{... | collective-permute-start | bytes 2211848 | tf_op jit(solution)/shard_map/ppermute | solution.py:472
  28.1 51.0 %collective-permute-start = (bf16[320,1152]{1,0:T(8,128)(2,1)S(1)}, bf16[320,1152]{1,0:T(8,128)(2,1)S(1)}, u32[]{:S(2)}, u32[]{:S(2)}) collective-permute-start(bf16[320,1152]{1,0:T(8,128)(2,1)S(1)} %prep_square.1), channel_id=1, source_target_pairs={{0,8},{4,12},{8,0},{12,4},{16,24},{20,28},{24,16},{28,20},{1,9},{5... | collective-permute-start | bytes 2211848 | tf_op jit(solution)/shard_map/ppermute | solution.py:472
  81.0 38.3 %collective-permute-start.3 = (bf16[4,320,1152]{2,1,0:T(8,128)(2,1)}, bf16[4,320,1152]{2,1,0:T(8,128)(2,1)}, u32[]{:S(2)}, u32[]{:S(2)}) collective-permute-start(bf16[4,320,1152]{2,1,0:T(8,128)(2,1)} %pad_maximum_fusion), channel_id=1, source_target_pairs={{0,4},{4,0},{8,12},{12,8},{16,20},{20,16},{24,28},{28,24},{1,5},{5... | collective-permute-start | bytes 8847368 | tf_op jit(solution)/shard_map/ppermute | solution.py:472
  83.0 17.0 %collective-permute-start.11 = (bf16[272,1152]{1,0:T(8,128)(2,1)S(1)}, bf16[272,1152]{1,0:T(8,128)(2,1)S(1)}, u32[]{:S(2)}, u32[]{:S(2)}) collective-permute-start(bf16[272,1152]{1,0:T(8,128)(2,1)S(1)} %pad_maximum_fusion.7), channel_id=1, source_target_pairs={{0,8},{4,12},{8,0},{12,4},{16,24},{20,28},{24,16},{28,20},{1,9},{5... | collective-permute-start | bytes 1880072 | tf_op jit(solution)/shard_map/ppermute | solution.py:472
  85.0 29.6 %collective-permute-start.12 = (bf16[272,1152]{1,0:T(8,128)(2,1)S(1)}, bf16[272,1152]{1,0:T(8,128)(2,1)S(1)}, u32[]{:S(2)}, u32[]{:S(2)}) collective-permute-start(bf16[272,1152]{1,0:T(8,128)(2,1)S(1)} %pad_maximum_fusion.7), channel_id=1, source_target_pairs={{0,16},{4,20},{8,24},{12,28},{16,0},{20,4},{24,8},{28,12},{1,17},{... | collective-permute-start | bytes 1880072 | tf_op jit(solution)/shard_map/ppermute | solution.py:472
  85.6 60.6 %copy-start.49 = (s32[1024]{0:T(1024)}, s32[1024]{0:T(1024)S(1)}, u32[]{:S(2)}) copy-start(s32[1024]{0:T(1024)S(1)} %add_select_fusion.4) | copy-start | bytes 12292
  89.2 26.3 %collective-permute-start.13 = (bf16[272,1152]{1,0:T(8,128)(2,1)S(1)}, bf16[272,1152]{1,0:T(8,128)(2,1)S(1)}, u32[]{:S(2)}, u32[]{:S(2)}) collective-permute-start(bf16[272,1152]{1,0:T(8,128)(2,1)S(1)} %pad_maximum_fusion.7), channel_id=1, source_target_pairs={{0,24},{4,28},{8,16},{12,20},{16,8},{20,12},{24,0},{28,4},{1,25},{... | collective-permute-start | bytes 1880072 | tf_op jit(solution)/shard_map/ppermute | solution.py:472
  117.6 60.9 %collective-permute-start.15 = (bf16[544,1152]{1,0:T(8,128)(2,1)}, bf16[544,1152]{1,0:T(8,128)(2,1)}, u32[]{:S(2)}, u32[]{:S(2)}) collective-permute-start(bf16[544,1152]{1,0:T(8,128)(2,1)} %pad_maximum_fusion.3), channel_id=1, source_target_pairs={{0,4},{4,0},{8,12},{12,8},{16,20},{20,16},{24,28},{28,24},{1,5},{5... | collective-permute-start | bytes 3760136 | tf_op jit(solution)/shard_map/ppermute | solution.py:472
  118.7 62.2 %collective-permute-start.14 = (bf16[544,1152]{1,0:T(8,128)(2,1)}, bf16[544,1152]{1,0:T(8,128)(2,1)}, u32[]{:S(2)}, u32[]{:S(2)}) collective-permute-start(bf16[544,1152]{1,0:T(8,128)(2,1)} %pad_maximum_fusion.2), channel_id=1, source_target_pairs={{0,4},{4,0},{8,12},{12,8},{16,20},{20,16},{24,28},{28,24},{1,5},{5... | collective-permute-start | bytes 3760136 | tf_op jit(solution)/shard_map/ppermute | solution.py:472
  120.2 12.8 %collective-permute-start.6 = (bf16[40,1152]{1,0:T(8,128)(2,1)S(1)}, bf16[40,1152]{1,0:T(8,128)(2,1)S(1)}, u32[]{:S(2)}, u32[]{:S(2)}) collective-permute-start(bf16[40,1152]{1,0:T(8,128)(2,1)S(1)} %get-tuple-element.50), channel_id=1, source_target_pairs={{0,3},{1,0},{2,1},{3,2},{4,7},{5,4},{6,5},{7,6},{8,11},{9,8},{10,9... | collective-permute-start | bytes 276488 | tf_op jit(solution)/shard_map/ppermute | solution.py:507
  124.5 8.6 %collective-permute-start.5 = (bf16[40,1152]{1,0:T(8,128)(2,1)S(1)}, bf16[40,1152]{1,0:T(8,128)(2,1)S(1)}, u32[]{:S(2)}, u32[]{:S(2)}) collective-permute-start(bf16[40,1152]{1,0:T(8,128)(2,1)S(1)} %get-tuple-element.50), channel_id=1, source_target_pairs={{0,2},{1,3},{2,0},{3,1},{4,6},{5,7},{6,4},{7,5},{8,10},{9,11},{10,... | collective-permute-start | bytes 276488 | tf_op jit(solution)/shard_map/ppermute | solution.py:507
  124.5 7.0 %collective-permute-start.4 = (bf16[40,1152]{1,0:T(8,128)(2,1)S(1)}, bf16[40,1152]{1,0:T(8,128)(2,1)S(1)}, u32[]{:S(2)}, u32[]{:S(2)}) collective-permute-start(bf16[40,1152]{1,0:T(8,128)(2,1)S(1)} %get-tuple-element.50), channel_id=1, source_target_pairs={{0,1},{1,2},{2,3},{3,0},{4,5},{5,6},{6,7},{7,4},{8,9},{9,10},{10,1... | collective-permute-start | bytes 276488 | tf_op jit(solution)/shard_map/ppermute | solution.py:507
  133.6 41.4 %collective-permute-start.9 = (bf16[160,1152]{1,0:T(8,128)(2,1)S(1)}, bf16[160,1152]{1,0:T(8,128)(2,1)}, u32[]{:S(2)}, u32[]{:S(2)}) collective-permute-start(bf16[160,1152]{1,0:T(8,128)(2,1)S(1)} %bitcast.198), channel_id=1, source_target_pairs={{0,24},{4,28},{8,16},{12,20},{16,8},{20,12},{24,0},{28,4},{1,25},{... | collective-permute-start | bytes 1105928 | tf_op jit(solution)/shard_map/ppermute | solution.py:472
  135.2 38.7 %collective-permute-start.8 = (bf16[160,1152]{1,0:T(8,128)(2,1)S(1)}, bf16[160,1152]{1,0:T(8,128)(2,1)}, u32[]{:S(2)}, u32[]{:S(2)}) collective-permute-start(bf16[160,1152]{1,0:T(8,128)(2,1)S(1)} %bitcast.199), channel_id=1, source_target_pairs={{0,16},{4,20},{8,24},{12,28},{16,0},{20,4},{24,8},{28,12},{1,17},{... | collective-permute-start | bytes 1105928 | tf_op jit(solution)/shard_map/ppermute | solution.py:472
  135.7 37.1 %collective-permute-start.7 = (bf16[160,1152]{1,0:T(8,128)(2,1)S(1)}, bf16[160,1152]{1,0:T(8,128)(2,1)}, u32[]{:S(2)}, u32[]{:S(2)}) collective-permute-start(bf16[160,1152]{1,0:T(8,128)(2,1)S(1)} %bitcast.200), channel_id=1, source_target_pairs={{0,8},{4,12},{8,0},{12,4},{16,24},{20,28},{24,16},{28,20},{1,9},{5... | collective-permute-start | bytes 1105928 | tf_op jit(solution)/shard_map/ppermute | solution.py:472
  145.7 12.4 %copy-start.45 = (f32[1152]{0:T(1024)}, f32[1152]{0:T(1024)S(1)}, u32[]{:S(2)}) copy-start(f32[1152]{0:T(1024)S(1)} %get-tuple-element.86) | copy-start | bytes 13828
  154.5 8.5 %copy-start.42 = (f32[768]{0:T(1024)}, f32[768]{0:T(1024)S(1)}, u32[]{:S(2)}) copy-start(f32[768]{0:T(1024)S(1)} %broadcast_multiply_fusion.1) | copy-start | bytes 9220
  172.4 112.5 %reduce-scatter.5.cloned.1.call-start = ((), (), s32[]{:S(2)}) async-start(), calls=%async_computation.8 | async-start | bytes 2211840 | tf_op jit(solution)/shard_map/reduce_scatter | solution.py:735
  177.4 8.0 %collective-permute-start.10 = (bf16[4,1,160,1152]{3,2,1,0:T(8,128)(2,1)}, bf16[4,1,160,1152]{3,2,1,0:T(8,128)(2,1)}, u32[]{:S(2)}, u32[]{:S(2)}) collective-permute-start(bf16[4,1,160,1152]{3,2,1,0:T(8,128)(2,1)} %constant_dynamic-slice_fusion.5), channel_id=1, source_target_pairs={{0,4},{4,0},{8,12},{12,8},{16,20},{20,16},{24,28},{28,24},{1,5},{5... | collective-permute-start | bytes 4423688 | tf_op jit(solution)/shard_map/ppermute | solution.py:472
  219.0 8.1 %copy-start.10 = (f32[768,1152]{1,0:T(8,128)}, f32[768,1152]{1,0:T(8,128)S(1)}, u32[]{:S(2)}) copy-start(f32[768,1152]{1,0:T(8,128)S(1)} %subtract_multiply_fusion) | copy-start | bytes 10616836
  222.9 9.0 %copy-start.62 = (f32[768,1088]{0,1:T(8,128)}, f32[768,1088]{0,1:T(8,128)S(1)}, u32[]{:S(2)}) copy-start(f32[768,1088]{0,1:T(8,128)S(1)} %convolution_add_fusion) | copy-start | bytes 10027012
  232.0 15.6 %collective-permute-start.16 = (bf16[1,2,2,136,1152]{4,3,2,1,0:T(8,128)(2,1)}, bf16[1,2,2,136,1152]{4,3,2,1,0:T(8,128)(2,1)}, u32[]{:S(2)}, u32[]{:S(2)}) collective-permute-start(bf16[1,2,2,136,1152]{4,3,2,1,0:T(8,128)(2,1)} %bitcast.50), channel_id=1, source_target_pairs={{0,4},{4,0},{8,12},{12,8},{16,20},{20,16},{24,28},{28,24},{1,5},{5... | collective-permute-start | bytes 3760136 | tf_op jit(solution)/shard_map/ppermute | solution.py:472
  237.2 14.0 %collective-permute-start.19 = (bf16[1,2,2,136,1152]{4,3,2,1,0:T(8,128)(2,1)}, bf16[1,2,2,136,1152]{4,3,2,1,0:T(8,128)(2,1)}, u32[]{:S(2)}, u32[]{:S(2)}) collective-permute-start(bf16[1,2,2,136,1152]{4,3,2,1,0:T(8,128)(2,1)} %bitcast.53), channel_id=1, source_target_pairs={{0,4},{4,0},{8,12},{12,8},{16,20},{20,16},{24,28},{28,24},{1,5},{5... | collective-permute-start | bytes 3760136 | tf_op jit(solution)/shard_map/ppermute | solution.py:472
  247.5 101.7 %all-gather.9.cloned.1.call-start = ((), (), s32[]{:S(2)}) async-start(), calls=%async_computation.9 | async-start | bytes 2211840 | tf_op jit(solution)/shard_map/all_gather | solution.py:750
  249.7 16.1 %collective-permute-start.17 = (bf16[1,1,2,136,1152]{4,3,2,1,0:T(8,128)(2,1)S(1)}, bf16[1,1,2,136,1152]{4,3,2,1,0:T(8,128)(2,1)S(1)}, u32[]{:S(2)}, u32[]{:S(2)}) collective-permute-start(bf16[1,1,2,136,1152]{4,3,2,1,0:T(8,128)(2,1)S(1)} %slice.340), channel_id=1, source_target_pairs={{0,16},{4,20},{8,24},{12,28},{16,0},{20,4},{24,8},{28,12},{1,17},{... | collective-permute-start | bytes 1880072 | tf_op jit(solution)/shard_map/ppermute | solution.py:472
  252.9 16.5 %collective-permute-start.20 = (bf16[1,2,1,136,1152]{4,3,2,1,0:T(8,128)(2,1)S(1)}, bf16[1,2,1,136,1152]{4,3,2,1,0:T(8,128)(2,1)S(1)}, u32[]{:S(2)}, u32[]{:S(2)}) collective-permute-start(bf16[1,2,1,136,1152]{4,3,2,1,0:T(8,128)(2,1)S(1)} %slice.346), channel_id=1, source_target_pairs={{0,8},{4,12},{8,0},{12,4},{16,24},{20,28},{24,16},{28,20},{1,9},{5... | collective-permute-start | bytes 1880072 | tf_op jit(solution)/shard_map/ppermute | solution.py:472
  266.0 9.4 %collective-permute-start.18 = (bf16[1,1,1,136,1152]{4,3,2,1,0:T(8,128)(2,1)S(1)}, bf16[1,1,1,136,1152]{4,3,2,1,0:T(8,128)(2,1)S(1)}, u32[]{:S(2)}, u32[]{:S(2)}) collective-permute-start(bf16[1,1,1,136,1152]{4,3,2,1,0:T(8,128)(2,1)S(1)} %slice.342), channel_id=1, source_target_pairs={{0,8},{4,12},{8,0},{12,4},{16,24},{20,28},{24,16},{28,20},{1,9},{5... | collective-permute-start | bytes 940040 | tf_op jit(solution)/shard_map/ppermute | solution.py:472
  269.6 7.5 %collective-permute-start.21 = (bf16[1,1,1,136,1152]{4,3,2,1,0:T(8,128)(2,1)S(1)}, bf16[1,1,1,136,1152]{4,3,2,1,0:T(8,128)(2,1)S(1)}, u32[]{:S(2)}, u32[]{:S(2)}) collective-permute-start(bf16[1,1,1,136,1152]{4,3,2,1,0:T(8,128)(2,1)S(1)} %slice.348), channel_id=1, source_target_pairs={{0,16},{4,20},{8,24},{12,28},{16,0},{20,4},{24,8},{28,12},{1,17},{... | collective-permute-start | bytes 940040 | tf_op jit(solution)/shard_map/ppermute | solution.py:472
  295.4 35.5 %all-to-all-start.1 = ((bf16[8,136,1152]{2,1,0:T(8,128)(2,1)}), bf16[8,136,1152]{2,1,0:T(8,128)(2,1)}, u32[]{:S(2)}, u32[]{:S(2)}) async-start(bf16[8,136,1152]{2,1,0:T(8,128)(2,1)} %copy-done.9), calls=%async_computation.2 | async-start | bytes 5013504 | tf_op jit(solution)/shard_map/all_to_all | solution.py:652
  299.8 104.2 %reduce-scatter.7.cloned.1.call-start = ((), (), s32[]{:S(2)}) async-start(), calls=%async_computation.10 | async-start | bytes 3686400 | tf_op jit(solution)/shard_map/reduce_scatter | solution.py:761
  338.6 9.0 %copy-start = (bf16[1088,1152]{1,0:T(8,128)(2,1)}, bf16[1088,1152]{1,0:T(8,128)(2,1)S(1)}, u32[]{:S(2)}) copy-start(bf16[1088,1152]{1,0:T(8,128)(2,1)S(1)} %get-tuple-element.20.top_ref.refs_1_) | copy-start | bytes 7520260
  349.1 118.8 %all-gather.11.cloned.1.call-start = ((), (), s32[]{:S(2)}) async-start(), calls=%async_computation.11 | async-start | bytes 3686400 | tf_op jit(solution)/shard_map/all_gather | solution.py:762
  354.5 9.3 %copy-start.43 = (f32[768]{0:T(1024)S(1)}, f32[768]{0:T(1024)}, u32[]{:S(2)}) copy-start(f32[768]{0:T(1024)} %copy-done.42) | copy-start | bytes 9220
  354.5 9.3 %copy-start.46 = (f32[1152]{0:T(1024)S(1)}, f32[1152]{0:T(1024)}, u32[]{:S(2)}) copy-start(f32[1152]{0:T(1024)} %copy-done.45) | copy-start | bytes 13828
  354.5 9.3 %copy-start.53 = (f32[768]{0:T(1024)S(1)}, f32[768]{0:T(1024)}, u32[]{:S(2)}) copy-start(f32[768]{0:T(1024)} %copy-done.52) | copy-start | bytes 9220
  370.0 9.3 %collective-permute-start.22 = (bf16[2,2,1,80,1152]{4,3,2,1,0:T(8,128)(2,1)}, bf16[2,2,1,80,1152]{4,3,2,1,0:T(8,128)(2,1)}, u32[]{:S(2)}, u32[]{:S(2)}) collective-permute-start(bf16[2,2,1,80,1152]{4,3,2,1,0:T(8,128)(2,1)} %fusion.28), channel_id=1, source_target_pairs={{0,4},{4,0},{8,12},{12,8},{16,20},{20,16},{24,28},{28,24},{1,5},{5... | collective-permute-start | bytes 2211848 | tf_op jit(solution)/shard_map/ppermute | solution.py:472
  371.0 11.0 %collective-permute-start.25 = (bf16[2,2,1,80,1152]{4,3,2,1,0:T(8,128)(2,1)}, bf16[2,2,1,80,1152]{4,3,2,1,0:T(8,128)(2,1)}, u32[]{:S(2)}, u32[]{:S(2)}) collective-permute-start(bf16[2,2,1,80,1152]{4,3,2,1,0:T(8,128)(2,1)} %fusion.26), channel_id=1, source_target_pairs={{0,4},{4,0},{8,12},{12,8},{16,20},{20,16},{24,28},{28,24},{1,5},{5... | collective-permute-start | bytes 2211848 | tf_op jit(solution)/shard_map/ppermute | solution.py:472
  381.2 10.6 %collective-permute-start.23 = (bf16[2,1,1,80,1152]{4,3,2,1,0:T(8,128)(2,1)S(1)}, bf16[2,1,1,80,1152]{4,3,2,1,0:T(8,128)(2,1)S(1)}, u32[]{:S(2)}, u32[]{:S(2)}) collective-permute-start(bf16[2,1,1,80,1152]{4,3,2,1,0:T(8,128)(2,1)S(1)} %constant_dynamic-slice_fusion.3), channel_id=1, source_target_pairs={{0,8},{4,12},{8,0},{12,4},{16,24},{20,28},{24,16},{28,20},{1,9},{5... | collective-permute-start | bytes 1105928 | tf_op jit(solution)/shard_map/ppermute | solution.py:472
  383.3 28.9 %copy-start.56 = (pred[8]{0:T(512)(128)(4,1)S(1)}, pred[8]{0:T(512)(128)(4,1)}, u32[]{:S(2)}) copy-start(pred[8]{0:T(512)(128)(4,1)} %get-tuple-element.111) | copy-start | bytes 28
  383.4 28.9 %copy-start.57 = (pred[8]{0:T(512)(128)(4,1)S(1)}, pred[8]{0:T(512)(128)(4,1)}, u32[]{:S(2)}) copy-start(pred[8]{0:T(512)(128)(4,1)} %get-tuple-element.112) | copy-start | bytes 28
  383.4 28.9 %copy-start.58 = (pred[8]{0:T(512)(128)(4,1)S(1)}, pred[8]{0:T(512)(128)(4,1)}, u32[]{:S(2)}) copy-start(pred[8]{0:T(512)(128)(4,1)} %get-tuple-element.109) | copy-start | bytes 28
  383.4 28.9 %copy-start.59 = (pred[8]{0:T(512)(128)(4,1)S(1)}, pred[8]{0:T(512)(128)(4,1)}, u32[]{:S(2)}) copy-start(pred[8]{0:T(512)(128)(4,1)} %get-tuple-element.110) | copy-start | bytes 28
  383.4 10.3 %collective-permute-start.26 = (bf16[1,2,1,80,1152]{4,3,2,1,0:T(8,128)(2,1)S(1)}, bf16[1,2,1,80,1152]{4,3,2,1,0:T(8,128)(2,1)S(1)}, u32[]{:S(2)}, u32[]{:S(2)}) collective-permute-start(bf16[1,2,1,80,1152]{4,3,2,1,0:T(8,128)(2,1)S(1)} %constant_dynamic-slice_fusion.1), channel_id=1, source_target_pairs={{0,16},{4,20},{8,24},{12,28},{16,0},{20,4},{24,8},{28,12},{1,17},{... | collective-permute-start | bytes 1105928 | tf_op jit(solution)/shard_map/ppermute | solution.py:472
  391.9 13.7 %collective-permute-start.24 = (bf16[1,1,1,80,1152]{4,3,2,1,0:T(8,128)(2,1)S(1)}, bf16[1,1,1,80,1152]{4,3,2,1,0:T(8,128)(2,1)S(1)}, u32[]{:S(2)}, u32[]{:S(2)}) collective-permute-start(bf16[1,1,1,80,1152]{4,3,2,1,0:T(8,128)(2,1)S(1)} %constant_dynamic-slice_fusion.2), channel_id=1, source_target_pairs={{0,16},{4,20},{8,24},{12,28},{16,0},{20,4},{24,8},{28,12},{1,17},{... | collective-permute-start | bytes 552968 | tf_op jit(solution)/shard_map/ppermute | solution.py:472
  404.0 13.4 %copy-start.34 = (f32[1152]{0:T(1024)S(1)}, f32[1152]{0:T(1024)}, u32[]{:S(2)}) copy-start(f32[1152]{0:T(1024)} %get-tuple-element.61) | copy-start | bytes 13828
  404.0 14.2 %copy-start.50 = (s32[1024]{0:T(1024)S(1)}, s32[1024]{0:T(1024)}, u32[]{:S(2)}) copy-start(s32[1024]{0:T(1024)} %copy-done.49) | copy-start | bytes 12292
  404.0 6.3 collective-permute-start.27
  413.6 15.7 %all-to-all-start.2 = ((bf16[8,40,1152]{2,1,0:T(8,128)(2,1)}), bf16[8,40,1152]{2,1,0:T(8,128)(2,1)S(1)}, u32[]{:S(2)}, u32[]{:S(2)}) async-start(bf16[8,40,1152]{2,1,0:T(8,128)(2,1)} %add_add_fusion), calls=%async_computation.4 | async-start | bytes 1474560 | tf_op jit(solution)/shard_map/all_to_all | solution.py:652
  417.2 106.9 %all-gather.13.cloned.1.call-start = ((), (), s32[]{:S(2)}) async-start(), calls=%async_computation.12 | async-start | bytes 3317760 | tf_op jit(solution)/shard_map/all_gather | solution.py:826
  435.8 1.3 collective-permute-start.28
  437.1 4.2 collective-permute-start.29
  441.4 4.2 collective-permute-start.30
  445.6 9.4 %collective-permute-start.31 = (f32[112,128]{1,0:T(8,128)S(1)}, f32[112,128]{1,0:T(8,128)S(1)}, u32[]{:S(2)}, u32[]{:S(2)}) collective-permute-start(f32[112,128]{1,0:T(8,128)S(1)} %add.589), channel_id=1, source_target_pairs={{0,1},{1,0},{2,3},{3,2},{4,5},{5,4},{6,7},{7,6},{8,9},{9,8},{10,11... | collective-permute-start | bytes 172040 | tf_op jit(solution)/shard_map/ppermute | solution.py:472
  455.1 8.7 %collective-permute-start.32 = (f32[112,128]{1,0:T(8,128)S(1)}, f32[112,128]{1,0:T(8,128)S(1)}, u32[]{:S(2)}, u32[]{:S(2)}) collective-permute-start(f32[112,128]{1,0:T(8,128)S(1)} %add.590), channel_id=1, source_target_pairs={{0,2},{1,3},{2,0},{3,1},{4,6},{5,7},{6,4},{7,5},{8,10},{9,11},{10,... | collective-permute-start | bytes 172040 | tf_op jit(solution)/shard_map/ppermute | solution.py:472
  463.7 66.1 %copy-start.6 = (f32[112,128]{1,0:T(8,128)}, f32[112,128]{1,0:T(8,128)S(1)}, u32[]{:S(2)}) copy-start(f32[112,128]{1,0:T(8,128)S(1)} %add.591.refs_2_.first_ref) | copy-start | bytes 172036
  469.7 58.3 %copy-start.41 = (s32[6]{0:T(128)S(1)}, s32[6]{0:T(128)}, u32[]{:S(2)}) copy-start(s32[6]{0:T(128)} %param.13) | copy-start | bytes 76
  469.8 59.6 %copy-start.38 = (f32[2,3380]{1,0:T(2,128)S(1)}, f32[2,3380]{1,0:T(2,128)}, u32[]{:S(2)}) copy-start(f32[2,3380]{1,0:T(2,128)} %param.17) | copy-start | bytes 81124
  469.8 59.7 %copy-start.51 = (f32[256]{0:T(256)S(1)}, f32[256]{0:T(256)}, u32[]{:S(2)}) copy-start(f32[256]{0:T(256)} %get-tuple-element.62) | copy-start | bytes 3076
  469.8 156.4 %reduce-scatter.11.cloned.1.call-start = ((), (), s32[]{:S(2)}) async-start(), calls=%async_computation.14 | async-start | bytes 2949120 | tf_op jit(solution)/shard_map/reduce_scatter | solution.py:837
  524.2 103.5 %reduce-scatter.9.cloned.1.call-start = ((), (), s32[]{:S(2)}) async-start(), calls=%async_computation.13 | async-start | bytes 2949120 | tf_op jit(solution)/shard_map/reduce_scatter | solution.py:840
  (45 other events, 155.9 us)
Sparse Core Ops, SparseCore 0:
  21.0 94.1 all-gather.14
  172.5 39.2 all-gather.6
  247.6 37.2 reduce-scatter.4
  290.5 39.4 all-gather.8
  349.2 54.6 reduce-scatter.6
  405.4 62.4 all-gather.10
  470.0 54.0 all-gather.12
  526.4 46.7 reduce-scatter.10
  575.6 47.5 reduce-scatter.8

commit v4 on v3

--- a/solution.py
+++ b/solution.py
@@ -625,26 +625,23 @@
     cot_own = (cotangent[0] * own_valid).astype(low)
     payload = jnp.concatenate([rows_in.astype(low), payload.astype(low), cot_own], axis=0)
     gathered = lax.all_gather(payload, "seq", axis=0, tiled=False)
-    token_slots = gathered[:, : capacity + extra].reshape(seq_count * (capacity + extra), width)
-    cot_slots = gathered[:, capacity + extra :].reshape(slots, width)
 
     counts_row = counts[0]
     starts = jnp.cumsum(counts_row) - counts_row
 
-    def rows_of(per):
-        ids = jnp.arange(per * seq_count)
-        real = (ids % per) < jnp.repeat(counts_row, per)
-        return jnp.where(real, jnp.repeat(starts, per) + ids % per, packed)
+    def rows_of(per, skip=0):
+        ids = jnp.arange(per * seq_count) % per - skip
+        real = (ids >= 0) & (ids < jnp.repeat(counts_row, per))
+        return jnp.where(real, jnp.repeat(starts, per) + ids, packed)
 
     def picks(row):
         return (jnp.arange(packed)[:, None] == row[None, :]).astype(low)
 
     slot_row = rows_of(capacity)
-    token_pick = picks(rows_of(capacity + extra))
+    token_pick = picks(rows_of(payload.shape[0]))
+    cot_pick = picks(rows_of(payload.shape[0], capacity + extra))
     own_row = lax.dynamic_slice_in_dim(slot_row, seq_index * capacity, capacity)
     own_pick = picks(own_row)
-    grad_rows = product("rc,cd->rd", picks(slot_row), cot_slots).astype(low)
-
     slab = jnp.transpose(owned_weights[0], (2, 1, 0))
     moments = jnp.transpose(owned_moments[0], (2, 1, 0))
 
@@ -669,6 +666,9 @@
     wide_pieces = [lax.dynamic_index_in_dim(got_wide, owner_table[m], 0, keepdims=False) for m in (4, 5)]
 
     w_up, w_down = gather_relative(wide_pieces)
+    (gathered,) = touch([gathered], w_up, w_down, w_out_part)
+    gathered_rows = gathered.reshape(seq_count * payload.shape[0], width)
+    grad_rows = product("rc,cd->rd", cot_pick, gathered_rows).astype(low)
 
     vector_full = gathered[:, capacity : capacity + vector_rows].reshape(seq_count, -1)
     vector_full = vector_full[:, :vector_count].reshape(-1).astype(f32)
@@ -685,10 +685,10 @@
         [head_bias(row_params[2]), jnp.zeros((square_rows,), f32), head_bias(row_params[3])]
     )
 
-    token_rows = product("rc,cd->rd", token_pick, token_slots)
+    token_rows = product("rc,cd->rd", token_pick, gathered_rows)
     hat_packed = whiten(token_rows)[0]
     normed = (hat_packed * row_params[0] + row_params[1]).astype(low)
-    qkv_bias = after(qkv_bias, w_up[0, 0] + w_down[0, 0] + grad_rows[0, 0] + w_out_part[0, 0])
+    qkv_bias = after(qkv_bias, grad_rows[0, 0])
     qkv = (product("ed,rd->er", w_qkv, normed) + qkv_bias[:, None]).astype(low)
     qkv = qkv.reshape(3, heads, head_pad, packed)
     context_own, soft = attend(qkv, head_size, score_scale)

time: 644 us -> 641 us (level)
  local copies, waits for them, and re-layouts: 74.2 us -> 60.8 us
  waiting for transfers between devices: 233 us -> 246 us
    slice x7 -> x1, local copies, waits for them, and re-layouts: 9.61 us -> 0.51 us  [local(): qkv_bias = after(qkv_bias, grad_rows[0, 0])]
    all_to_all x3, waiting for transfers between devices: 10.5 us -> 18.4 us  [send(): return lax.all_to_all(x, 'dp', split_axis=0, concat_axis=0, tiled=True)]
    unnamed x143 -> x106, local copies, waits for them, and re-layouts: 21.2 us -> 23.4 us
  transfers between devices with their start and end apart: 45 -> 45, of which waited for: 26 -> 27; matrix products, arithmetic and copies ran while one was open for 23% -> 21% of each run, Pallas kernels for 21% -> 21%
where the time goes in v4:
time: 641 us; the launch traced here: 636 us
  waiting for transfers between devices  246 us (38%)
  Pallas kernels  138 us (22%)
  matrix products  71.3 us (11%)
  local copies, waits for them, and re-layouts  60.8 us (9%)
  other arithmetic  46.1 us (7%)
  starting transfers between devices  42 us (7%)
  between operations  31.5 us (5%)
    ppermute x30, waiting for transfers between devices, flip(): return lax.ppermute(x, axis, [(i, i ^ mask) for i in range(count)])  128 us
    pallas_call x1, Pallas kernels, iterate(): call(functools.partial(iterate_body, total), 'iterate', vmem=56, in_specs...  95.6 us
    dot_general x16, matrix products, product(): return jnp.einsum(form, left, right, preferred_element_type=f32)  71.3 us
    all_gather x1, waiting for transfers between devices, local(): direction = lax.all_gather(direction, 'seq', axis=0, tiled=True)  54.3 us
    unnamed x106, local copies, waits for them, and re-layouts  23.4 us
    ppermute x30, starting transfers between devices, flip(): return lax.ppermute(x, axis, [(i, i ^ mask) for i in range(count)])  22.7 us
    all_gather x1, waiting for transfers between devices, local(): lax.all_gather(context_own.reshape(cols, packed), 'seq', axis=0, tiled=True)  22.1 us
    all_to_all x3, waiting for transfers between devices, send(): return lax.all_to_all(x, 'dp', split_axis=0, concat_axis=0, tiled=True)  18.4 us
  transfers between devices with their start and end apart: 45, of which 27 were waited for; matrix products, arithmetic and copies ran while one was open for 21% of the time, Pallas kernels for 21%

profile of v4, /device:TPU:0, one launch (start us, length us, event | category | flops | bytes accessed | tf_op | source)
XLA Modules:
  0.0 635.8 jit_solution(4309472829074178999)
XLA Ops:
  7.2 4.9 prep_wide.1
  12.0 5.3 all-to-all-start
  23.4 2.2 prep_square.1
  25.6 3.2 collective-permute-start.2
  33.7 31.1 %collective-permute-done.2 = bf16[320,1152]{1,0:T(8,128)(2,1)S(1)} collective-permute-done((bf16[320,1152]{1,0:T(8,128)(2,1)S(1)}, bf16[320,1152]{1,0:T(8,128)(2,1)S(1)}, u32[]{:S(2)}, u32[]{:S(2)}) %collective-permute-start.2) | collective-permute-done | bytes 737312 | tf_op jit(solution)/shard_map/ppermute | solution.py:472
  64.8 14.2 %collective-permute-done.1 = bf16[320,1152]{1,0:T(8,128)(2,1)S(1)} collective-permute-done((bf16[320,1152]{1,0:T(8,128)(2,1)S(1)}, bf16[320,1152]{1,0:T(8,128)(2,1)S(1)}, u32[]{:S(2)}, u32[]{:S(2)}) %collective-permute-start.1) | collective-permute-done | bytes 737312 | tf_op jit(solution)/shard_map/ppermute | solution.py:472
  79.1 1.8 pad_maximum_fusion
  81.0 1.9 constant_dynamic-update-slice_fusion.9
  90.5 10.4 %collective-permute-done.4 = bf16[272,1152]{1,0:T(8,128)(2,1)} collective-permute-done((bf16[272,1152]{1,0:T(8,128)(2,1)}, bf16[272,1152]{1,0:T(8,128)(2,1)}, u32[]{:S(2)}, u32[]{:S(2)}) %collective-permute-start.4) | collective-permute-done | bytes 626720 | tf_op jit(solution)/shard_map/ppermute | solution.py:472
  100.9 1.9 fusion.73
  102.8 12.8 %collective-permute-done.5 = bf16[272,1152]{1,0:T(8,128)(2,1)} collective-permute-done((bf16[272,1152]{1,0:T(8,128)(2,1)}, bf16[272,1152]{1,0:T(8,128)(2,1)}, u32[]{:S(2)}, u32[]{:S(2)}) %collective-permute-start.5) | collective-permute-done | bytes 626720 | tf_op jit(solution)/shard_map/ppermute | solution.py:472
  115.6 1.9 fusion.74
  120.1 4.3 collective-permute-start.11
  125.6 3.7 select_bitcast_fusion.2
  129.3 2.2 collective-permute-done.9
  142.8 7.2 %fusion.5 = bf16[768,1152]{1,0:T(8,128)(2,1)S(1)} fusion(bf16[2112,1152]{1,0:T(8,128)(2,1)} %bitcast.195, s32[2112]{0:T(1024)S(1)} %get-tuple-element.89), kind=kOutput, calls=%fused_computation.24 | convolution fusion | flops 3739631616 | bytes 6643968 | tf_op jit(solution)/shard_map/rc,cd->rd/dot_general | solution.py:467
  152.4 7.3 %fusion.79 = (f32[768]{0:T(1024)S(1)}, f32[768,1152]{1,0:T(8,128)S(1)}) fusion(bf16[2112,1152]{1,0:T(8,128)(2,1)} %bitcast.196, s32[2112]{0:T(1024)S(1)} %get-tuple-element.88), kind=kOutput, calls=%fused_computation.248 | convolution fusion | flops 3739630848 | bytes 8416512 | tf_op jit(solution)/shard_map/rc,cd->rd/dot_general | solution.py:467
  162.6 2.2 add_convert_fusion.2
  164.8 6.5 %attend.1 = (bf16[4,72,768]{2,1,0:T(8,128)(2,1)}, bf16[4,768,768]{2,1,0:T(8,128)(2,1)}) custom-call(bf16[3,4,80,768]{3,2,1,0:T(8,128)(2,1)S(1)} %bitcast.164), custom_call_target="tpu_custom_call" | custom-call | tf_op jit(solution)/shard_map/attend/pallas_call | solution.py:394
  178.7 2.7 constant_dynamic-slice_fusion.5
  182.5 2.6 collective-permute-done.15
  185.1 2.6 constant_dynamic-update-slice_fusion.11
  187.7 2.1 copy.23
  191.6 22.1 %all-gather.7.cloned.1.call-done = bf16[1152,768]{1,0:T(8,128)(2,1)} async-done(((bf16[288,768]{1,0:T(8,128)(2,1)}), bf16[1152,768]{1,0:T(8,128)(2,1)}) %all-gather.7.cloned.1.call-update) | async-done | bytes 1769488 | tf_op jit(solution)/shard_map/all_gather | solution.py:704
  213.6 6.1 fusion.80
  221.5 1.8 copy-done.9
  223.4 2.4 convolution_add_fusion
  225.8 3.6 convert_reduce_fusion
  229.4 3.2 convolution_convert_fusion.1
  232.6 2.4 convolution_convert_fusion
  243.4 6.1 fusion.6
  249.6 2.1 fusion.11
  257.7 10.1 %collective-permute-done.17 = bf16[1,1,2,136,1152]{4,3,2,1,0:T(8,128)(2,1)S(1)} collective-permute-done((bf16[1,1,2,136,1152]{4,3,2,1,0:T(8,128)(2,1)S(1)}, bf16[1,1,2,136,1152]{4,3,2,1,0:T(8,128)(2,1)S(1)}, u32[]{:S(2)}, u32[]{:S(2)}) %collective-permute-start.17) | collective-permute-done | bytes 626720 | tf_op jit(solution)/shard_map/ppermute | solution.py:472
  269.5 1.9 collective-permute-done.20
  271.7 5.7 collective-permute-done.18
  282.6 4.3 reduce-scatter.5.cloned.1.call-done
  288.6 2.6 convert_reduce_fusion.4
  293.2 4.4 all-to-all-start.1
  301.8 2.0 pad.32
  306.8 10.0 %convolution_convert_fusion.3.other_ref.refs_1_ = bf16[1024,1152]{1,0:T(8,128)(2,1)} fusion(s32[1024]{0:T(1024)S(1)} %add_select_fusion.5, f32[768,1152]{1,0:T(8,128)} %copy-done.14, bf16[1088,1152]{1,0:T(8,128)(2,1)S(1)} %constant_dynamic-update-slice_fusion.5.refs_2_, f32[]{:T(128)S(6)} %convert.29, f32[1152]{0:T(1024)S(1)} %get-tuple-element.80, ...), kind=kOutput, calls=%fused_computation.16 | convolution fusion | flops 3751034880 | bytes 11756804 | tf_op jit(solution)/shard_map/cr,rd->cd/dot_general | solution.py:467
  316.9 11.8 %all-to-all-done.1 = bf16[8,136,1152]{2,1,0:T(8,128)(2,1)} async-done(((bf16[8,136,1152]{2,1,0:T(8,128)(2,1)}), bf16[8,136,1152]{2,1,0:T(8,128)(2,1)}, u32[]{:S(2)}, u32[]{:S(2)}) %all-to-all-start.1) | async-done | bytes 2506784 | tf_op jit(solution)/shard_map/all_to_all | solution.py:649
  328.7 7.6 %momentum.1 = (f32[1076,1,1152]{2,1,0:T(1,128)}, bf16[1088,1152]{1,0:T(8,128)(2,1)S(1)}, bf16[1088,1152]{1,0:T(8,128)(2,1)S(1)}) custom-call(f32[1076,1,1152]{2,1,0:T(1,128)} %bitcast.176, bf16[1088,1152]{1,0:T(8,128)(2,1)} %bitcast.57.grad_ref), custom_call_target="tpu_custom_call" | custom-call | tf_op jit(solution)/shard_map/momentum/pallas_call | solution.py:110
  336.3 9.0 %gram.1.first_ref = f32[5760,128]{1,0:T(8,128)} custom-call(bf16[1088,1152]{1,0:T(8,128)(2,1)S(1)} %get-tuple-element.20.top_ref.refs_1_, bf16[1088,1152]{1,0:T(8,128)(2,1)S(1)} %get-tuple-element.21.rest_ref.refs_2_), custom_call_target="tpu_custom_call" | custom-call | tf_op jit(solution)/shard_map/gram/pallas_call | solution.py:169
  346.9 3.1 convolution_convert_fusion.5
  351.6 8.8 %attend_back.1 = bf16[3,4,80,768]{3,2,1,0:T(8,128)(2,1)S(1)} custom-call(bf16[3,4,80,768]{3,2,1,0:T(8,128)(2,1)S(1)} %bitcast.165, bf16[4,768,768]{2,1,0:T(8,128)(2,1)} %get-tuple-element.18.soft_ref, bf16[4,80,768]{2,1,0:T(8,128)(2,1)S(1)} %bitcast.174, f32[5760,128]{1,0:T(8,128)} %gram.1.first_ref, ...), custom_call_target="tpu_custom_call" | custom-call | tf_op jit(solution)/shard_map/attend_back/pallas_call | solution.py:425
  360.8 4.4 convolution_convert_fusion.4
  369.1 6.5 %fusion.66 = (f32[1152]{0:T(1024)S(1)}, f32[1152]{0:T(1024)S(1)}, bf16[768,1152]{1,0:T(8,128)(2,1)}) fusion(f32[768]{0:T(1024)S(1)} %add_rsqrt_fusion.1, f32[768,1152]{1,0:T(8,128)} %copy-done.22, f32[768]{0:T(1024)S(1)} %broadcast_multiply_fusion.1, bf16[960,768]{1,0:T(8,128)(2,1)S(1)} %bitcast.167, bf16[320,1152]{1,0:T(8,128)(2,1)} %get-tuple-element.48, ...), kind=kOutput, calls=%fused_computation.237 | convolution fusion | flops 1710634752 | bytes 9010176 | tf_op jit(solution)/shard_map/er,ed->rd/dot_general | solution.py:467
  380.9 8.0 %collective-permute-done.23 = bf16[2,1,1,80,1152]{4,3,2,1,0:T(8,128)(2,1)S(1)} collective-permute-done((bf16[2,1,1,80,1152]{4,3,2,1,0:T(8,128)(2,1)S(1)}, bf16[2,1,1,80,1152]{4,3,2,1,0:T(8,128)(2,1)S(1)}, u32[]{:S(2)}, u32[]{:S(2)}) %collective-permute-start.23) | collective-permute-done | bytes 368672 | tf_op jit(solution)/shard_map/ppermute | solution.py:472
  390.5 11.1 %reduce-scatter.7.cloned.1.call-done = f32[1440,128]{1,0:T(8,128)} async-done(((f32[5760,128]{1,0:T(8,128)}), f32[1440,128]{1,0:T(8,128)}) %reduce-scatter.7.cloned.1.call-update) | async-done | bytes 737296 | tf_op jit(solution)/shard_map/reduce_scatter | solution.py:761
  403.3 4.7 collective-permute-done.27
  411.2 3.6 all-to-all-start.2
  415.0 5.2 convolution_convert_fusion.2.refs_3_.refs_0_
  420.3 6.6 %all-to-all-done.2 = bf16[8,40,1152]{2,1,0:T(8,128)(2,1)S(1)} async-done(((bf16[8,40,1152]{2,1,0:T(8,128)(2,1)}), bf16[8,40,1152]{2,1,0:T(8,128)(2,1)S(1)}, u32[]{:S(2)}, u32[]{:S(2)}) %all-to-all-start.2) | async-done | bytes 737312 | tf_op jit(solution)/shard_map/all_to_all | solution.py:649
  428.1 3.5 momentum_again.1
  435.3 3.7 collective-permute-done.29
  439.6 3.6 collective-permute-done.30
  444.4 8.3 %collective-permute-done.31 = f32[112,128]{1,0:T(8,128)S(1)} collective-permute-done((f32[112,128]{1,0:T(8,128)S(1)}, f32[112,128]{1,0:T(8,128)S(1)}, u32[]{:S(2)}, u32[]{:S(2)}) %collective-permute-start.31) | collective-permute-done | bytes 57376 | tf_op jit(solution)/shard_map/ppermute | solution.py:472
  452.8 2.0 slice.281.refs_0_
  454.8 6.6 %collective-permute-done.32 = f32[112,128]{1,0:T(8,128)S(1)} collective-permute-done((f32[112,128]{1,0:T(8,128)S(1)}, f32[112,128]{1,0:T(8,128)S(1)}, u32[]{:S(2)}, u32[]{:S(2)}) %collective-permute-start.32) | collective-permute-done | bytes 57376 | tf_op jit(solution)/shard_map/ppermute | solution.py:472
  461.4 4.2 all-gather.11.cloned.1.call-done.refs_1_.refs_3_.gram_ref
  465.5 1.8 copy-done.1
  467.5 54.3 %all-gather.13.cloned.1.call-done.refs_2_.full_hbm = bf16[1152,1152]{1,0:T(8,128)(2,1)} async-done(((bf16[288,1152]{1,0:T(8,128)(2,1)}), bf16[1152,1152]{1,0:T(8,128)(2,1)}) %all-gather.13.cloned.1.call-update) | async-done | bytes 2654224 | tf_op jit(solution)/shard_map/all_gather | solution.py:826
  528.2 95.6 %iterate.1 = f32[1076,1,1152]{2,1,0:T(1,128)} custom-call(s32[1]{0:T(128)} %bitcast.79.square_ref, f32[1]{0:T(128)} %bitcast.80.rate_ref, f32[5760,128]{1,0:T(8,128)} %all-gather.11.cloned.1.call-done.refs_1_.refs_3_.gram_ref, bf16[1152,1152]{1,0:T(8,128)(2,1)} %all-gather.13.cloned.1.call-done.refs_2_.full_hbm, ...), custom_call_target="tpu_custom_call" | custom-call | flops 80000000000 | bytes 20000000 | tf_op jit(solution)/shard_map/iterate/pallas_call | solution.py:361
  625.4 2.2 bitcast_convert_fusion.1
  (325 shorter events, 102.4 us)
Async XLA Ops:
  12.0 5.4 copy-start.34
  12.0 5.5 copy-start.11
  12.0 6.2 copy-start.42
  12.0 68.9 %all-to-all-start = ((bf16[8,136,1152]{2,1,0:T(8,128)(2,1)}), bf16[8,136,1152]{2,1,0:T(8,128)(2,1)}, u32[]{:S(2)}, u32[]{:S(2)}) async-start(bf16[8,136,1152]{2,1,0:T(8,128)(2,1)} %bitcast.20), calls=%async_computation | async-start | bytes 5013504 | tf_op jit(solution)/shard_map/all_to_all | solution.py:649
  17.4 122.1 %all-gather.15.cloned.1.call-start = ((), (), s32[]{:S(2)}) async-start(), calls=%async_computation.15 | async-start | bytes 6082560 | tf_op jit(solution)/shard_map/all_gather | solution.py:627
  22.1 191.6 %all-gather.7.cloned.1.call-start = ((), (), s32[]{:S(2)}) async-start(), calls=%async_computation.7 | async-start | bytes 2211840 | tf_op jit(solution)/shard_map/all_gather | solution.py:704
  23.4 6.0 copy-start.37
  25.6 39.2 %collective-permute-start.2 = (bf16[320,1152]{1,0:T(8,128)(2,1)S(1)}, bf16[320,1152]{1,0:T(8,128)(2,1)S(1)}, u32[]{:S(2)}, u32[]{:S(2)}) collective-permute-start(bf16[320,1152]{1,0:T(8,128)(2,1)S(1)} %prep_square.1), channel_id=1, source_target_pairs={{0,24},{4,28},{8,16},{12,20},{16,8},{20,12},{24,0},{28,4},{1,25},{... | collective-permute-start | bytes 2211848 | tf_op jit(solution)/shard_map/ppermute | solution.py:472
  28.8 50.3 %collective-permute-start.1 = (bf16[320,1152]{1,0:T(8,128)(2,1)S(1)}, bf16[320,1152]{1,0:T(8,128)(2,1)S(1)}, u32[]{:S(2)}, u32[]{:S(2)}) collective-permute-start(bf16[320,1152]{1,0:T(8,128)(2,1)S(1)} %prep_square.1), channel_id=1, source_target_pairs={{0,16},{4,20},{8,24},{12,28},{16,0},{20,4},{24,8},{28,12},{1,17},{... | collective-permute-start | bytes 2211848 | tf_op jit(solution)/shard_map/ppermute | solution.py:472
  29.3 49.8 %collective-permute-start = (bf16[320,1152]{1,0:T(8,128)(2,1)S(1)}, bf16[320,1152]{1,0:T(8,128)(2,1)S(1)}, u32[]{:S(2)}, u32[]{:S(2)}) collective-permute-start(bf16[320,1152]{1,0:T(8,128)(2,1)S(1)} %prep_square.1), channel_id=1, source_target_pairs={{0,8},{4,12},{8,0},{12,4},{16,24},{20,28},{24,16},{28,20},{1,9},{5... | collective-permute-start | bytes 2211848 | tf_op jit(solution)/shard_map/ppermute | solution.py:472
  80.9 38.2 %collective-permute-start.3 = (bf16[4,320,1152]{2,1,0:T(8,128)(2,1)}, bf16[4,320,1152]{2,1,0:T(8,128)(2,1)}, u32[]{:S(2)}, u32[]{:S(2)}) collective-permute-start(bf16[4,320,1152]{2,1,0:T(8,128)(2,1)} %pad_maximum_fusion), channel_id=1, source_target_pairs={{0,4},{4,0},{8,12},{12,8},{16,20},{20,16},{24,28},{28,24},{1,5},{5... | collective-permute-start | bytes 8847368 | tf_op jit(solution)/shard_map/ppermute | solution.py:472
  83.7 17.2 %collective-permute-start.4 = (bf16[272,1152]{1,0:T(8,128)(2,1)}, bf16[272,1152]{1,0:T(8,128)(2,1)}, u32[]{:S(2)}, u32[]{:S(2)}) collective-permute-start(bf16[272,1152]{1,0:T(8,128)(2,1)} %pad_maximum_fusion.7), channel_id=1, source_target_pairs={{0,8},{4,12},{8,0},{12,4},{16,24},{20,28},{24,16},{28,20},{1,9},{5... | collective-permute-start | bytes 1880072 | tf_op jit(solution)/shard_map/ppermute | solution.py:472
  85.7 29.9 %collective-permute-start.5 = (bf16[272,1152]{1,0:T(8,128)(2,1)}, bf16[272,1152]{1,0:T(8,128)(2,1)}, u32[]{:S(2)}, u32[]{:S(2)}) collective-permute-start(bf16[272,1152]{1,0:T(8,128)(2,1)} %pad_maximum_fusion.7), channel_id=1, source_target_pairs={{0,16},{4,20},{8,24},{12,28},{16,0},{20,4},{24,8},{28,12},{1,17},{... | collective-permute-start | bytes 1880072 | tf_op jit(solution)/shard_map/ppermute | solution.py:472
  89.0 28.4 %collective-permute-start.6 = (bf16[272,1152]{1,0:T(8,128)(2,1)}, bf16[272,1152]{1,0:T(8,128)(2,1)S(1)}, u32[]{:S(2)}, u32[]{:S(2)}) collective-permute-start(bf16[272,1152]{1,0:T(8,128)(2,1)} %pad_maximum_fusion.7), channel_id=1, source_target_pairs={{0,24},{4,28},{8,16},{12,20},{16,8},{20,12},{24,0},{28,4},{1,25},{... | collective-permute-start | bytes 1880072 | tf_op jit(solution)/shard_map/ppermute | solution.py:472
  118.4 18.5 %collective-permute-start.7 = (bf16[544,1152]{1,0:T(8,128)(2,1)S(1)}, bf16[544,1152]{1,0:T(8,128)(2,1)S(1)}, u32[]{:S(2)}, u32[]{:S(2)}) collective-permute-start(bf16[544,1152]{1,0:T(8,128)(2,1)S(1)} %pad_maximum_fusion.2), channel_id=1, source_target_pairs={{0,4},{4,0},{8,12},{12,8},{16,20},{20,16},{24,28},{28,24},{1,5},{5... | collective-permute-start | bytes 3760136 | tf_op jit(solution)/shard_map/ppermute | solution.py:472
  118.6 20.1 %collective-permute-start.8 = (bf16[544,1152]{1,0:T(8,128)(2,1)S(1)}, bf16[544,1152]{1,0:T(8,128)(2,1)S(1)}, u32[]{:S(2)}, u32[]{:S(2)}) collective-permute-start(bf16[544,1152]{1,0:T(8,128)(2,1)S(1)} %pad_maximum_fusion.3), channel_id=1, source_target_pairs={{0,4},{4,0},{8,12},{12,8},{16,20},{20,16},{24,28},{28,24},{1,5},{5... | collective-permute-start | bytes 3760136 | tf_op jit(solution)/shard_map/ppermute | solution.py:472
  120.1 12.9 %collective-permute-start.11 = (bf16[40,1152]{1,0:T(8,128)(2,1)S(1)}, bf16[40,1152]{1,0:T(8,128)(2,1)S(1)}, u32[]{:S(2)}, u32[]{:S(2)}) collective-permute-start(bf16[40,1152]{1,0:T(8,128)(2,1)S(1)} %get-tuple-element.50), channel_id=1, source_target_pairs={{0,3},{1,0},{2,1},{3,2},{4,7},{5,4},{6,5},{7,6},{8,11},{9,8},{10,9... | collective-permute-start | bytes 276488 | tf_op jit(solution)/shard_map/ppermute | solution.py:507
  124.4 8.6 %collective-permute-start.10 = (bf16[40,1152]{1,0:T(8,128)(2,1)S(1)}, bf16[40,1152]{1,0:T(8,128)(2,1)S(1)}, u32[]{:S(2)}, u32[]{:S(2)}) collective-permute-start(bf16[40,1152]{1,0:T(8,128)(2,1)S(1)} %get-tuple-element.50), channel_id=1, source_target_pairs={{0,2},{1,3},{2,0},{3,1},{4,6},{5,7},{6,4},{7,5},{8,10},{9,11},{10,... | collective-permute-start | bytes 276488 | tf_op jit(solution)/shard_map/ppermute | solution.py:507
  124.4 7.1 %collective-permute-start.9 = (bf16[40,1152]{1,0:T(8,128)(2,1)S(1)}, bf16[40,1152]{1,0:T(8,128)(2,1)S(1)}, u32[]{:S(2)}, u32[]{:S(2)}) collective-permute-start(bf16[40,1152]{1,0:T(8,128)(2,1)S(1)} %get-tuple-element.50), channel_id=1, source_target_pairs={{0,1},{1,2},{2,3},{3,0},{4,5},{5,6},{6,7},{7,4},{8,9},{9,10},{10,1... | collective-permute-start | bytes 276488 | tf_op jit(solution)/shard_map/ppermute | solution.py:507
  129.3 7.6 %copy-start.6 = (bf16[1088,1152]{1,0:T(8,128)(2,1)S(1)}, bf16[1088,1152]{1,0:T(8,128)(2,1)}, u32[]{:S(2)}) copy-start(bf16[1088,1152]{1,0:T(8,128)(2,1)} %get-tuple-element.73) | copy-start | bytes 7520260
  133.0 44.9 %collective-permute-start.14 = (bf16[160,1152]{1,0:T(8,128)(2,1)S(1)}, bf16[160,1152]{1,0:T(8,128)(2,1)S(1)}, u32[]{:S(2)}, u32[]{:S(2)}) collective-permute-start(bf16[160,1152]{1,0:T(8,128)(2,1)S(1)} %bitcast.168), channel_id=1, source_target_pairs={{0,24},{4,28},{8,16},{12,20},{16,8},{20,12},{24,0},{28,4},{1,25},{... | collective-permute-start | bytes 1105928 | tf_op jit(solution)/shard_map/ppermute | solution.py:472
  134.7 41.5 %collective-permute-start.13 = (bf16[160,1152]{1,0:T(8,128)(2,1)S(1)}, bf16[160,1152]{1,0:T(8,128)(2,1)}, u32[]{:S(2)}, u32[]{:S(2)}) collective-permute-start(bf16[160,1152]{1,0:T(8,128)(2,1)S(1)} %bitcast.169), channel_id=1, source_target_pairs={{0,16},{4,20},{8,24},{12,28},{16,0},{20,4},{24,8},{28,12},{1,17},{... | collective-permute-start | bytes 1105928 | tf_op jit(solution)/shard_map/ppermute | solution.py:472
  135.2 39.1 %collective-permute-start.12 = (bf16[160,1152]{1,0:T(8,128)(2,1)S(1)}, bf16[160,1152]{1,0:T(8,128)(2,1)}, u32[]{:S(2)}, u32[]{:S(2)}) collective-permute-start(bf16[160,1152]{1,0:T(8,128)(2,1)S(1)} %bitcast.170), channel_id=1, source_target_pairs={{0,8},{4,12},{8,0},{12,4},{16,24},{20,28},{24,16},{28,20},{1,9},{5... | collective-permute-start | bytes 1105928 | tf_op jit(solution)/shard_map/ppermute | solution.py:472
  159.7 5.1 copy-start.22
  174.3 112.6 %reduce-scatter.5.cloned.1.call-start = ((), (), s32[]{:S(2)}) async-start(), calls=%async_computation.8 | async-start | bytes 2211840 | tf_op jit(solution)/shard_map/reduce_scatter | solution.py:735
  181.5 3.6 collective-permute-start.15
  221.5 11.0 %copy-start.16 = (f32[768,1152]{1,0:T(8,128)}, f32[768,1152]{1,0:T(8,128)S(1)}, u32[]{:S(2)}) copy-start(f32[768,1152]{1,0:T(8,128)S(1)} %subtract_multiply_fusion) | copy-start | bytes 10616836
  232.5 4.7 copy-start.23
  237.2 12.4 %collective-permute-start.16 = (bf16[1,2,2,136,1152]{4,3,2,1,0:T(8,128)(2,1)}, bf16[1,2,2,136,1152]{4,3,2,1,0:T(8,128)(2,1)}, u32[]{:S(2)}, u32[]{:S(2)}) collective-permute-start(bf16[1,2,2,136,1152]{4,3,2,1,0:T(8,128)(2,1)} %bitcast.48), channel_id=1, source_target_pairs={{0,4},{4,0},{8,12},{12,8},{16,20},{20,16},{24,28},{28,24},{1,5},{5... | collective-permute-start | bytes 3760136 | tf_op jit(solution)/shard_map/ppermute | solution.py:472
  238.9 14.3 %collective-permute-start.19 = (bf16[1,2,2,136,1152]{4,3,2,1,0:T(8,128)(2,1)}, bf16[1,2,2,136,1152]{4,3,2,1,0:T(8,128)(2,1)}, u32[]{:S(2)}, u32[]{:S(2)}) collective-permute-start(bf16[1,2,2,136,1152]{4,3,2,1,0:T(8,128)(2,1)} %bitcast.51), channel_id=1, source_target_pairs={{0,4},{4,0},{8,12},{12,8},{16,20},{20,16},{24,28},{28,24},{1,5},{5... | collective-permute-start | bytes 3760136 | tf_op jit(solution)/shard_map/ppermute | solution.py:472
  249.5 97.3 %all-gather.9.cloned.1.call-start = ((), (), s32[]{:S(2)}) async-start(), calls=%async_computation.9 | async-start | bytes 2211840 | tf_op jit(solution)/shard_map/all_gather | solution.py:750
  249.6 3.7 copy-start.21
  251.7 16.1 %collective-permute-start.17 = (bf16[1,1,2,136,1152]{4,3,2,1,0:T(8,128)(2,1)S(1)}, bf16[1,1,2,136,1152]{4,3,2,1,0:T(8,128)(2,1)S(1)}, u32[]{:S(2)}, u32[]{:S(2)}) collective-permute-start(bf16[1,1,2,136,1152]{4,3,2,1,0:T(8,128)(2,1)S(1)} %slice.315), channel_id=1, source_target_pairs={{0,16},{4,20},{8,24},{12,28},{16,0},{20,4},{24,8},{28,12},{1,17},{... | collective-permute-start | bytes 1880072 | tf_op jit(solution)/shard_map/ppermute | solution.py:472
  255.0 16.5 %collective-permute-start.20 = (bf16[1,2,1,136,1152]{4,3,2,1,0:T(8,128)(2,1)S(1)}, bf16[1,2,1,136,1152]{4,3,2,1,0:T(8,128)(2,1)S(1)}, u32[]{:S(2)}, u32[]{:S(2)}) collective-permute-start(bf16[1,2,1,136,1152]{4,3,2,1,0:T(8,128)(2,1)S(1)} %slice.321), channel_id=1, source_target_pairs={{0,8},{4,12},{8,0},{12,4},{16,24},{20,28},{24,16},{28,20},{1,9},{5... | collective-permute-start | bytes 1880072 | tf_op jit(solution)/shard_map/ppermute | solution.py:472
  268.0 9.4 %collective-permute-start.18 = (bf16[1,1,1,136,1152]{4,3,2,1,0:T(8,128)(2,1)S(1)}, bf16[1,1,1,136,1152]{4,3,2,1,0:T(8,128)(2,1)S(1)}, u32[]{:S(2)}, u32[]{:S(2)}) collective-permute-start(bf16[1,1,1,136,1152]{4,3,2,1,0:T(8,128)(2,1)S(1)} %slice.317), channel_id=1, source_target_pairs={{0,8},{4,12},{8,0},{12,4},{16,24},{20,28},{24,16},{28,20},{1,9},{5... | collective-permute-start | bytes 940040 | tf_op jit(solution)/shard_map/ppermute | solution.py:472
  271.6 7.5 %collective-permute-start.21 = (bf16[1,1,1,136,1152]{4,3,2,1,0:T(8,128)(2,1)S(1)}, bf16[1,1,1,136,1152]{4,3,2,1,0:T(8,128)(2,1)S(1)}, u32[]{:S(2)}, u32[]{:S(2)}) collective-permute-start(bf16[1,1,1,136,1152]{4,3,2,1,0:T(8,128)(2,1)S(1)} %slice.323), channel_id=1, source_target_pairs={{0,16},{4,20},{8,24},{12,28},{16,0},{20,4},{24,8},{28,12},{1,17},{... | collective-permute-start | bytes 940040 | tf_op jit(solution)/shard_map/ppermute | solution.py:472
  293.2 35.4 %all-to-all-start.1 = ((bf16[8,136,1152]{2,1,0:T(8,128)(2,1)}), bf16[8,136,1152]{2,1,0:T(8,128)(2,1)}, u32[]{:S(2)}, u32[]{:S(2)}) async-start(bf16[8,136,1152]{2,1,0:T(8,128)(2,1)} %copy-done.15), calls=%async_computation.2 | async-start | bytes 5013504 | tf_op jit(solution)/shard_map/all_to_all | solution.py:649
  297.6 104.0 %reduce-scatter.7.cloned.1.call-start = ((), (), s32[]{:S(2)}) async-start(), calls=%async_computation.10 | async-start | bytes 3686400 | tf_op jit(solution)/shard_map/reduce_scatter | solution.py:761
  336.3 9.0 %copy-start = (bf16[1088,1152]{1,0:T(8,128)(2,1)}, bf16[1088,1152]{1,0:T(8,128)(2,1)S(1)}, u32[]{:S(2)}) copy-start(bf16[1088,1152]{1,0:T(8,128)(2,1)S(1)} %get-tuple-element.20.top_ref.refs_1_) | copy-start | bytes 7520260
  346.8 118.7 %all-gather.11.cloned.1.call-start = ((), (), s32[]{:S(2)}) async-start(), calls=%async_computation.11 | async-start | bytes 3686400 | tf_op jit(solution)/shard_map/all_gather | solution.py:762
  367.2 9.3 %collective-permute-start.22 = (bf16[2,2,1,80,1152]{4,3,2,1,0:T(8,128)(2,1)}, bf16[2,2,1,80,1152]{4,3,2,1,0:T(8,128)(2,1)}, u32[]{:S(2)}, u32[]{:S(2)}) collective-permute-start(bf16[2,2,1,80,1152]{4,3,2,1,0:T(8,128)(2,1)} %fusion.30), channel_id=1, source_target_pairs={{0,4},{4,0},{8,12},{12,8},{16,20},{20,16},{24,28},{28,24},{1,5},{5... | collective-permute-start | bytes 2211848 | tf_op jit(solution)/shard_map/ppermute | solution.py:472
  368.2 10.4 %collective-permute-start.25 = (bf16[2,2,1,80,1152]{4,3,2,1,0:T(8,128)(2,1)}, bf16[2,2,1,80,1152]{4,3,2,1,0:T(8,128)(2,1)}, u32[]{:S(2)}, u32[]{:S(2)}) collective-permute-start(bf16[2,2,1,80,1152]{4,3,2,1,0:T(8,128)(2,1)} %fusion.28), channel_id=1, source_target_pairs={{0,4},{4,0},{8,12},{12,8},{16,20},{20,16},{24,28},{28,24},{1,5},{5... | collective-permute-start | bytes 2211848 | tf_op jit(solution)/shard_map/ppermute | solution.py:472
  369.1 6.6 %copy-start.27 = (bf16[768,1152]{1,0:T(8,128)(2,1)S(1)}, bf16[768,1152]{1,0:T(8,128)(2,1)}, u32[]{:S(2)}) copy-start(bf16[768,1152]{1,0:T(8,128)(2,1)} %all-gather.9.cloned.1.call-done) | copy-start | bytes 5308420
  378.3 10.6 %collective-permute-start.23 = (bf16[2,1,1,80,1152]{4,3,2,1,0:T(8,128)(2,1)S(1)}, bf16[2,1,1,80,1152]{4,3,2,1,0:T(8,128)(2,1)S(1)}, u32[]{:S(2)}, u32[]{:S(2)}) collective-permute-start(bf16[2,1,1,80,1152]{4,3,2,1,0:T(8,128)(2,1)S(1)} %constant_dynamic-slice_fusion.3), channel_id=1, source_target_pairs={{0,8},{4,12},{8,0},{12,4},{16,24},{20,28},{24,16},{28,20},{1,9},{5... | collective-permute-start | bytes 1105928 | tf_op jit(solution)/shard_map/ppermute | solution.py:472
  380.0 10.5 %collective-permute-start.26 = (bf16[1,2,1,80,1152]{4,3,2,1,0:T(8,128)(2,1)S(1)}, bf16[1,2,1,80,1152]{4,3,2,1,0:T(8,128)(2,1)S(1)}, u32[]{:S(2)}, u32[]{:S(2)}) collective-permute-start(bf16[1,2,1,80,1152]{4,3,2,1,0:T(8,128)(2,1)S(1)} %constant_dynamic-slice_fusion.1), channel_id=1, source_target_pairs={{0,16},{4,20},{8,24},{12,28},{16,0},{20,4},{24,8},{28,12},{1,17},{... | collective-permute-start | bytes 1105928 | tf_op jit(solution)/shard_map/ppermute | solution.py:472
  389.0 14.1 %collective-permute-start.24 = (bf16[1,1,1,80,1152]{4,3,2,1,0:T(8,128)(2,1)S(1)}, bf16[1,1,1,80,1152]{4,3,2,1,0:T(8,128)(2,1)S(1)}, u32[]{:S(2)}, u32[]{:S(2)}) collective-permute-start(bf16[1,1,1,80,1152]{4,3,2,1,0:T(8,128)(2,1)S(1)} %constant_dynamic-slice_fusion.2), channel_id=1, source_target_pairs={{0,16},{4,20},{8,24},{12,28},{16,0},{20,4},{24,8},{28,12},{1,17},{... | collective-permute-start | bytes 552968 | tf_op jit(solution)/shard_map/ppermute | solution.py:472
  401.7 6.3 collective-permute-start.27
  411.2 15.7 %all-to-all-start.2 = ((bf16[8,40,1152]{2,1,0:T(8,128)(2,1)}), bf16[8,40,1152]{2,1,0:T(8,128)(2,1)S(1)}, u32[]{:S(2)}, u32[]{:S(2)}) async-start(bf16[8,40,1152]{2,1,0:T(8,128)(2,1)} %add_add_fusion), calls=%async_computation.4 | async-start | bytes 1474560 | tf_op jit(solution)/shard_map/all_to_all | solution.py:649
  414.8 107.0 %all-gather.13.cloned.1.call-start = ((), (), s32[]{:S(2)}) async-start(), calls=%async_computation.12 | async-start | bytes 3317760 | tf_op jit(solution)/shard_map/all_gather | solution.py:826
  433.4 1.3 collective-permute-start.28
  434.8 4.2 collective-permute-start.29
  439.0 4.2 collective-permute-start.30
  443.3 9.4 %collective-permute-start.31 = (f32[112,128]{1,0:T(8,128)S(1)}, f32[112,128]{1,0:T(8,128)S(1)}, u32[]{:S(2)}, u32[]{:S(2)}) collective-permute-start(f32[112,128]{1,0:T(8,128)S(1)} %add.590), channel_id=1, source_target_pairs={{0,1},{1,0},{2,3},{3,2},{4,5},{5,4},{6,7},{7,6},{8,9},{9,8},{10,11... | collective-permute-start | bytes 172040 | tf_op jit(solution)/shard_map/ppermute | solution.py:472
  452.7 8.7 %collective-permute-start.32 = (f32[112,128]{1,0:T(8,128)S(1)}, f32[112,128]{1,0:T(8,128)S(1)}, u32[]{:S(2)}, u32[]{:S(2)}) collective-permute-start(f32[112,128]{1,0:T(8,128)S(1)} %add.591), channel_id=1, source_target_pairs={{0,2},{1,3},{2,0},{3,1},{4,6},{5,7},{6,4},{7,5},{8,10},{9,11},{10,... | collective-permute-start | bytes 172040 | tf_op jit(solution)/shard_map/ppermute | solution.py:472
  461.4 66.1 %copy-start.10 = (f32[112,128]{1,0:T(8,128)}, f32[112,128]{1,0:T(8,128)S(1)}, u32[]{:S(2)}) copy-start(f32[112,128]{1,0:T(8,128)S(1)} %add.592.refs_2_.first_ref) | copy-start | bytes 172036
  467.4 58.3 %copy-start.38 = (s32[6]{0:T(128)S(1)}, s32[6]{0:T(128)}, u32[]{:S(2)}) copy-start(s32[6]{0:T(128)} %param.13) | copy-start | bytes 76
  467.4 59.6 %copy-start.36 = (f32[2,3380]{1,0:T(2,128)S(1)}, f32[2,3380]{1,0:T(2,128)}, u32[]{:S(2)}) copy-start(f32[2,3380]{1,0:T(2,128)} %param.17) | copy-start | bytes 81124
  467.4 59.7 %copy-start.39 = (f32[256]{0:T(256)S(1)}, f32[256]{0:T(256)}, u32[]{:S(2)}) copy-start(f32[256]{0:T(256)} %get-tuple-element.62) | copy-start | bytes 3076
  467.4 156.4 %reduce-scatter.11.cloned.1.call-start = ((), (), s32[]{:S(2)}) async-start(), calls=%async_computation.14 | async-start | bytes 2949120 | tf_op jit(solution)/shard_map/reduce_scatter | solution.py:837
  521.8 5.4 copy-start.12
  521.8 5.7 copy-start.35
  521.8 103.6 %reduce-scatter.9.cloned.1.call-start = ((), (), s32[]{:S(2)}) async-start(), calls=%async_computation.13 | async-start | bytes 2949120 | tf_op jit(solution)/shard_map/reduce_scatter | solution.py:840
  623.8 3.8 copy-start.41
  623.8 3.7 copy-start.25
  (26 other events, 52.9 us)
Sparse Core Ops, SparseCore 0:
  22.2 94.1 all-gather.14
  174.4 39.2 all-gather.6
  249.6 37.2 reduce-scatter.4
  291.4 39.4 all-gather.8
  346.9 54.6 reduce-scatter.6
  403.0 62.4 all-gather.10
  467.7 54.0 all-gather.12
  524.1 46.7 reduce-scatter.10
  573.2 47.5 reduce-scatter.8

commit v5 on v4

--- a/solution.py
+++ b/solution.py
@@ -735,7 +735,7 @@
         lax.psum_scatter(grad_normed_two_part, "seq", scatter_dimension=0, tiled=True),
         wide_back[0, 0, 0],
     ).astype(f32)
-    back_wide = send(wide_back).reshape(wide_rows, width)
+
     def own_share(x):
         return lax.dynamic_slice_in_dim(x, seq_index * share, share)
 
@@ -748,6 +748,8 @@
     grad_attn_own = (own_grad + grad_mid_norm).astype(low)
     grad_bias_out = jnp.sum(grad_attn_own.astype(f32), axis=0)
     grad_attn = lax.all_gather(grad_attn_own, "seq", axis=0, tiled=True)
+    (wide_back,) = touch([wide_back], grad_attn_own)
+    back_wide = send(wide_back).reshape(wide_rows, width)
     unpick = (slot_row[:, None] == jnp.arange(packed)[None, :]).astype(low)
     placed_middle = jnp.where(
         (jnp.arange(packed) // share == seq_index)[:, None], middle + row_params[7], 0.0
@@ -758,12 +760,17 @@
     out_slots = product("cr,rd->cd", unpick, out_part).astype(low)
     first_moment, top, rest = momentum(moments, back_wide)
     wide_gram = gram_of(top, rest)
-    gram_share = lax.psum_scatter(wide_gram, "seq", scatter_dimension=0, tiled=True)
-    first_gram = lax.all_gather(gram_share, "seq", axis=0, tiled=True)
+    gram_parts = send(wide_gram.reshape(dp_count, -1, 128))
+    gram_two = jnp.concatenate(
+        [lax.dynamic_index_in_dim(gram_parts, owner_table[m], 0, keepdims=False) for m in (4, 5)],
+        axis=0,
+    )
 
 
     grad_context = product("de,rd->er", w_out_own, grad_attn).astype(low)
     grad_qkv = attend_back(qkv, soft, grad_context.reshape(heads, head_pad, packed), wide_gram, out_slots, score_scale)
+    (gram_two,) = touch([gram_two], grad_qkv)
+    gram_sums = lax.psum(gram_two, "seq")
     grad_qkv_flat = grad_qkv.reshape(3 * square_rows, packed)
     grad_attn_cols = lax.dynamic_slice_in_dim(grad_attn, seq_index * cols, cols, axis=1)
     grad_w_out = product("rd,er->de", grad_attn_cols, context)
@@ -786,7 +793,8 @@
         grad_w_out.reshape(heads, head_size, width), ((0, 0), (0, head_pad - head_size), (0, 0))
     )
     late.append(square_parts(grad_w_out.reshape(square_rows, width)))
-    sum_qk = scatter_sum(jnp.concatenate(late[:2], axis=1), orders[0])
+    token = gram_two[0, 0].astype(low)
+    sum_qk = scatter_sum(after(jnp.concatenate(late[:2], axis=1), token), orders[0])
     sum_vo = scatter_sum(jnp.concatenate(late[2:], axis=1), orders[1])
     square_back = to_owner(
         [
@@ -795,11 +803,6 @@
             (sum_vo[:square_chunk], 2),
             (sum_vo[square_chunk:], 3),
         ]
-    )
-    back_square = send(after(square_back, gram_share[0, 0])).reshape(square_total, width)[:square_rows]
-    back_square = back_square.reshape(heads, head_pad, width)[:, :head_size].reshape(cols, width)
-    first_moment, top, rest = momentum_again(
-        moments, back_wide[:cols] + back_square, first_moment, top, rest, grad_normed_slots, grad_mid_slots
     )
     def spot(piece):
         return lax.dynamic_update_slice_in_dim(
@@ -821,9 +824,20 @@
     )
     padded = -(-vector_grad.shape[0] // 1024) * 1024
     vector_grad = jnp.pad(vector_grad, (0, padded - vector_grad.shape[0])).reshape(-1, 128)
-    vector_block = total_sum(after(vector_grad, top[0, 0].astype(f32)))
-    (direction,) = touch([top[:cols]], first_gram, vector_block)
-    direction = lax.all_gather(direction, "seq", axis=0, tiled=True)
+    vector_block = total_sum(vector_grad)
+    back_square = send(after(square_back, gram_sums[0, 0] + vector_block[0, 0])).reshape(square_total, width)[:square_rows]
+    back_square = back_square.reshape(heads, head_pad, width)[:, :head_size].reshape(cols, width)
+    first_moment, top, rest = momentum_again(
+        moments, back_wide[:cols] + back_square, first_moment, top, rest, grad_normed_slots, grad_mid_slots
+    )
+    direction = lax.all_gather(top[:cols], "seq", axis=0, tiled=True)
+    chunk_rows = gram_sums.shape[0] // 2
+    (gram_sums,) = touch([gram_sums], vector_block)
+    gram_back = jnp.zeros((), f32)
+    for k, m in enumerate((4, 5)):
+        here = (jnp.arange(dp_count) == owner_table[m])[:, None, None]
+        gram_back = gram_back + jnp.where(here, gram_sums[k * chunk_rows : (k + 1) * chunk_rows][None], 0.0)
+    first_gram = send(gram_back).reshape(wide_gram.shape)
     is_square = jnp.any(owner_table[:4] == dp_index).astype(jnp.int32).reshape(1)
     grad_normed_slots, out_slots = touch([grad_normed_slots, out_slots], direction, first_gram)
     update_scale = jnp.zeros((), f32)

time: 641 us -> 657 us (1.025)
  blocking collectives: 0 us -> 38.9 us
  waiting for transfers between devices: 246 us -> 214 us
  starting transfers between devices: 42 us -> 50.9 us
    all_gather x2 -> x1, waiting for transfers between devices: 58.5 us -> 13.8 us  [local(): direction = lax.all_gather(top[:cols], 'seq', axis=0, tiled=True)]
    all_to_all x0 -> x1, blocking collectives: none -> 38.9 us  [send(): return lax.all_to_all(x, 'dp', split_axis=0, concat_axis=0, tiled=True)]
    psum x0 -> x1, waiting for transfers between devices: none -> 31.7 us  [local(): gram_sums = lax.psum(gram_two, 'seq')]
    reduce_scatter x1 -> x0, waiting for transfers between devices: 11.1 us -> none  [local(): lax.psum_scatter(wide_gram, 'seq', scatter_dimension=0, tiled=True)]
    ppermute x30, waiting for transfers between devices: 128 us -> 118 us  [flip(): return lax.ppermute(x, axis, [(i, i ^ mask) for i in range(count)])]
    all_to_all x3 -> x4, starting transfers between devices: 13.3 us -> 18.2 us  [send(): return lax.all_to_all(x, 'dp', split_axis=0, concat_axis=0, tiled=True)]
    unnamed x106 -> x112, local copies, waits for them, and re-layouts: 23.4 us -> 20.4 us
    all_to_all x3 -> x4, waiting for transfers between devices: 18.4 us -> 19.6 us  [send(): return lax.all_to_all(x, 'dp', split_axis=0, concat_axis=0, tiled=True)]
  transfers between devices with their start and end apart: 45 -> 45, of which waited for: 27 -> 23; matrix products, arithmetic and copies ran while one was open for 21% -> 20% of each run, Pallas kernels for 21% -> 19%
where the time goes in v5:
time: 657 us; the launch traced here: 648 us
  waiting for transfers between devices  214 us (33%)
  Pallas kernels  135 us (21%)
  matrix products  71.5 us (11%)
  local copies, waits for them, and re-layouts  58.5 us (9%)
  starting transfers between devices  50.9 us (8%)
  other arithmetic  47.8 us (7%)
  blocking collectives  38.9 us (6%)
  between operations  32.4 us (5%)
    ppermute x30, waiting for transfers between devices, flip(): return lax.ppermute(x, axis, [(i, i ^ mask) for i in range(count)])  118 us
    pallas_call x1, Pallas kernels, iterate(): call(functools.partial(iterate_body, total), 'iterate', vmem=56, in_specs...  92.3 us
    dot_general x16, matrix products, product(): return jnp.einsum(form, left, right, preferred_element_type=f32)  71.5 us
    all_to_all x1, blocking collectives, send(): return lax.all_to_all(x, 'dp', split_axis=0, concat_axis=0, tiled=True)  38.9 us
    psum x1, waiting for transfers between devices, local(): gram_sums = lax.psum(gram_two, 'seq')  31.7 us
    ppermute x30, starting transfers between devices, flip(): return lax.ppermute(x, axis, [(i, i ^ mask) for i in range(count)])  26.8 us
    all_gather x1, waiting for transfers between devices, local(): lax.all_gather(context_own.reshape(cols, packed), 'seq', axis=0, tiled=True)  22.4 us
    unnamed x112, local copies, waits for them, and re-layouts  20.4 us
  transfers between devices with their start and end apart: 45, of which 23 were waited for; matrix products, arithmetic and copies ran while one was open for 20% of the time, Pallas kernels for 19%

profile of v5, /device:TPU:0, one launch (start us, length us, event | category | flops | bytes accessed | tf_op | source)
XLA Modules:
  0.0 648.5 jit_solution(4290610157207361865)
XLA Ops:
  7.2 4.9 prep_wide.1
  12.1 5.3 all-to-all-start
  22.6 2.2 prep_square.1
  24.8 3.1 collective-permute-start.2
  33.0 31.8 %collective-permute-done.2 = bf16[320,1152]{1,0:T(8,128)(2,1)S(1)} collective-permute-done((bf16[320,1152]{1,0:T(8,128)(2,1)S(1)}, bf16[320,1152]{1,0:T(8,128)(2,1)S(1)}, u32[]{:S(2)}, u32[]{:S(2)}) %collective-permute-start.2) | collective-permute-done | bytes 737312 | tf_op jit(solution)/shard_map/ppermute | solution.py:472
  64.8 14.3 %collective-permute-done.1 = bf16[320,1152]{1,0:T(8,128)(2,1)S(1)} collective-permute-done((bf16[320,1152]{1,0:T(8,128)(2,1)S(1)}, bf16[320,1152]{1,0:T(8,128)(2,1)S(1)}, u32[]{:S(2)}, u32[]{:S(2)}) %collective-permute-start.1) | collective-permute-done | bytes 737312 | tf_op jit(solution)/shard_map/ppermute | solution.py:472
  79.1 1.8 pad_maximum_fusion
  81.0 1.9 constant_dynamic-update-slice_fusion.9
  90.3 10.7 %collective-permute-done.4 = bf16[272,1152]{1,0:T(8,128)(2,1)} collective-permute-done((bf16[272,1152]{1,0:T(8,128)(2,1)}, bf16[272,1152]{1,0:T(8,128)(2,1)}, u32[]{:S(2)}, u32[]{:S(2)}) %collective-permute-start.4) | collective-permute-done | bytes 626720 | tf_op jit(solution)/shard_map/ppermute | solution.py:472
  100.9 1.9 fusion.73
  102.8 12.8 %collective-permute-done.5 = bf16[272,1152]{1,0:T(8,128)(2,1)} collective-permute-done((bf16[272,1152]{1,0:T(8,128)(2,1)}, bf16[272,1152]{1,0:T(8,128)(2,1)}, u32[]{:S(2)}, u32[]{:S(2)}) %collective-permute-start.5) | collective-permute-done | bytes 626720 | tf_op jit(solution)/shard_map/ppermute | solution.py:472
  115.6 1.9 fusion.74
  120.8 4.2 collective-permute-start.11
  126.3 3.3 select_bitcast_fusion.2
  129.6 3.0 collective-permute-done.9
  147.5 7.2 %fusion.5 = bf16[768,1152]{1,0:T(8,128)(2,1)S(1)} fusion(bf16[2112,1152]{1,0:T(8,128)(2,1)} %bitcast.200, s32[2112]{0:T(1024)S(1)} %get-tuple-element.93), kind=kOutput, calls=%fused_computation.24 | convolution fusion | flops 3739631616 | bytes 6643968 | tf_op jit(solution)/shard_map/rc,cd->rd/dot_general | solution.py:467
  157.2 7.3 %fusion.79 = (f32[768]{0:T(1024)S(1)}, f32[768,1152]{1,0:T(8,128)S(1)}) fusion(bf16[2112,1152]{1,0:T(8,128)(2,1)} %bitcast.201, s32[2112]{0:T(1024)S(1)} %get-tuple-element.92), kind=kOutput, calls=%fused_computation.250 | convolution fusion | flops 3739630848 | bytes 8416512 | tf_op jit(solution)/shard_map/rc,cd->rd/dot_general | solution.py:467
  166.2 2.3 add_convert_fusion.2
  168.5 6.5 attend.1
  182.1 2.7 constant_dynamic-slice_fusion.6
  185.8 2.5 collective-permute-done.15
  189.6 2.1 copy.25
  193.4 22.4 %all-gather.6.cloned.1.call-done = bf16[1152,768]{1,0:T(8,128)(2,1)} async-done(((bf16[288,768]{1,0:T(8,128)(2,1)}), bf16[1152,768]{1,0:T(8,128)(2,1)}) %all-gather.6.cloned.1.call-update) | async-done | bytes 1769488 | tf_op jit(solution)/shard_map/all_gather | solution.py:704
  215.8 6.1 fusion.80
  225.5 2.4 convolution_add_fusion
  227.9 3.6 convert_reduce_fusion
  231.5 3.1 convolution_convert_fusion.1
  234.7 2.4 convolution_convert_fusion
  244.9 6.2 fusion.6
  251.1 2.0 fusion.11
  259.2 10.0 %collective-permute-done.17 = bf16[1,1,2,136,1152]{4,3,2,1,0:T(8,128)(2,1)S(1)} collective-permute-done((bf16[1,1,2,136,1152]{4,3,2,1,0:T(8,128)(2,1)S(1)}, bf16[1,1,2,136,1152]{4,3,2,1,0:T(8,128)(2,1)S(1)}, u32[]{:S(2)}, u32[]{:S(2)}) %collective-permute-start.17) | collective-permute-done | bytes 626720 | tf_op jit(solution)/shard_map/ppermute | solution.py:472
  271.0 1.9 collective-permute-done.20
  273.2 5.7 collective-permute-done.18
  280.8 2.1 select_add_fusion.1.refs_0_
  284.9 3.6 reduce-scatter.4.cloned.1.call-done
  290.2 2.6 convert_reduce_fusion.4
  293.9 4.4 all-to-all-start.1
  303.5 10.7 %convolution_convert_fusion.3.other_ref.refs_1_ = bf16[1024,1152]{1,0:T(8,128)(2,1)} fusion(s32[1024]{0:T(1024)S(1)} %add_select_fusion.5, f32[768,1152]{1,0:T(8,128)} %copy-done.18, bf16[1088,1152]{1,0:T(8,128)(2,1)} %copy-done.6, f32[]{:T(128)S(6)} %convert.33, f32[1152]{0:T(1024)S(1)} %get-tuple-element.84, pred[768]{0:T(1024)(128)(4,1)S(1)} %fusion.48, ...), kind=kOutput, calls=%fused_computation.16 | convolution fusion | flops 3751034880 | bytes 11756804 | tf_op jit(solution)/shard_map/cr,rd->cd/dot_general | solution.py:467
  314.2 15.1 %all-to-all-done.1 = bf16[8,136,1152]{2,1,0:T(8,128)(2,1)} async-done(((bf16[8,136,1152]{2,1,0:T(8,128)(2,1)}), bf16[8,136,1152]{2,1,0:T(8,128)(2,1)}, u32[]{:S(2)}, u32[]{:S(2)}) %all-to-all-start.1) | async-done | bytes 2506784 | tf_op jit(solution)/shard_map/all_to_all | solution.py:649
  329.4 7.6 %momentum.1 = (f32[1076,1,1152]{2,1,0:T(1,128)}, bf16[1088,1152]{1,0:T(8,128)(2,1)S(1)}, bf16[1088,1152]{1,0:T(8,128)(2,1)S(1)}) custom-call(f32[1076,1,1152]{2,1,0:T(1,128)} %bitcast.183, bf16[1088,1152]{1,0:T(8,128)(2,1)} %bitcast.57.grad_ref), custom_call_target="tpu_custom_call" | custom-call | tf_op jit(solution)/shard_map/momentum/pallas_call | solution.py:110
  337.0 9.0 %gram.1.first_ref = f32[5760,128]{1,0:T(8,128)} custom-call(bf16[1088,1152]{1,0:T(8,128)(2,1)S(1)} %get-tuple-element.20.top_ref.refs_1_, bf16[1088,1152]{1,0:T(8,128)(2,1)S(1)} %get-tuple-element.21.rest_ref.refs_2_), custom_call_target="tpu_custom_call" | custom-call | tf_op jit(solution)/shard_map/gram/pallas_call | solution.py:169
  346.0 4.9 all-to-all-start.2
  350.9 2.3 convolution_convert_fusion.6
  353.3 8.5 %attend_back.1.refs_1_ = bf16[3,4,80,768]{3,2,1,0:T(8,128)(2,1)S(1)} custom-call(bf16[3,4,80,768]{3,2,1,0:T(8,128)(2,1)S(1)} %bitcast.173, bf16[4,768,768]{2,1,0:T(8,128)(2,1)} %get-tuple-element.18.soft_ref, bf16[4,80,768]{2,1,0:T(8,128)(2,1)S(1)} %bitcast.180, f32[5760,128]{1,0:T(8,128)} %gram.1.first_ref, ...), custom_call_target="tpu_custom_call" | custom-call | tf_op jit(solution)/shard_map/attend_back/pallas_call | solution.py:425
  361.9 3.7 fusion.65
  365.5 3.6 convolution_convert_fusion.4
  370.3 3.1 convolution_convert_fusion.5
  376.2 2.0 collective-permute-start.29
  378.3 8.6 %collective-permute-done.29 = f32[112,128]{1,0:T(8,128)S(1)} collective-permute-done((f32[112,128]{1,0:T(8,128)S(1)}, f32[112,128]{1,0:T(8,128)S(1)}, u32[]{:S(2)}, u32[]{:S(2)}) %collective-permute-start.29) | collective-permute-done | bytes 57376 | tf_op jit(solution)/shard_map/ppermute | solution.py:472
  388.4 2.7 collective-permute-done.30
  393.0 2.4 collective-permute-done.31
  412.6 5.1 collective-permute-done.27
  417.8 7.4 %collective-permute-done.23 = bf16[2,1,1,80,1152]{4,3,2,1,0:T(8,128)(2,1)S(1)} collective-permute-done((bf16[2,1,1,80,1152]{4,3,2,1,0:T(8,128)(2,1)S(1)}, bf16[2,1,1,80,1152]{4,3,2,1,0:T(8,128)(2,1)S(1)}, u32[]{:S(2)}, u32[]{:S(2)}) %collective-permute-start.23) | collective-permute-done | bytes 368672 | tf_op jit(solution)/shard_map/ppermute | solution.py:472
  425.9 31.7 %all-reduce.9.cloned.1.call-done.refs_0_ = f32[1440,128]{1,0:T(8,128)} async-done(((f32[1440,128]{1,0:T(8,128)}), f32[1440,128]{1,0:T(8,128)}) %all-reduce.9.cloned.1.call-update) | async-done | bytes 737296 | tf_op jit(solution)/shard_map/psum | solution.py:773
  461.5 3.7 all-to-all-start.3
  465.4 2.2 fusion.27.refs_4_
  467.6 5.2 convolution_convert_fusion.2.refs_3_.refs_0_
  472.8 4.4 all-to-all-done.3
  478.5 3.6 momentum_again.1
  482.1 2.0 slice.300
  484.5 38.9 %all_to_all.25 = f32[8,720,128]{2,1,0:T(8,128)} all-to-all(f32[8,720,128]{2,1,0:T(8,128)S(1)} %select_add_fusion), channel_id=1, replica_groups=mesh['dp'=8,'seq'=4] {'dp'}, dimensions={0} | all-to-all | bytes 5898240 | tf_op jit(solution)/shard_map/all_to_all | solution.py:649
  523.5 13.8 %all-gather.10.cloned.1.call-done.refs_2_.full_hbm = bf16[1152,1152]{1,0:T(8,128)(2,1)} async-done(((bf16[288,1152]{1,0:T(8,128)(2,1)}), bf16[1152,1152]{1,0:T(8,128)(2,1)}) %all-gather.10.cloned.1.call-update) | async-done | bytes 2654224 | tf_op jit(solution)/shard_map/all_gather | solution.py:833
  543.6 92.3 %iterate.1 = f32[1076,1,1152]{2,1,0:T(1,128)} custom-call(s32[1]{0:T(128)} %bitcast.83.square_ref, f32[1]{0:T(128)} %bitcast.84.rate_ref, f32[5760,128]{1,0:T(8,128)} %bitcast.190, bf16[1152,1152]{1,0:T(8,128)(2,1)} %all-gather.10.cloned.1.call-done.refs_2_.full_hbm, bf16[1088,1152]{1,0:T(8,128)(2,1)} %get-tuple-element.23.top_hbm, ...), custom_call_target="tpu_custom_call" | custom-call | flops 80000000000 | bytes 20000000 | tf_op jit(solution)/shard_map/iterate/pallas_call | solution.py:361
  637.6 2.2 bitcast_convert_fusion.1
  (339 shorter events, 107.1 us)
Async XLA Ops:
  12.0 5.4 copy-start.37
  12.0 5.5 copy-start.15
  12.0 6.2 copy-start.45
  12.0 7.5 %copy-start.28 = (f32[1,256,1152]{2,1,0:T(8,128)S(1)}, f32[1,256,1152]{2,1,0:T(8,128)}, u32[]{:S(2)}) copy-start(f32[1,256,1152]{2,1,0:T(8,128)} %param.11) | copy-start | bytes 3538948
  12.1 68.9 %all-to-all-start = ((bf16[8,136,1152]{2,1,0:T(8,128)(2,1)}), bf16[8,136,1152]{2,1,0:T(8,128)(2,1)}, u32[]{:S(2)}, u32[]{:S(2)}) async-start(bf16[8,136,1152]{2,1,0:T(8,128)(2,1)} %bitcast.20), calls=%async_computation | async-start | bytes 5013504 | tf_op jit(solution)/shard_map/all_to_all | solution.py:649
  17.4 125.1 %all-gather.12.cloned.1.call-start = ((), (), s32[]{:S(2)}) async-start(), calls=%async_computation.15 | async-start | bytes 6082560 | tf_op jit(solution)/shard_map/all_gather | solution.py:627
  21.2 194.6 %all-gather.6.cloned.1.call-start = ((), (), s32[]{:S(2)}) async-start(), calls=%async_computation.8 | async-start | bytes 2211840 | tf_op jit(solution)/shard_map/all_gather | solution.py:704
  22.6 6.0 copy-start.40
  24.8 40.0 %collective-permute-start.2 = (bf16[320,1152]{1,0:T(8,128)(2,1)S(1)}, bf16[320,1152]{1,0:T(8,128)(2,1)S(1)}, u32[]{:S(2)}, u32[]{:S(2)}) collective-permute-start(bf16[320,1152]{1,0:T(8,128)(2,1)S(1)} %prep_square.1), channel_id=1, source_target_pairs={{0,24},{4,28},{8,16},{12,20},{16,8},{20,12},{24,0},{28,4},{1,25},{... | collective-permute-start | bytes 2211848 | tf_op jit(solution)/shard_map/ppermute | solution.py:472
  28.0 51.1 %collective-permute-start.1 = (bf16[320,1152]{1,0:T(8,128)(2,1)S(1)}, bf16[320,1152]{1,0:T(8,128)(2,1)S(1)}, u32[]{:S(2)}, u32[]{:S(2)}) collective-permute-start(bf16[320,1152]{1,0:T(8,128)(2,1)S(1)} %prep_square.1), channel_id=1, source_target_pairs={{0,16},{4,20},{8,24},{12,28},{16,0},{20,4},{24,8},{28,12},{1,17},{... | collective-permute-start | bytes 2211848 | tf_op jit(solution)/shard_map/ppermute | solution.py:472
  28.5 50.7 %collective-permute-start = (bf16[320,1152]{1,0:T(8,128)(2,1)S(1)}, bf16[320,1152]{1,0:T(8,128)(2,1)S(1)}, u32[]{:S(2)}, u32[]{:S(2)}) collective-permute-start(bf16[320,1152]{1,0:T(8,128)(2,1)S(1)} %prep_square.1), channel_id=1, source_target_pairs={{0,8},{4,12},{8,0},{12,4},{16,24},{20,28},{24,16},{28,20},{1,9},{5... | collective-permute-start | bytes 2211848 | tf_op jit(solution)/shard_map/ppermute | solution.py:472
  81.0 38.9 %collective-permute-start.3 = (bf16[4,320,1152]{2,1,0:T(8,128)(2,1)}, bf16[4,320,1152]{2,1,0:T(8,128)(2,1)}, u32[]{:S(2)}, u32[]{:S(2)}) collective-permute-start(bf16[4,320,1152]{2,1,0:T(8,128)(2,1)} %pad_maximum_fusion), channel_id=1, source_target_pairs={{0,4},{4,0},{8,12},{12,8},{16,20},{20,16},{24,28},{28,24},{1,5},{5... | collective-permute-start | bytes 8847368 | tf_op jit(solution)/shard_map/ppermute | solution.py:472
  83.7 17.2 %collective-permute-start.4 = (bf16[272,1152]{1,0:T(8,128)(2,1)}, bf16[272,1152]{1,0:T(8,128)(2,1)}, u32[]{:S(2)}, u32[]{:S(2)}) collective-permute-start(bf16[272,1152]{1,0:T(8,128)(2,1)} %pad_maximum_fusion.8), channel_id=1, source_target_pairs={{0,8},{4,12},{8,0},{12,4},{16,24},{20,28},{24,16},{28,20},{1,9},{5... | collective-permute-start | bytes 1880072 | tf_op jit(solution)/shard_map/ppermute | solution.py:472
  85.7 29.9 %collective-permute-start.5 = (bf16[272,1152]{1,0:T(8,128)(2,1)}, bf16[272,1152]{1,0:T(8,128)(2,1)}, u32[]{:S(2)}, u32[]{:S(2)}) collective-permute-start(bf16[272,1152]{1,0:T(8,128)(2,1)} %pad_maximum_fusion.8), channel_id=1, source_target_pairs={{0,16},{4,20},{8,24},{12,28},{16,0},{20,4},{24,8},{28,12},{1,17},{... | collective-permute-start | bytes 1880072 | tf_op jit(solution)/shard_map/ppermute | solution.py:472
  88.8 28.7 %collective-permute-start.6 = (bf16[272,1152]{1,0:T(8,128)(2,1)}, bf16[272,1152]{1,0:T(8,128)(2,1)S(1)}, u32[]{:S(2)}, u32[]{:S(2)}) collective-permute-start(bf16[272,1152]{1,0:T(8,128)(2,1)} %pad_maximum_fusion.8), channel_id=1, source_target_pairs={{0,24},{4,28},{8,16},{12,20},{16,8},{20,12},{24,0},{28,4},{1,25},{... | collective-permute-start | bytes 1880072 | tf_op jit(solution)/shard_map/ppermute | solution.py:472
  118.4 19.9 %collective-permute-start.7 = (bf16[544,1152]{1,0:T(8,128)(2,1)S(1)}, bf16[544,1152]{1,0:T(8,128)(2,1)S(1)}, u32[]{:S(2)}, u32[]{:S(2)}) collective-permute-start(bf16[544,1152]{1,0:T(8,128)(2,1)S(1)} %pad_maximum_fusion.2), channel_id=1, source_target_pairs={{0,4},{4,0},{8,12},{12,8},{16,20},{20,16},{24,28},{28,24},{1,5},{5... | collective-permute-start | bytes 3760136 | tf_op jit(solution)/shard_map/ppermute | solution.py:472
  119.8 20.2 %collective-permute-start.8 = (bf16[544,1152]{1,0:T(8,128)(2,1)S(1)}, bf16[544,1152]{1,0:T(8,128)(2,1)S(1)}, u32[]{:S(2)}, u32[]{:S(2)}) collective-permute-start(bf16[544,1152]{1,0:T(8,128)(2,1)S(1)} %pad_maximum_fusion.3), channel_id=1, source_target_pairs={{0,4},{4,0},{8,12},{12,8},{16,20},{20,16},{24,28},{28,24},{1,5},{5... | collective-permute-start | bytes 3760136 | tf_op jit(solution)/shard_map/ppermute | solution.py:472
  120.8 13.6 %collective-permute-start.11 = (bf16[40,1152]{1,0:T(8,128)(2,1)S(1)}, bf16[40,1152]{1,0:T(8,128)(2,1)S(1)}, u32[]{:S(2)}, u32[]{:S(2)}) collective-permute-start(bf16[40,1152]{1,0:T(8,128)(2,1)S(1)} %get-tuple-element.50), channel_id=1, source_target_pairs={{0,3},{1,0},{2,1},{3,2},{4,7},{5,4},{6,5},{7,6},{8,11},{9,8},{10,9... | collective-permute-start | bytes 276488 | tf_op jit(solution)/shard_map/ppermute | solution.py:507
  125.1 9.3 %collective-permute-start.10 = (bf16[40,1152]{1,0:T(8,128)(2,1)S(1)}, bf16[40,1152]{1,0:T(8,128)(2,1)S(1)}, u32[]{:S(2)}, u32[]{:S(2)}) collective-permute-start(bf16[40,1152]{1,0:T(8,128)(2,1)S(1)} %get-tuple-element.50), channel_id=1, source_target_pairs={{0,2},{1,3},{2,0},{3,1},{4,6},{5,7},{6,4},{7,5},{8,10},{9,11},{10,... | collective-permute-start | bytes 276488 | tf_op jit(solution)/shard_map/ppermute | solution.py:507
  125.1 7.6 %collective-permute-start.9 = (bf16[40,1152]{1,0:T(8,128)(2,1)S(1)}, bf16[40,1152]{1,0:T(8,128)(2,1)S(1)}, u32[]{:S(2)}, u32[]{:S(2)}) collective-permute-start(bf16[40,1152]{1,0:T(8,128)(2,1)S(1)} %get-tuple-element.50), channel_id=1, source_target_pairs={{0,1},{1,2},{2,3},{3,0},{4,5},{5,6},{6,7},{7,4},{8,9},{9,10},{10,1... | collective-permute-start | bytes 276488 | tf_op jit(solution)/shard_map/ppermute | solution.py:507
  129.6 36.0 %copy-start.29 = (bf16[320,1152]{1,0:T(8,128)(2,1)}, bf16[320,1152]{1,0:T(8,128)(2,1)S(1)}, u32[]{:S(2)}) copy-start(bf16[320,1152]{1,0:T(8,128)(2,1)S(1)} %get-tuple-element.47) | copy-start | bytes 2211844
  129.6 36.0 %copy-start.31 = (bf16[320,1152]{1,0:T(8,128)(2,1)}, bf16[320,1152]{1,0:T(8,128)(2,1)S(1)}, u32[]{:S(2)}) copy-start(bf16[320,1152]{1,0:T(8,128)(2,1)S(1)} %get-tuple-element.48) | copy-start | bytes 2211844
  129.6 8.7 %copy-start.9 = (bf16[1088,1152]{1,0:T(8,128)(2,1)S(1)}, bf16[1088,1152]{1,0:T(8,128)(2,1)}, u32[]{:S(2)}) copy-start(bf16[1088,1152]{1,0:T(8,128)(2,1)} %get-tuple-element.77) | copy-start | bytes 7520260
  134.5 45.9 %collective-permute-start.14 = (bf16[160,1152]{1,0:T(8,128)(2,1)S(1)}, bf16[160,1152]{1,0:T(8,128)(2,1)}, u32[]{:S(2)}, u32[]{:S(2)}) collective-permute-start(bf16[160,1152]{1,0:T(8,128)(2,1)S(1)} %bitcast.174), channel_id=1, source_target_pairs={{0,24},{4,28},{8,16},{12,20},{16,8},{20,12},{24,0},{28,4},{1,25},{... | collective-permute-start | bytes 1105928 | tf_op jit(solution)/shard_map/ppermute | solution.py:472
  136.1 42.5 %collective-permute-start.13 = (bf16[160,1152]{1,0:T(8,128)(2,1)S(1)}, bf16[160,1152]{1,0:T(8,128)(2,1)}, u32[]{:S(2)}, u32[]{:S(2)}) collective-permute-start(bf16[160,1152]{1,0:T(8,128)(2,1)S(1)} %bitcast.175), channel_id=1, source_target_pairs={{0,16},{4,20},{8,24},{12,28},{16,0},{20,4},{24,8},{28,12},{1,17},{... | collective-permute-start | bytes 1105928 | tf_op jit(solution)/shard_map/ppermute | solution.py:472
  136.6 40.1 %collective-permute-start.12 = (bf16[160,1152]{1,0:T(8,128)(2,1)S(1)}, bf16[160,1152]{1,0:T(8,128)(2,1)}, u32[]{:S(2)}, u32[]{:S(2)}) collective-permute-start(bf16[160,1152]{1,0:T(8,128)(2,1)S(1)} %bitcast.176), channel_id=1, source_target_pairs={{0,8},{4,12},{8,0},{12,4},{16,24},{20,28},{24,16},{28,20},{1,9},{5... | collective-permute-start | bytes 1105928 | tf_op jit(solution)/shard_map/ppermute | solution.py:472
  176.7 111.8 %reduce-scatter.4.cloned.1.call-start = ((), (), s32[]{:S(2)}) async-start(), calls=%async_computation.9 | async-start | bytes 2211840 | tf_op jit(solution)/shard_map/reduce_scatter | solution.py:735
  184.9 3.5 collective-permute-start.15
  223.7 11.0 %copy-start.19 = (f32[768,1152]{1,0:T(8,128)}, f32[768,1152]{1,0:T(8,128)S(1)}, u32[]{:S(2)}) copy-start(f32[768,1152]{1,0:T(8,128)S(1)} %subtract_multiply_fusion) | copy-start | bytes 10616836
  239.3 11.8 %collective-permute-start.16 = (bf16[1,2,2,136,1152]{4,3,2,1,0:T(8,128)(2,1)}, bf16[1,2,2,136,1152]{4,3,2,1,0:T(8,128)(2,1)}, u32[]{:S(2)}, u32[]{:S(2)}) collective-permute-start(bf16[1,2,2,136,1152]{4,3,2,1,0:T(8,128)(2,1)} %bitcast.48), channel_id=1, source_target_pairs={{0,4},{4,0},{8,12},{12,8},{16,20},{20,16},{24,28},{28,24},{1,5},{5... | collective-permute-start | bytes 3760136 | tf_op jit(solution)/shard_map/ppermute | solution.py:472
  240.6 14.1 %collective-permute-start.19 = (bf16[1,2,2,136,1152]{4,3,2,1,0:T(8,128)(2,1)}, bf16[1,2,2,136,1152]{4,3,2,1,0:T(8,128)(2,1)}, u32[]{:S(2)}, u32[]{:S(2)}) collective-permute-start(bf16[1,2,2,136,1152]{4,3,2,1,0:T(8,128)(2,1)} %bitcast.51), channel_id=1, source_target_pairs={{0,4},{4,0},{8,12},{12,8},{16,20},{20,16},{24,28},{28,24},{1,5},{5... | collective-permute-start | bytes 3760136 | tf_op jit(solution)/shard_map/ppermute | solution.py:472
  251.1 99.8 %all-gather.8.cloned.1.call-start = ((), (), s32[]{:S(2)}) async-start(), calls=%async_computation.10 | async-start | bytes 2211840 | tf_op jit(solution)/shard_map/all_gather | solution.py:750
  253.2 16.1 %collective-permute-start.17 = (bf16[1,1,2,136,1152]{4,3,2,1,0:T(8,128)(2,1)S(1)}, bf16[1,1,2,136,1152]{4,3,2,1,0:T(8,128)(2,1)S(1)}, u32[]{:S(2)}, u32[]{:S(2)}) collective-permute-start(bf16[1,1,2,136,1152]{4,3,2,1,0:T(8,128)(2,1)S(1)} %slice.332), channel_id=1, source_target_pairs={{0,16},{4,20},{8,24},{12,28},{16,0},{20,4},{24,8},{28,12},{1,17},{... | collective-permute-start | bytes 1880072 | tf_op jit(solution)/shard_map/ppermute | solution.py:472
  256.4 16.5 %collective-permute-start.20 = (bf16[1,2,1,136,1152]{4,3,2,1,0:T(8,128)(2,1)S(1)}, bf16[1,2,1,136,1152]{4,3,2,1,0:T(8,128)(2,1)S(1)}, u32[]{:S(2)}, u32[]{:S(2)}) collective-permute-start(bf16[1,2,1,136,1152]{4,3,2,1,0:T(8,128)(2,1)S(1)} %slice.338), channel_id=1, source_target_pairs={{0,8},{4,12},{8,0},{12,4},{16,24},{20,28},{24,16},{28,20},{1,9},{5... | collective-permute-start | bytes 1880072 | tf_op jit(solution)/shard_map/ppermute | solution.py:472
  269.4 9.4 %collective-permute-start.18 = (bf16[1,1,1,136,1152]{4,3,2,1,0:T(8,128)(2,1)S(1)}, bf16[1,1,1,136,1152]{4,3,2,1,0:T(8,128)(2,1)S(1)}, u32[]{:S(2)}, u32[]{:S(2)}) collective-permute-start(bf16[1,1,1,136,1152]{4,3,2,1,0:T(8,128)(2,1)S(1)} %slice.334), channel_id=1, source_target_pairs={{0,8},{4,12},{8,0},{12,4},{16,24},{20,28},{24,16},{28,20},{1,9},{5... | collective-permute-start | bytes 940040 | tf_op jit(solution)/shard_map/ppermute | solution.py:472
  273.1 7.6 %collective-permute-start.21 = (bf16[1,1,1,136,1152]{4,3,2,1,0:T(8,128)(2,1)S(1)}, bf16[1,1,1,136,1152]{4,3,2,1,0:T(8,128)(2,1)S(1)}, u32[]{:S(2)}, u32[]{:S(2)}) collective-permute-start(bf16[1,1,1,136,1152]{4,3,2,1,0:T(8,128)(2,1)S(1)} %slice.340), channel_id=1, source_target_pairs={{0,16},{4,20},{8,24},{12,28},{16,0},{20,4},{24,8},{28,12},{1,17},{... | collective-permute-start | bytes 940040 | tf_op jit(solution)/shard_map/ppermute | solution.py:472
  293.9 35.4 %all-to-all-start.1 = ((bf16[8,136,1152]{2,1,0:T(8,128)(2,1)}), bf16[8,136,1152]{2,1,0:T(8,128)(2,1)}, u32[]{:S(2)}, u32[]{:S(2)}) async-start(bf16[8,136,1152]{2,1,0:T(8,128)(2,1)} %touch.6), calls=%async_computation.2 | async-start | bytes 5013504 | tf_op jit(solution)/shard_map/all_to_all | solution.py:649
  337.0 9.1 %copy-start = (bf16[1088,1152]{1,0:T(8,128)(2,1)}, bf16[1088,1152]{1,0:T(8,128)(2,1)S(1)}, u32[]{:S(2)}) copy-start(bf16[1088,1152]{1,0:T(8,128)(2,1)S(1)} %get-tuple-element.20.top_ref.refs_1_) | copy-start | bytes 7520260
  337.0 9.1 %copy-start.2 = (bf16[1088,1152]{1,0:T(8,128)(2,1)}, bf16[1088,1152]{1,0:T(8,128)(2,1)S(1)}, u32[]{:S(2)}) copy-start(bf16[1088,1152]{1,0:T(8,128)(2,1)S(1)} %get-tuple-element.21.rest_ref.refs_2_) | copy-start | bytes 7520260
  346.0 54.8 %all-to-all-start.2 = ((f32[8,720,128]{2,1,0:T(8,128)}), f32[8,720,128]{2,1,0:T(8,128)}, u32[]{:S(2)}, u32[]{:S(2)}) async-start(f32[8,720,128]{2,1,0:T(8,128)} %bitcast.182), calls=%async_computation.3 | async-start | bytes 5898240 | tf_op jit(solution)/shard_map/all_to_all | solution.py:649
  353.2 8.6 %copy-start.21 = (f32[768,1152]{1,0:T(8,128)S(1)}, f32[768,1152]{1,0:T(8,128)}, u32[]{:S(2)}) copy-start(f32[768,1152]{1,0:T(8,128)} %copy-done.20) | copy-start | bytes 10616836
  353.2 8.6 %copy-start.30 = (bf16[320,1152]{1,0:T(8,128)(2,1)S(1)}, bf16[320,1152]{1,0:T(8,128)(2,1)}, u32[]{:S(2)}) copy-start(bf16[320,1152]{1,0:T(8,128)(2,1)} %copy-done.29) | copy-start | bytes 2211844
  353.2 8.6 %copy-start.32 = (bf16[320,1152]{1,0:T(8,128)(2,1)S(1)}, bf16[320,1152]{1,0:T(8,128)(2,1)}, u32[]{:S(2)}) copy-start(bf16[320,1152]{1,0:T(8,128)(2,1)} %copy-done.31) | copy-start | bytes 2211844
  353.3 8.6 %copy-start.34 = (bf16[320,1152]{1,0:T(8,128)(2,1)S(1)}, bf16[320,1152]{1,0:T(8,128)(2,1)}, u32[]{:S(2)}) copy-start(bf16[320,1152]{1,0:T(8,128)(2,1)} %get-tuple-element.49) | copy-start | bytes 2211844
  373.4 2.8 collective-permute-start.28
  376.1 20.8 %collective-permute-start.25 = (bf16[2,2,1,80,1152]{4,3,2,1,0:T(8,128)(2,1)}, bf16[2,2,1,80,1152]{4,3,2,1,0:T(8,128)(2,1)}, u32[]{:S(2)}, u32[]{:S(2)}) collective-permute-start(bf16[2,2,1,80,1152]{4,3,2,1,0:T(8,128)(2,1)} %fusion.28), channel_id=1, source_target_pairs={{0,4},{4,0},{8,12},{12,8},{16,20},{20,16},{24,28},{28,24},{1,5},{5... | collective-permute-start | bytes 2211848 | tf_op jit(solution)/shard_map/ppermute | solution.py:472
  376.2 10.6 %collective-permute-start.29 = (f32[112,128]{1,0:T(8,128)S(1)}, f32[112,128]{1,0:T(8,128)S(1)}, u32[]{:S(2)}, u32[]{:S(2)}) collective-permute-start(f32[112,128]{1,0:T(8,128)S(1)} %fusion.64), channel_id=1, source_target_pairs={{0,8},{4,12},{8,0},{12,4},{16,24},{20,28},{24,16},{28,20},{1,9},{5... | collective-permute-start | bytes 172040 | tf_op jit(solution)/shard_map/ppermute | solution.py:472
  386.9 4.2 collective-permute-start.30
  391.1 4.2 collective-permute-start.31
  395.4 13.2 %collective-permute-start.32 = (f32[112,128]{1,0:T(8,128)S(1)}, f32[112,128]{1,0:T(8,128)S(1)}, u32[]{:S(2)}, u32[]{:S(2)}) collective-permute-start(f32[112,128]{1,0:T(8,128)S(1)} %add.594), channel_id=1, source_target_pairs={{0,2},{1,3},{2,0},{3,1},{4,6},{5,7},{6,4},{7,5},{8,10},{9,11},{10,... | collective-permute-start | bytes 172040 | tf_op jit(solution)/shard_map/ppermute | solution.py:472
  399.2 9.9 %collective-permute-start.26 = (bf16[1,2,1,80,1152]{4,3,2,1,0:T(8,128)(2,1)S(1)}, bf16[1,2,1,80,1152]{4,3,2,1,0:T(8,128)(2,1)}, u32[]{:S(2)}, u32[]{:S(2)}) collective-permute-start(bf16[1,2,1,80,1152]{4,3,2,1,0:T(8,128)(2,1)S(1)} %constant_dynamic-slice_fusion.1), channel_id=1, source_target_pairs={{0,16},{4,20},{8,24},{12,28},{16,0},{20,4},{24,8},{28,12},{1,17},{... | collective-permute-start | bytes 1105928 | tf_op jit(solution)/shard_map/ppermute | solution.py:472
  402.9 6.2 copy-start.23
  404.2 53.4 %all-reduce.9.cloned.1.call-start = ((), (), s32[]{:S(2)}) async-start(), calls=%async_computation.11 | async-start | bytes 1474560 | tf_op jit(solution)/shard_map/psum | solution.py:773
  407.4 3.5 collective-permute-start.22
  408.6 134.3 %copy-start.14 = (f32[112,128]{1,0:T(8,128)}, f32[112,128]{1,0:T(8,128)S(1)}, u32[]{:S(2)}) copy-start(f32[112,128]{1,0:T(8,128)S(1)} %add.595.refs_1_.first_ref) | copy-start | bytes 172036
  410.2 7.5 %collective-permute-start.27 = (bf16[1,1,1,80,1152]{4,3,2,1,0:T(8,128)(2,1)S(1)}, bf16[1,1,1,80,1152]{4,3,2,1,0:T(8,128)(2,1)S(1)}, u32[]{:S(2)}, u32[]{:S(2)}) collective-permute-start(bf16[1,1,1,80,1152]{4,3,2,1,0:T(8,128)(2,1)S(1)} %constant_dynamic-slice_fusion), channel_id=1, source_target_pairs={{0,8},{4,12},{8,0},{12,4},{16,24},{20,28},{24,16},{28,20},{1,9},{5... | collective-permute-start | bytes 552968 | tf_op jit(solution)/shard_map/ppermute | solution.py:472
  411.1 14.1 %collective-permute-start.23 = (bf16[2,1,1,80,1152]{4,3,2,1,0:T(8,128)(2,1)S(1)}, bf16[2,1,1,80,1152]{4,3,2,1,0:T(8,128)(2,1)S(1)}, u32[]{:S(2)}, u32[]{:S(2)}) collective-permute-start(bf16[2,1,1,80,1152]{4,3,2,1,0:T(8,128)(2,1)S(1)} %constant_dynamic-slice_fusion.3), channel_id=1, source_target_pairs={{0,8},{4,12},{8,0},{12,4},{16,24},{20,28},{24,16},{28,20},{1,9},{5... | collective-permute-start | bytes 1105928 | tf_op jit(solution)/shard_map/ppermute | solution.py:472
  425.4 34.8 %collective-permute-start.24 = (bf16[1,1,1,80,1152]{4,3,2,1,0:T(8,128)(2,1)S(1)}, bf16[1,1,1,80,1152]{4,3,2,1,0:T(8,128)(2,1)S(1)}, u32[]{:S(2)}, u32[]{:S(2)}) collective-permute-start(bf16[1,1,1,80,1152]{4,3,2,1,0:T(8,128)(2,1)S(1)} %constant_dynamic-slice_fusion.2), channel_id=1, source_target_pairs={{0,16},{4,20},{8,24},{12,28},{16,0},{20,4},{24,8},{28,12},{1,17},{... | collective-permute-start | bytes 552968 | tf_op jit(solution)/shard_map/ppermute | solution.py:472
  461.5 15.7 %all-to-all-start.3 = ((bf16[8,40,1152]{2,1,0:T(8,128)(2,1)}), bf16[8,40,1152]{2,1,0:T(8,128)(2,1)S(1)}, u32[]{:S(2)}, u32[]{:S(2)}) async-start(bf16[8,40,1152]{2,1,0:T(8,128)(2,1)} %add_add_fusion), calls=%async_computation.4 | async-start | bytes 1474560 | tf_op jit(solution)/shard_map/all_to_all | solution.py:649
  465.2 72.1 %all-gather.10.cloned.1.call-start = ((), (), s32[]{:S(2)}) async-start(), calls=%async_computation.12 | async-start | bytes 3317760 | tf_op jit(solution)/shard_map/all_gather | solution.py:833
  478.5 5.6 copy-start.13
  484.1 151.9 %reduce-scatter.8.cloned.1.call-start = ((), (), s32[]{:S(2)}) async-start(), calls=%async_computation.14 | async-start | bytes 2949120 | tf_op jit(solution)/shard_map/reduce_scatter | solution.py:851
  537.3 5.6 copy-start.38
  537.3 100.2 %reduce-scatter.6.cloned.1.call-start = ((), (), s32[]{:S(2)}) async-start(), calls=%async_computation.13 | async-start | bytes 2949120 | tf_op jit(solution)/shard_map/reduce_scatter | solution.py:854
  (29 other events, 77.9 us)
Sparse Core Ops, SparseCore 0:
  21.4 94.1 all-gather.11
  176.8 38.9 all-gather.5
  251.2 37.2 reduce-scatter.3
  292.9 39.4 all-gather.7
  417.9 39.6 all-reduce.8
  484.2 53.0 all-gather.9
  539.7 46.7 reduce-scatter.7
  588.9 47.5 reduce-scatter.5
